TPU v7x, 768 devices: a whole 4x8x12 slice. The times are simulated.
768 devices in a mesh: dp: 256 (over x, z_hi, y, core), mp: 3 (over z_lo).
Axes of the slice: x: 4, y: 8, z: 12 (z_hi: 4, z_lo: 3; z = z_hi * 3 + z_lo), core: 2. Of those that a mesh axis runs over, the one named last changes fastest.
Arguments:
- picture_embedding_matrix: bfloat16 [147456, 1152], P(('dp', 'mp')), may hold values from -0.1875 to 0.1875
- caption_embedding_matrix: bfloat16 [147456, 1152], P(('dp', 'mp')), may hold values from -0.1875 to 0.1875
- positive_caption_indices: int32 [147456], P(('dp', 'mp')), may hold values from 0 to 147455, as said below
- sharpness_multiplier: float32 [1], replicated, may hold values from 5 to 15
- additive_shift_term: float32 [1], replicated, may hold values from -3 to -1
Outputs:
- grad_image: float32 [147456, 1152], P(('dp', 'mp'))
- grad_text: float32 [147456, 1152], P(('dp', 'mp'))
Inputs may be any that keep to these rules, and one draw needn't show every extreme that they name: positive_caption_indices[i] names a text of row i's own block of 192 rows, and each text of a block is named once.
All inputs are finite; a program needn't handle non-finite values.
Results may differ from a plain program's by a relative error of at most 0.0027.
Values may be sent and summed in bfloat16 or wider, within the bound.
No kernel may reach another device: no remote copies, remote signals or barrier semaphores. Data moves between devices by JAX's collectives and lax.ppermute only.
A program may use at most 32 MiB of HBM per device.

v0:
```python
import jax
import jax.numpy as jnp
from jax import lax
from jax.sharding import PartitionSpec as P

STEPS = 8


def passed_along(value, axis, by):
    length = lax.axis_size(axis)
    return lax.ppermute(value, axis, [(i, (i + by) % length) for i in range(length)])


def on_device(
    picture_embedding_matrix,
    caption_embedding_matrix,
    positive_caption_indices,
    sharpness_multiplier,
    additive_shift_term,
):
    rows = picture_embedding_matrix.shape[0]
    here = lax.axis_index(("dp", "mp"))
    cycle_size = lax.axis_size(("dp", "mp"))
    grad_image = jnp.zeros(picture_embedding_matrix.shape, jnp.float32)
    texts = caption_embedding_matrix
    carried = jnp.zeros(caption_embedding_matrix.shape, jnp.float32)
    for step in range(STEPS):
        owner = (here - step) % cycle_size
        segment_start_position = owner * rows
        couple_similarity_scores = lax.dot_general(
            picture_embedding_matrix,
            texts,
            (((1,), (1,)), ((), ())),
            preferred_element_type=jnp.float32,
        )
        tempered_similarity_scores = (
            sharpness_multiplier[0] * couple_similarity_scores + additive_shift_term[0]
        )
        columns = segment_start_position + jnp.arange(rows, dtype=jnp.int32)
        match_polarity = jnp.where(
            positive_caption_indices[:, None] == columns[None, :], 1.0, -1.0
        ).astype(jnp.float32)
        couple_coefficient = (
            sharpness_multiplier[0]
            * -match_polarity
            * jax.nn.sigmoid(-match_polarity * tempered_similarity_scores)
        ).astype(jnp.bfloat16)
        grad_image = grad_image + jnp.dot(
            couple_coefficient, texts, preferred_element_type=jnp.float32
        )
        share = lax.dot_general(
            couple_coefficient,
            picture_embedding_matrix,
            (((0,), (0,)), ((), ())),
            preferred_element_type=jnp.float32,
        )
        carried = carried + share
        if step + 1 < STEPS:
            texts, carried = (
                passed_along(texts.astype(jnp.float32), ("dp", "mp"), 1).astype(texts.dtype),
                passed_along(carried, ("dp", "mp"), 1),
            )
    grad_text = passed_along(carried, ("dp", "mp"), -(STEPS - 1))
    return (grad_image, grad_text)


def solution(mesh):
    in_specs = (P(("dp", "mp"), None), P(("dp", "mp"), None), P(("dp", "mp")), P(), P())
    out_specs = (P(("dp", "mp"), None), P(("dp", "mp"), None))
    return jax.shard_map(
        on_device, mesh=mesh, in_specs=in_specs, out_specs=out_specs, check_vma=False
    )
```

profile of v0, /device:TPU:1, one launch (start us, length us, event | category | flops | bytes accessed | tf_op | source)
XLA Modules:
  0.0 288.6 jit_solution(10996368403306857003)
XLA Ops:
  5.1 4.8 %collective-permute-start.7 = (f32[192,1152]{1,0:T(8,128)S(1)}, f32[192,1152]{1,0:T(8,128)S(1)}, u32[]{:S(2)}, u32[]{:S(2)}) collective-permute-start(f32[192,1152]{1,0:T(8,128)S(1)} %fusion.89), channel_id=1, source_target_pairs={{0,1},{1,2},{2,3},{3,4},{4,5},{5,6},{6,7},{7,8},{8,9},{9,10},{10,1... | collective-permute-start | bytes 2654216 | tf_op jit(solution)/shard_map/ppermute | solution.py:11
  9.9 4.0 %collective-permute-start = (bf16[192,1152]{1,0:T(8,128)(2,1)S(1)}, bf16[192,1152]{1,0:T(8,128)(2,1)}, u32[]{:S(2)}, u32[]{:S(2)}) collective-permute-start(bf16[192,1152]{1,0:T(8,128)(2,1)S(1)} %copy-done.1), channel_id=1, source_target_pairs={{0,1},{1,2},{2,3},{3,4},{4,5},{5,6},{6,7},{7,8},{8,9},{9,10},{10,1... | collective-permute-start | bytes 1327112 | tf_op jit(solution)/shard_map/ppermute | solution.py:11
  13.9 27.3 %collective-permute-done = bf16[192,1152]{1,0:T(8,128)(2,1)} collective-permute-done((bf16[192,1152]{1,0:T(8,128)(2,1)S(1)}, bf16[192,1152]{1,0:T(8,128)(2,1)}, u32[]{:S(2)}, u32[]{:S(2)}) %collective-permute-start) | collective-permute-done | bytes 442400 | tf_op jit(solution)/shard_map/ppermute | solution.py:11
  45.5 2.7 collective-permute-start.8
  48.3 8.3 %collective-permute-done.1 = bf16[192,1152]{1,0:T(8,128)(2,1)S(1)} collective-permute-done((bf16[192,1152]{1,0:T(8,128)(2,1)}, bf16[192,1152]{1,0:T(8,128)(2,1)S(1)}, u32[]{:S(2)}, u32[]{:S(2)}) %collective-permute-start.1) | collective-permute-done | bytes 442400 | tf_op jit(solution)/shard_map/ppermute | solution.py:11
  56.6 1.9 collective-permute-start.2
  59.5 16.4 %collective-permute-done.8 = f32[192,1152]{1,0:T(8,128)S(1)} collective-permute-done((f32[192,1152]{1,0:T(8,128)S(1)}, f32[192,1152]{1,0:T(8,128)S(1)}, u32[]{:S(2)}, u32[]{:S(2)}) %collective-permute-start.8) | collective-permute-done | bytes 884768 | tf_op jit(solution)/shard_map/ppermute | solution.py:11
  76.0 1.9 collective-permute-start.9
  78.0 7.1 %collective-permute-done.2 = bf16[192,1152]{1,0:T(8,128)(2,1)} collective-permute-done((bf16[192,1152]{1,0:T(8,128)(2,1)S(1)}, bf16[192,1152]{1,0:T(8,128)(2,1)}, u32[]{:S(2)}, u32[]{:S(2)}) %collective-permute-start.2) | collective-permute-done | bytes 442400 | tf_op jit(solution)/shard_map/ppermute | solution.py:11
  89.1 15.1 %collective-permute-done.9 = f32[192,1152]{1,0:T(8,128)S(1)} collective-permute-done((f32[192,1152]{1,0:T(8,128)S(1)}, f32[192,1152]{1,0:T(8,128)S(1)}, u32[]{:S(2)}, u32[]{:S(2)}) %collective-permute-start.9) | collective-permute-done | bytes 884768 | tf_op jit(solution)/shard_map/ppermute | solution.py:11
  104.3 1.9 collective-permute-start.10
  106.3 7.1 %collective-permute-done.3 = bf16[192,1152]{1,0:T(8,128)(2,1)S(1)} collective-permute-done((bf16[192,1152]{1,0:T(8,128)(2,1)}, bf16[192,1152]{1,0:T(8,128)(2,1)S(1)}, u32[]{:S(2)}, u32[]{:S(2)}) %collective-permute-start.3) | collective-permute-done | bytes 442400 | tf_op jit(solution)/shard_map/ppermute | solution.py:11
  116.4 16.2 %collective-permute-done.10 = f32[192,1152]{1,0:T(8,128)S(1)} collective-permute-done((f32[192,1152]{1,0:T(8,128)S(1)}, f32[192,1152]{1,0:T(8,128)S(1)}, u32[]{:S(2)}, u32[]{:S(2)}) %collective-permute-start.10) | collective-permute-done | bytes 884768 | tf_op jit(solution)/shard_map/ppermute | solution.py:11
  132.6 1.9 collective-permute-start.11
  135.8 6.2 %collective-permute-done.4 = bf16[192,1152]{1,0:T(8,128)(2,1)} collective-permute-done((bf16[192,1152]{1,0:T(8,128)(2,1)S(1)}, bf16[192,1152]{1,0:T(8,128)(2,1)}, u32[]{:S(2)}, u32[]{:S(2)}) %collective-permute-start.4) | collective-permute-done | bytes 442400 | tf_op jit(solution)/shard_map/ppermute | solution.py:11
  145.6 15.5 %collective-permute-done.11 = f32[192,1152]{1,0:T(8,128)S(1)} collective-permute-done((f32[192,1152]{1,0:T(8,128)S(1)}, f32[192,1152]{1,0:T(8,128)S(1)}, u32[]{:S(2)}, u32[]{:S(2)}) %collective-permute-start.11) | collective-permute-done | bytes 884768 | tf_op jit(solution)/shard_map/ppermute | solution.py:11
  161.2 2.1 collective-permute-start.12
  165.9 4.5 %collective-permute-done.5 = bf16[192,1152]{1,0:T(8,128)(2,1)S(1)} collective-permute-done((bf16[192,1152]{1,0:T(8,128)(2,1)}, bf16[192,1152]{1,0:T(8,128)(2,1)S(1)}, u32[]{:S(2)}, u32[]{:S(2)}) %collective-permute-start.5) | collective-permute-done | bytes 442400 | tf_op jit(solution)/shard_map/ppermute | solution.py:11
  173.0 16.5 %collective-permute-done.12 = f32[192,1152]{1,0:T(8,128)S(1)} collective-permute-done((f32[192,1152]{1,0:T(8,128)S(1)}, f32[192,1152]{1,0:T(8,128)S(1)}, u32[]{:S(2)}, u32[]{:S(2)}) %collective-permute-start.12) | collective-permute-done | bytes 884768 | tf_op jit(solution)/shard_map/ppermute | solution.py:11
  189.6 1.9 collective-permute-start.13
  193.1 5.7 %collective-permute-done.6 = bf16[192,1152]{1,0:T(8,128)(2,1)S(1)} collective-permute-done((bf16[192,1152]{1,0:T(8,128)(2,1)S(1)}, bf16[192,1152]{1,0:T(8,128)(2,1)S(1)}, u32[]{:S(2)}, u32[]{:S(2)}) %collective-permute-start.6) | collective-permute-done | bytes 442400 | tf_op jit(solution)/shard_map/ppermute | solution.py:11
  199.5 18.3 %collective-permute-done.13 = f32[192,1152]{1,0:T(8,128)S(1)} collective-permute-done((f32[192,1152]{1,0:T(8,128)S(1)}, f32[192,1152]{1,0:T(8,128)S(1)}, u32[]{:S(2)}, u32[]{:S(2)}) %collective-permute-start.13) | collective-permute-done | bytes 884768 | tf_op jit(solution)/shard_map/ppermute | solution.py:11
  217.8 15.3 %collective-permute-start.14 = (f32[192,1152]{1,0:T(8,128)S(1)}, f32[192,1152]{1,0:T(8,128)S(1)}, u32[]{:S(2)}, u32[]{:S(2)}) collective-permute-start(f32[192,1152]{1,0:T(8,128)S(1)} %add.270), channel_id=1, source_target_pairs={{0,761},{1,762},{2,763},{3,764},{4,765},{5,766},{6,767},{7,0},{8,1... | collective-permute-start | bytes 2654216 | tf_op jit(solution)/shard_map/ppermute | solution.py:11
  235.6 52.0 %collective-permute-done.14 = f32[192,1152]{1,0:T(8,128)S(1)} collective-permute-done((f32[192,1152]{1,0:T(8,128)S(1)}, f32[192,1152]{1,0:T(8,128)S(1)}, u32[]{:S(2)}, u32[]{:S(2)}) %collective-permute-start.14) | collective-permute-done | bytes 884768 | tf_op jit(solution)/shard_map/ppermute | solution.py:11
  (71 shorter events, 31.3 us)
Async XLA Ops:
  0.6 1.4 copy-start
  2.0 0.7 copy-start.12
  4.7 5.2 %copy-start.1 = (bf16[192,1152]{1,0:T(8,128)(2,1)S(1)}, bf16[192,1152]{1,0:T(8,128)(2,1)}, u32[]{:S(2)}) copy-start(bf16[192,1152]{1,0:T(8,128)(2,1)} %param.6) | copy-start | bytes 1327108
  5.1 39.5 %collective-permute-start.7 = (f32[192,1152]{1,0:T(8,128)S(1)}, f32[192,1152]{1,0:T(8,128)S(1)}, u32[]{:S(2)}, u32[]{:S(2)}) collective-permute-start(f32[192,1152]{1,0:T(8,128)S(1)} %fusion.89), channel_id=1, source_target_pairs={{0,1},{1,2},{2,3},{3,4},{4,5},{5,6},{6,7},{7,8},{8,9},{9,10},{10,1... | collective-permute-start | bytes 2654216 | tf_op jit(solution)/shard_map/ppermute | solution.py:11
  9.9 31.3 %collective-permute-start = (bf16[192,1152]{1,0:T(8,128)(2,1)S(1)}, bf16[192,1152]{1,0:T(8,128)(2,1)}, u32[]{:S(2)}, u32[]{:S(2)}) collective-permute-start(bf16[192,1152]{1,0:T(8,128)(2,1)S(1)} %copy-done.1), channel_id=1, source_target_pairs={{0,1},{1,2},{2,3},{3,4},{4,5},{5,6},{6,7},{7,8},{8,9},{9,10},{10,1... | collective-permute-start | bytes 1327112 | tf_op jit(solution)/shard_map/ppermute | solution.py:11
  41.2 15.4 %collective-permute-start.1 = (bf16[192,1152]{1,0:T(8,128)(2,1)}, bf16[192,1152]{1,0:T(8,128)(2,1)S(1)}, u32[]{:S(2)}, u32[]{:S(2)}) collective-permute-start(bf16[192,1152]{1,0:T(8,128)(2,1)} %collective-permute-done), channel_id=1, source_target_pairs={{0,1},{1,2},{2,3},{3,4},{4,5},{5,6},{6,7},{7,8},{8,9},{9,10},{10,1... | collective-permute-start | bytes 1327112 | tf_op jit(solution)/shard_map/ppermute | solution.py:11
  44.5 0.7 copy-start.3
  45.5 30.4 %collective-permute-start.8 = (f32[192,1152]{1,0:T(8,128)S(1)}, f32[192,1152]{1,0:T(8,128)S(1)}, u32[]{:S(2)}, u32[]{:S(2)}) collective-permute-start(f32[192,1152]{1,0:T(8,128)S(1)} %convolution_add_fusion), channel_id=1, source_target_pairs={{0,1},{1,2},{2,3},{3,4},{4,5},{5,6},{6,7},{7,8},{8,9},{9,10},{10,1... | collective-permute-start | bytes 2654216 | tf_op jit(solution)/shard_map/ppermute | solution.py:11
  56.6 28.5 %collective-permute-start.2 = (bf16[192,1152]{1,0:T(8,128)(2,1)S(1)}, bf16[192,1152]{1,0:T(8,128)(2,1)}, u32[]{:S(2)}, u32[]{:S(2)}) collective-permute-start(bf16[192,1152]{1,0:T(8,128)(2,1)S(1)} %collective-permute-done.1), channel_id=1, source_target_pairs={{0,1},{1,2},{2,3},{3,4},{4,5},{5,6},{6,7},{7,8},{8,9},{9,10},{10,1... | collective-permute-start | bytes 1327112 | tf_op jit(solution)/shard_map/ppermute | solution.py:11
  76.0 28.2 %collective-permute-start.9 = (f32[192,1152]{1,0:T(8,128)S(1)}, f32[192,1152]{1,0:T(8,128)S(1)}, u32[]{:S(2)}, u32[]{:S(2)}) collective-permute-start(f32[192,1152]{1,0:T(8,128)S(1)} %add.265), channel_id=1, source_target_pairs={{0,1},{1,2},{2,3},{3,4},{4,5},{5,6},{6,7},{7,8},{8,9},{9,10},{10,1... | collective-permute-start | bytes 2654216 | tf_op jit(solution)/shard_map/ppermute | solution.py:11
  85.1 28.3 %collective-permute-start.3 = (bf16[192,1152]{1,0:T(8,128)(2,1)}, bf16[192,1152]{1,0:T(8,128)(2,1)S(1)}, u32[]{:S(2)}, u32[]{:S(2)}) collective-permute-start(bf16[192,1152]{1,0:T(8,128)(2,1)} %collective-permute-done.2), channel_id=1, source_target_pairs={{0,1},{1,2},{2,3},{3,4},{4,5},{5,6},{6,7},{7,8},{8,9},{9,10},{10,1... | collective-permute-start | bytes 1327112 | tf_op jit(solution)/shard_map/ppermute | solution.py:11
  104.3 28.2 %collective-permute-start.10 = (f32[192,1152]{1,0:T(8,128)S(1)}, f32[192,1152]{1,0:T(8,128)S(1)}, u32[]{:S(2)}, u32[]{:S(2)}) collective-permute-start(f32[192,1152]{1,0:T(8,128)S(1)} %add.266), channel_id=1, source_target_pairs={{0,1},{1,2},{2,3},{3,4},{4,5},{5,6},{6,7},{7,8},{8,9},{9,10},{10,1... | collective-permute-start | bytes 2654216 | tf_op jit(solution)/shard_map/ppermute | solution.py:11
  113.5 28.5 %collective-permute-start.4 = (bf16[192,1152]{1,0:T(8,128)(2,1)S(1)}, bf16[192,1152]{1,0:T(8,128)(2,1)}, u32[]{:S(2)}, u32[]{:S(2)}) collective-permute-start(bf16[192,1152]{1,0:T(8,128)(2,1)S(1)} %collective-permute-done.3), channel_id=1, source_target_pairs={{0,1},{1,2},{2,3},{3,4},{4,5},{5,6},{6,7},{7,8},{8,9},{9,10},{10,1... | collective-permute-start | bytes 1327112 | tf_op jit(solution)/shard_map/ppermute | solution.py:11
  116.4 18.2 %copy-start.2 = (bf16[192,1152]{1,0:T(8,128)(2,1)S(1)}, bf16[192,1152]{1,0:T(8,128)(2,1)}, u32[]{:S(2)}) copy-start(bf16[192,1152]{1,0:T(8,128)(2,1)} %param.6) | copy-start | bytes 1327108
  132.6 28.4 %collective-permute-start.11 = (f32[192,1152]{1,0:T(8,128)S(1)}, f32[192,1152]{1,0:T(8,128)S(1)}, u32[]{:S(2)}, u32[]{:S(2)}) collective-permute-start(f32[192,1152]{1,0:T(8,128)S(1)} %add.267), channel_id=1, source_target_pairs={{0,1},{1,2},{2,3},{3,4},{4,5},{5,6},{6,7},{7,8},{8,9},{9,10},{10,1... | collective-permute-start | bytes 2654216 | tf_op jit(solution)/shard_map/ppermute | solution.py:11
  142.0 28.3 %collective-permute-start.5 = (bf16[192,1152]{1,0:T(8,128)(2,1)}, bf16[192,1152]{1,0:T(8,128)(2,1)S(1)}, u32[]{:S(2)}, u32[]{:S(2)}) collective-permute-start(bf16[192,1152]{1,0:T(8,128)(2,1)} %collective-permute-done.4), channel_id=1, source_target_pairs={{0,1},{1,2},{2,3},{3,4},{4,5},{5,6},{6,7},{7,8},{8,9},{9,10},{10,1... | collective-permute-start | bytes 1327112 | tf_op jit(solution)/shard_map/ppermute | solution.py:11
  145.6 17.6 %copy-start.4 = (bf16[192,192]{1,0:T(8,128)(2,1)S(1)}, bf16[192,192]{1,0:T(8,128)(2,1)}, u32[]{:S(2)}) copy-start(bf16[192,192]{1,0:T(8,128)(2,1)} %copy-done.3) | copy-start | bytes 221188
  161.2 3.4 %copy-start.7 = (bf16[192,192]{1,0:T(8,128)(2,1)S(1)}, bf16[192,192]{1,0:T(8,128)(2,1)}, u32[]{:S(2)}) copy-start(bf16[192,192]{1,0:T(8,128)(2,1)} %copy-done.6) | copy-start | bytes 221188
  161.2 28.3 %collective-permute-start.12 = (f32[192,1152]{1,0:T(8,128)S(1)}, f32[192,1152]{1,0:T(8,128)S(1)}, u32[]{:S(2)}, u32[]{:S(2)}) collective-permute-start(f32[192,1152]{1,0:T(8,128)S(1)} %add.268), channel_id=1, source_target_pairs={{0,1},{1,2},{2,3},{3,4},{4,5},{5,6},{6,7},{7,8},{8,9},{9,10},{10,1... | collective-permute-start | bytes 2654216 | tf_op jit(solution)/shard_map/ppermute | solution.py:11
  170.3 28.4 %collective-permute-start.6 = (bf16[192,1152]{1,0:T(8,128)(2,1)S(1)}, bf16[192,1152]{1,0:T(8,128)(2,1)S(1)}, u32[]{:S(2)}, u32[]{:S(2)}) collective-permute-start(bf16[192,1152]{1,0:T(8,128)(2,1)S(1)} %collective-permute-done.5), channel_id=1, source_target_pairs={{0,1},{1,2},{2,3},{3,4},{4,5},{5,6},{6,7},{7,8},{8,9},{9,10},{10,1... | collective-permute-start | bytes 1327112 | tf_op jit(solution)/shard_map/ppermute | solution.py:11
  173.0 18.5 %copy-start.9 = (bf16[192,192]{1,0:T(8,128)(2,1)S(1)}, bf16[192,192]{1,0:T(8,128)(2,1)}, u32[]{:S(2)}) copy-start(bf16[192,192]{1,0:T(8,128)(2,1)} %copy-done.8) | copy-start | bytes 221188
  189.6 28.2 %collective-permute-start.13 = (f32[192,1152]{1,0:T(8,128)S(1)}, f32[192,1152]{1,0:T(8,128)S(1)}, u32[]{:S(2)}, u32[]{:S(2)}) collective-permute-start(f32[192,1152]{1,0:T(8,128)S(1)} %add.269), channel_id=1, source_target_pairs={{0,1},{1,2},{2,3},{3,4},{4,5},{5,6},{6,7},{7,8},{8,9},{9,10},{10,1... | collective-permute-start | bytes 2654216 | tf_op jit(solution)/shard_map/ppermute | solution.py:11
  217.8 69.8 %collective-permute-start.14 = (f32[192,1152]{1,0:T(8,128)S(1)}, f32[192,1152]{1,0:T(8,128)S(1)}, u32[]{:S(2)}, u32[]{:S(2)}) collective-permute-start(f32[192,1152]{1,0:T(8,128)S(1)} %add.270), channel_id=1, source_target_pairs={{0,761},{1,762},{2,763},{3,764},{4,765},{5,766},{6,767},{7,0},{8,1... | collective-permute-start | bytes 2654216 | tf_op jit(solution)/shard_map/ppermute | solution.py:11
  233.4 0.9 copy-start.11
  (4 other events, 2.6 us)
where the time goes:
time: 289 us
  waiting for transfers between devices  216 us (75%)
  starting transfers between devices  48 us (17%)
  matrix products  16.8 us (6%)
  local copies, waits for them, and re-layouts  4.41 us (2%)
    ppermute x15, waiting for transfers between devices, passed_along(): lax.ppermute(value, axis, [(i, (i + by) % length) for i in range(length)])  216 us
    ppermute x15, starting transfers between devices, passed_along(): lax.ppermute(value, axis, [(i, (i + by) % length) for i in range(length)])  48 us
    dot_general x8, matrix products, on_device(): jnp.dot(couple_coefficient, texts, preferred_element_type=jnp.float32)  7.24 us
    dot_general x8, matrix products, on_device(): lax.dot_general(picture_embedding_matrix, texts, (((1,), (1,)), ((), ()))...  7.03 us
  transfers between devices with their start and end apart: 15, of which 14 were waited for; matrix products, arithmetic and copies ran while one was open for 5% of the time, Pallas kernels for 0%

commit v1 on v0

v1 whole, which is shorter than its diff:
```python
import jax
import jax.numpy as jnp
from jax import lax
from jax.sharding import PartitionSpec as P

AXES = ("dp", "mp")
ROWS = 192
LINE = 3
GROUP = 6
LAP = 8
NB = 768
LOW = jnp.bfloat16


def lap_of(b):
    return (b // GROUP) % LAP


def sent(value, target):
    pairs = [(b, target(b) % NB) for b in range(NB) if target(b) is not None]
    return lax.ppermute(value, AXES, pairs)


def line_turned(value, by):
    return sent(value, lambda b: b // LINE * LINE + (b + by) % LINE)


def group_onward(value, y):
    half = ROWS // 2
    main = sent(value, lambda b: b + GROUP if lap_of(b) < LAP - 1 else b - GROUP * (LAP - 1))
    direct = sent(value[half:], lambda b: b + GROUP if lap_of(b) == LAP - 1 else None)
    relayed = sent(main[:half], lambda b: b + GROUP * LAP if lap_of(b) == 0 else None)
    return jnp.where(y == 0, jnp.concatenate([relayed, direct]), main)


def group_back(value, y):
    half = ROWS // 2
    main = sent(value, lambda b: b - GROUP if lap_of(b) > 0 else b + GROUP * (LAP - 1))
    direct = sent(value[half:], lambda b: b - GROUP if lap_of(b) == 0 else None)
    relayed = sent(main[:half], lambda b: b - GROUP * LAP if lap_of(b) == LAP - 1 else None)
    return jnp.where(y == LAP - 1, jnp.concatenate([relayed, direct]), main)


def on_device(
    picture_embedding_matrix,
    caption_embedding_matrix,
    positive_caption_indices,
    sharpness_multiplier,
    additive_shift_term,
):
    here = lax.axis_index(AXES)
    k = here % LINE
    core = here // LINE % 2
    y = lap_of(here)
    scale = sharpness_multiplier[0]
    shift = additive_shift_term[0]
    images = [picture_embedding_matrix]
    text0 = caption_embedding_matrix
    text2 = group_onward(text0, y)
    images += [line_turned(picture_embedding_matrix, r) for r in (1, 2)]
    far = sent(text0, lambda b: b + 3 * LINE if b % GROUP == 5 else None)
    near = sent(text0, lambda b: b + LINE if b // LINE % 2 == 0 else None)
    crossed = sent(text2, lambda b: b + LINE if b // LINE % 2 == 0 else b - LINE)
    text1 = jnp.where(core == 1, near, crossed)
    text3 = jnp.where(core == 1, crossed, far)

    def negatives(logits):
        return scale * jax.nn.sigmoid(scale * logits + shift)

    def scores(a, b):
        return lax.dot_general(a, b, (((1,), (1,)), ((), ())), preferred_element_type=jnp.float32)

    def over_texts(coef, texts):
        return jnp.dot(coef, texts, preferred_element_type=jnp.float32)

    def over_images(coef, pictures):
        return lax.dot_general(coef, pictures, (((0,), (0,)), ((), ())), preferred_element_type=jnp.float32)

    pictures = jnp.concatenate(images)
    texts = jnp.concatenate([text0, text1, text2])
    logits = scores(pictures, texts)
    place = lax.broadcasted_iota(jnp.int32, logits.shape, 0)
    column = lax.broadcasted_iota(jnp.int32, logits.shape, 1)
    turn, which = place // ROWS, column // ROWS
    i = (k - turn + LINE) % LINE
    used = jnp.where(which == 0, i >= k, jnp.where(which == 1, True, i <= k + 1))
    wanted = jnp.concatenate([positive_caption_indices - here * ROWS, jnp.full((2 * ROWS,), -1, jnp.int32)])
    positive = wanted[:, None] == column
    tempered = scale * logits + shift
    sign = jnp.where(positive, -1.0, 1.0).astype(jnp.float32)
    coef = jnp.where(used, scale * sign * jax.nn.sigmoid(sign * tempered), 0.0).astype(LOW)
    coef3 = jnp.where(k == 2, negatives(scores(images[2], text3)), 0.0).astype(LOW)

    grad_texts = over_images(coef, pictures)
    grad_far = over_images(coef3, images[2])
    grad_images = over_texts(coef, texts)
    back = [
        line_turned(grad_images[ROWS : 2 * ROWS].astype(LOW), -1),
        line_turned((grad_images[2 * ROWS :] + over_texts(coef3, text3)).astype(LOW), -2),
    ]
    pair = jnp.stack([grad_texts[ROWS : 2 * ROWS].astype(LOW), grad_far.astype(LOW)])
    pair = sent(pair, lambda b: b + LINE if b // LINE % 2 == 0 else b - LINE).astype(jnp.float32)
    own = jnp.where(core == 0, pair[0], 0.0)
    earlier = grad_texts[2 * ROWS :] + jnp.where(core == 0, jnp.where(k == 2, pair[1], 0.0), pair[0])
    earlier = group_back(earlier.astype(LOW), y).astype(jnp.float32)
    far_back = sent(grad_far.astype(LOW), lambda b: b - 3 * LINE if b % GROUP == 2 else None).astype(jnp.float32)
    far_back = jnp.where(here % GROUP == 5, far_back, 0.0)
    grad_image = grad_images[:ROWS] + (back[0].astype(jnp.float32) + back[1].astype(jnp.float32))
    grad_text = grad_texts[:ROWS] + own + earlier + far_back
    return grad_image, grad_text


def solution(mesh):
    in_specs = (P(AXES, None), P(AXES, None), P(AXES), P(), P())
    out_specs = (P(AXES, None), P(AXES, None))
    return jax.shard_map(
        on_device, mesh=mesh, in_specs=in_specs, out_specs=out_specs, check_vma=False
    )
```

time: 289 us -> 126 us (0.44)
  the two profiles are of different devices: /device:TPU:1 before, /device:TPU:65 now
where the time goes in v1:
time: 126 us; the launch traced here: 125 us
  waiting for transfers between devices  59.9 us (48%)
  starting transfers between devices  42.9 us (34%)
  other arithmetic  7.9 us (6%)
  matrix products  7.25 us (6%)
  local copies, waits for them, and re-layouts  4.59 us (4%)
  between operations  2.46 us (2%)
    ppermute x15, waiting for transfers between devices, sent(): return lax.ppermute(value, AXES, pairs)  59.9 us
    ppermute x15, starting transfers between devices, sent(): return lax.ppermute(value, AXES, pairs)  42.9 us
    dot_general x2, matrix products, over_texts(): return jnp.dot(coef, texts, preferred_element_type=jnp.float32)  3.59 us
    unnamed x22, local copies, waits for them, and re-layouts  2.67 us
  transfers between devices with their start and end apart: 15, of which 7 were waited for; matrix products, arithmetic and copies ran while one was open for 10% of the time, Pallas kernels for 0%

profile of v1, /device:TPU:65, one launch (start us, length us, event | category | flops | bytes accessed | tf_op | source)
XLA Modules:
  0.0 125.0 jit_solution(10272437932387516755)
XLA Ops:
  0.6 4.1 %collective-permute-start = (bf16[192,1152]{1,0:T(8,128)(2,1)}, bf16[192,1152]{1,0:T(8,128)(2,1)S(1)}, u32[]{:S(2)}, u32[]{:S(2)}) collective-permute-start(bf16[192,1152]{1,0:T(8,128)(2,1)} %param.5), channel_id=1, source_target_pairs={{0,1},{1,2},{2,0},{3,4},{4,5},{5,3},{6,7},{7,8},{8,6},{9,10},{10,1... | collective-permute-start | bytes 1327112 | tf_op jit(solution)/shard_map/ppermute | solution.py:21
  4.8 1.9 %collective-permute-start.1 = (bf16[192,1152]{1,0:T(8,128)(2,1)}, bf16[192,1152]{1,0:T(8,128)(2,1)S(1)}, u32[]{:S(2)}, u32[]{:S(2)}) collective-permute-start(bf16[192,1152]{1,0:T(8,128)(2,1)} %param.5), channel_id=1, source_target_pairs={{0,2},{1,0},{2,1},{3,5},{4,3},{5,4},{6,8},{7,6},{8,7},{9,11},{10,9... | collective-permute-start | bytes 1327112 | tf_op jit(solution)/shard_map/ppermute | solution.py:21
  6.7 3.2 %collective-permute-start.3 = (bf16[192,1152]{1,0:T(8,128)(2,1)}, bf16[192,1152]{1,0:T(8,128)(2,1)S(1)}, u32[]{:S(2)}, u32[]{:S(2)}) collective-permute-start(bf16[192,1152]{1,0:T(8,128)(2,1)} %param.6), channel_id=1, source_target_pairs={{0,6},{1,7},{2,8},{3,9},{4,10},{5,11},{6,12},{7,13},{8,14},{9,15},... | collective-permute-start | bytes 1327112 | tf_op jit(solution)/shard_map/ppermute | solution.py:21
  9.9 1.3 %collective-permute-start.2 = (bf16[192,1152]{1,0:T(8,128)(2,1)}, bf16[192,1152]{1,0:T(8,128)(2,1)S(1)}, u32[]{:S(2)}, u32[]{:S(2)}) collective-permute-start(bf16[192,1152]{1,0:T(8,128)(2,1)} %param.6), channel_id=1, source_target_pairs={{0,3},{1,4},{2,5},{6,9},{7,10},{8,11},{12,15},{13,16},{14,17},{18,... | collective-permute-start | bytes 1327112 | tf_op jit(solution)/shard_map/ppermute | solution.py:21
  12.2 1.3 %collective-permute-start.5 = (bf16[96,1152]{1,0:T(8,128)(2,1)S(1)}, bf16[96,1152]{1,0:T(8,128)(2,1)S(1)}, u32[]{:S(2)}, u32[]{:S(2)}) collective-permute-start(bf16[96,1152]{1,0:T(8,128)(2,1)S(1)} %slice.40), channel_id=1, source_target_pairs={{42,48},{43,49},{44,50},{45,51},{46,52},{47,53},{90,96},{91,97},{9... | collective-permute-start | bytes 663560 | tf_op jit(solution)/shard_map/ppermute | solution.py:21
  15.6 2.1 %collective-permute-done.3 = bf16[192,1152]{1,0:T(8,128)(2,1)S(1)} collective-permute-done((bf16[192,1152]{1,0:T(8,128)(2,1)}, bf16[192,1152]{1,0:T(8,128)(2,1)S(1)}, u32[]{:S(2)}, u32[]{:S(2)}) %collective-permute-start.3) | collective-permute-done | bytes 442400 | tf_op jit(solution)/shard_map/ppermute | solution.py:21
  17.7 13.0 %collective-permute-start.4 = (bf16[96,1152]{1,0:T(8,128)(2,1)S(1)}, bf16[96,1152]{1,0:T(8,128)(2,1)S(1)}, u32[]{:S(2)}, u32[]{:S(2)}) collective-permute-start(bf16[96,1152]{1,0:T(8,128)(2,1)S(1)} %slice.51), channel_id=1, source_target_pairs={{0,48},{1,49},{2,50},{3,51},{4,52},{5,53},{48,96},{49,97},{50,98},... | collective-permute-start | bytes 663560 | tf_op jit(solution)/shard_map/ppermute | solution.py:21
  31.8 24.0 %collective-permute-done.5 = bf16[96,1152]{1,0:T(8,128)(2,1)S(1)} collective-permute-done((bf16[96,1152]{1,0:T(8,128)(2,1)S(1)}, bf16[96,1152]{1,0:T(8,128)(2,1)S(1)}, u32[]{:S(2)}, u32[]{:S(2)}) %collective-permute-start.5) | collective-permute-done | bytes 221216 | tf_op jit(solution)/shard_map/ppermute | solution.py:21
  56.5 3.5 %collective-permute-start.6 = (bf16[192,1152]{1,0:T(8,128)(2,1)S(1)}, bf16[192,1152]{1,0:T(8,128)(2,1)S(1)}, u32[]{:S(2)}, u32[]{:S(2)}) collective-permute-start(bf16[192,1152]{1,0:T(8,128)(2,1)S(1)} %maximum_select_fusion), channel_id=1, source_target_pairs={{0,3},{1,4},{2,5},{3,0},{4,1},{5,2},{6,9},{7,10},{8,11},{9,6},{10,... | collective-permute-start | bytes 1327112 | tf_op jit(solution)/shard_map/ppermute | solution.py:21
  60.1 1.3 %collective-permute-done.6 = bf16[192,1152]{1,0:T(8,128)(2,1)S(1)} collective-permute-done((bf16[192,1152]{1,0:T(8,128)(2,1)S(1)}, bf16[192,1152]{1,0:T(8,128)(2,1)S(1)}, u32[]{:S(2)}, u32[]{:S(2)}) %collective-permute-start.6) | collective-permute-done | bytes 442400 | tf_op jit(solution)/shard_map/ppermute | solution.py:21
  61.5 1.7 %fusion.2 = bf16[576,576]{1,0:T(8,128)(2,1)S(1)} fusion(bf16[576,1152]{1,0:T(8,128)(2,1)S(1)} %constant_dynamic-update-slice_fusion, f32[]{:T(128)} %bitcast.23, s32[576]{0:T(1024)S(1)} %concatenate.15, f32[]{:T(128)} %bitcast.21, s32[]{:T(128)S(6)} %add.84, s32[576]{0:T(1024)S(1)} %get-tuple-element.2, s32[576]{0:T(1024)S(1)} %get-tuple-element.3, ...), kind=kOutput, calls=%fused_computation.8 | convolution fusion | flops 777682944 | bytes 3325264 | tf_op jit(solution)/shard_map/dot_general | solution.py:71
  63.2 1.3 %fusion.37 = f32[576,1152]{1,0:T(8,128)S(1)} fusion(bf16[576,576]{1,0:T(8,128)(2,1)S(1)} %fusion.2, bf16[576,1152]{1,0:T(8,128)(2,1)S(1)} %constant_dynamic-update-slice_fusion), kind=kOutput, calls=%fused_computation.66 | convolution fusion | flops 764411904 | bytes 4644864 | tf_op jit(solution)/shard_map/dot_general | solution.py:77
  66.9 2.3 %collective-permute-start.10 = (bf16[2,192,1152]{2,1,0:T(8,128)(2,1)S(1)}, bf16[2,192,1152]{2,1,0:T(8,128)(2,1)S(1)}, u32[]{:S(2)}, u32[]{:S(2)}) collective-permute-start(bf16[2,192,1152]{2,1,0:T(8,128)(2,1)S(1)} %pad_maximum_fusion.1), channel_id=1, source_target_pairs={{0,3},{1,4},{2,5},{3,0},{4,1},{5,2},{6,9},{7,10},{8,11},{9,6},{10,... | collective-permute-start | bytes 2654216 | tf_op jit(solution)/shard_map/ppermute | solution.py:21
  69.2 2.5 %fusion.29 = f32[576,1152]{1,0:T(8,128)S(1)} fusion(bf16[576,576]{1,0:T(8,128)(2,1)} %copy-done.9, bf16[192,1152]{1,0:T(8,128)(2,1)S(1)} %copy-done.5, bf16[192,1152]{1,0:T(8,128)(2,1)S(1)} %broadcast_select_fusion.1, bf16[192,1152]{1,0:T(8,128)(2,1)} %param.6), kind=kOutput, calls=%fused_computation.46 | convolution fusion | flops 768393216 | bytes 4644864 | tf_op jit(solution)/shard_map/dot_general | solution.py:74
  71.9 2.0 %fusion.25 = bf16[192,1152]{1,0:T(8,128)(2,1)S(1)} fusion(f32[2,192,1152]{2,1,0:T(8,128)S(1)} %convert_element_type.39, f32[576,1152]{1,0:T(8,128)} %copy-done, pred[]{:T(512)S(6)} %eq.50, pred[]{:T(512)S(6)} %eq.51), kind=kLoop, calls=%fused_computation.36 | loop fusion | flops 884736 | bytes 3096578 | tf_op jit(solution)/shard_map/convert_element_type | solution.py:105
  73.9 1.9 %collective-permute-start.11 = (bf16[192,1152]{1,0:T(8,128)(2,1)S(1)}, bf16[192,1152]{1,0:T(8,128)(2,1)S(1)}, u32[]{:S(2)}, u32[]{:S(2)}) collective-permute-start(bf16[192,1152]{1,0:T(8,128)(2,1)S(1)} %fusion.25), channel_id=1, source_target_pairs={{0,42},{1,43},{2,44},{3,45},{4,46},{5,47},{6,0},{7,1},{8,2},{9,3},... | collective-permute-start | bytes 1327112 | tf_op jit(solution)/shard_map/ppermute | solution.py:21
  77.8 1.9 %collective-permute-start.9 = (bf16[192,1152]{1,0:T(8,128)(2,1)}, bf16[192,1152]{1,0:T(8,128)(2,1)}, u32[]{:S(2)}, u32[]{:S(2)}) collective-permute-start(bf16[192,1152]{1,0:T(8,128)(2,1)} %fusion.28), channel_id=1, source_target_pairs={{0,1},{1,2},{2,0},{3,4},{4,5},{5,3},{6,7},{7,8},{8,6},{9,10},{10,1... | collective-permute-start | bytes 1327112 | tf_op jit(solution)/shard_map/ppermute | solution.py:21
  79.7 5.2 %collective-permute-start.7 = (bf16[192,1152]{1,0:T(8,128)(2,1)}, bf16[192,1152]{1,0:T(8,128)(2,1)}, u32[]{:S(2)}, u32[]{:S(2)}) collective-permute-start(bf16[192,1152]{1,0:T(8,128)(2,1)} %slice.87), channel_id=1, source_target_pairs={{0,2},{1,0},{2,1},{3,5},{4,3},{5,4},{6,8},{7,6},{8,7},{9,11},{10,9... | collective-permute-start | bytes 1327112 | tf_op jit(solution)/shard_map/ppermute | solution.py:21
  85.6 1.3 %collective-permute-start.13 = (bf16[96,1152]{1,0:T(8,128)(2,1)S(1)}, bf16[96,1152]{1,0:T(8,128)(2,1)S(1)}, u32[]{:S(2)}, u32[]{:S(2)}) collective-permute-start(bf16[96,1152]{1,0:T(8,128)(2,1)S(1)} %slice.61), channel_id=1, source_target_pairs={{0,762},{1,763},{2,764},{3,765},{4,766},{5,767},{48,42},{49,43},{5... | collective-permute-start | bytes 663560 | tf_op jit(solution)/shard_map/ppermute | solution.py:21
  88.3 5.4 %collective-permute-done.9 = bf16[192,1152]{1,0:T(8,128)(2,1)} collective-permute-done((bf16[192,1152]{1,0:T(8,128)(2,1)}, bf16[192,1152]{1,0:T(8,128)(2,1)}, u32[]{:S(2)}, u32[]{:S(2)}) %collective-permute-start.9) | collective-permute-done | bytes 442400 | tf_op jit(solution)/shard_map/ppermute | solution.py:21
  93.7 13.6 %collective-permute-done.7 = bf16[192,1152]{1,0:T(8,128)(2,1)} collective-permute-done((bf16[192,1152]{1,0:T(8,128)(2,1)}, bf16[192,1152]{1,0:T(8,128)(2,1)}, u32[]{:S(2)}, u32[]{:S(2)}) %collective-permute-start.7) | collective-permute-done | bytes 442400 | tf_op jit(solution)/shard_map/ppermute | solution.py:21
  107.3 2.4 %slice_add_fusion.2 = f32[192,1152]{1,0:T(8,128)} fusion(f32[576,1152]{1,0:T(8,128)} %copy-done.1, bf16[192,1152]{1,0:T(8,128)(2,1)} %collective-permute-done.9, bf16[192,1152]{1,0:T(8,128)(2,1)} %collective-permute-done.7), kind=kLoop, calls=%fused_computation.44 | loop fusion | flops 884736 | bytes 2654208 | tf_op jit(solution)/shard_map/add | solution.py:108
  109.7 12.9 %collective-permute-done.13 = bf16[96,1152]{1,0:T(8,128)(2,1)S(1)} collective-permute-done((bf16[96,1152]{1,0:T(8,128)(2,1)S(1)}, bf16[96,1152]{1,0:T(8,128)(2,1)S(1)}, u32[]{:S(2)}, u32[]{:S(2)}) %collective-permute-start.13) | collective-permute-done | bytes 221216 | tf_op jit(solution)/shard_map/ppermute | solution.py:21
  122.6 2.4 %fusion.27 = f32[192,1152]{1,0:T(8,128)} fusion(f32[576,1152]{1,0:T(8,128)} %copy-done, bf16[192,1152]{1,0:T(8,128)(2,1)S(1)} %collective-permute-done.14, f32[2,192,1152]{2,1,0:T(8,128)S(1)} %convert_element_type.39, bf16[192,1152]{1,0:T(8,128)(2,1)S(1)} %collective-permute-done.11, bf16[96,1152]{1,0:T(8,128)(2,1)S(1)} %collective-permute-done.13, ...), kind=kLoop, calls=%fused_computation.40 | loop fusion | flops 2654208 | bytes 3981315 | tf_op jit(solution)/shard_map/add | solution.py:109
  (52 shorter events, 10.1 us)
Async XLA Ops:
  0.6 55.1 %copy-start.8 = (bf16[192,1152]{1,0:T(8,128)(2,1)S(1)}, bf16[192,1152]{1,0:T(8,128)(2,1)}, u32[]{:S(2)}) copy-start(bf16[192,1152]{1,0:T(8,128)(2,1)} %param.6) | copy-start | bytes 1327108
  0.6 59.4 %collective-permute-start = (bf16[192,1152]{1,0:T(8,128)(2,1)}, bf16[192,1152]{1,0:T(8,128)(2,1)S(1)}, u32[]{:S(2)}, u32[]{:S(2)}) collective-permute-start(bf16[192,1152]{1,0:T(8,128)(2,1)} %param.5), channel_id=1, source_target_pairs={{0,1},{1,2},{2,0},{3,4},{4,5},{5,3},{6,7},{7,8},{8,6},{9,10},{10,1... | collective-permute-start | bytes 1327112 | tf_op jit(solution)/shard_map/ppermute | solution.py:21
  4.8 55.3 %collective-permute-start.1 = (bf16[192,1152]{1,0:T(8,128)(2,1)}, bf16[192,1152]{1,0:T(8,128)(2,1)S(1)}, u32[]{:S(2)}, u32[]{:S(2)}) collective-permute-start(bf16[192,1152]{1,0:T(8,128)(2,1)} %param.5), channel_id=1, source_target_pairs={{0,2},{1,0},{2,1},{3,5},{4,3},{5,4},{6,8},{7,6},{8,7},{9,11},{10,9... | collective-permute-start | bytes 1327112 | tf_op jit(solution)/shard_map/ppermute | solution.py:21
  6.7 11.0 %collective-permute-start.3 = (bf16[192,1152]{1,0:T(8,128)(2,1)}, bf16[192,1152]{1,0:T(8,128)(2,1)S(1)}, u32[]{:S(2)}, u32[]{:S(2)}) collective-permute-start(bf16[192,1152]{1,0:T(8,128)(2,1)} %param.6), channel_id=1, source_target_pairs={{0,6},{1,7},{2,8},{3,9},{4,10},{5,11},{6,12},{7,13},{8,14},{9,15},... | collective-permute-start | bytes 1327112 | tf_op jit(solution)/shard_map/ppermute | solution.py:21
  9.9 50.2 %collective-permute-start.2 = (bf16[192,1152]{1,0:T(8,128)(2,1)}, bf16[192,1152]{1,0:T(8,128)(2,1)S(1)}, u32[]{:S(2)}, u32[]{:S(2)}) collective-permute-start(bf16[192,1152]{1,0:T(8,128)(2,1)} %param.6), channel_id=1, source_target_pairs={{0,3},{1,4},{2,5},{6,9},{7,10},{8,11},{12,15},{13,16},{14,17},{18,... | collective-permute-start | bytes 1327112 | tf_op jit(solution)/shard_map/ppermute | solution.py:21
  12.2 43.5 %collective-permute-start.5 = (bf16[96,1152]{1,0:T(8,128)(2,1)S(1)}, bf16[96,1152]{1,0:T(8,128)(2,1)S(1)}, u32[]{:S(2)}, u32[]{:S(2)}) collective-permute-start(bf16[96,1152]{1,0:T(8,128)(2,1)S(1)} %slice.40), channel_id=1, source_target_pairs={{42,48},{43,49},{44,50},{45,51},{46,52},{47,53},{90,96},{91,97},{9... | collective-permute-start | bytes 663560 | tf_op jit(solution)/shard_map/ppermute | solution.py:21
  17.7 38.7 %collective-permute-start.4 = (bf16[96,1152]{1,0:T(8,128)(2,1)S(1)}, bf16[96,1152]{1,0:T(8,128)(2,1)S(1)}, u32[]{:S(2)}, u32[]{:S(2)}) collective-permute-start(bf16[96,1152]{1,0:T(8,128)(2,1)S(1)} %slice.51), channel_id=1, source_target_pairs={{0,48},{1,49},{2,50},{3,51},{4,52},{5,53},{48,96},{49,97},{50,98},... | collective-permute-start | bytes 663560 | tf_op jit(solution)/shard_map/ppermute | solution.py:21
  55.7 8.9 %collective-permute-start.8 = (bf16[192,1152]{1,0:T(8,128)(2,1)S(1)}, bf16[192,1152]{1,0:T(8,128)(2,1)S(1)}, u32[]{:S(2)}, u32[]{:S(2)}) collective-permute-start(bf16[192,1152]{1,0:T(8,128)(2,1)S(1)} %copy-done.8), channel_id=1, source_target_pairs={{5,14},{11,20},{17,26},{23,32},{29,38},{35,44},{41,50},{47,56},{53... | collective-permute-start | bytes 1327112 | tf_op jit(solution)/shard_map/ppermute | solution.py:21
  56.5 4.9 %copy-start.4 = (bf16[192,1152]{1,0:T(8,128)(2,1)}, bf16[192,1152]{1,0:T(8,128)(2,1)S(1)}, u32[]{:S(2)}) copy-start(bf16[192,1152]{1,0:T(8,128)(2,1)S(1)} %maximum_select_fusion) | copy-start | bytes 1327108
  56.5 4.9 %collective-permute-start.6 = (bf16[192,1152]{1,0:T(8,128)(2,1)S(1)}, bf16[192,1152]{1,0:T(8,128)(2,1)S(1)}, u32[]{:S(2)}, u32[]{:S(2)}) collective-permute-start(bf16[192,1152]{1,0:T(8,128)(2,1)S(1)} %maximum_select_fusion), channel_id=1, source_target_pairs={{0,3},{1,4},{2,5},{3,0},{4,1},{5,2},{6,9},{7,10},{8,11},{9,6},{10,... | collective-permute-start | bytes 1327112 | tf_op jit(solution)/shard_map/ppermute | solution.py:21
  63.2 1.4 %copy-start.9 = (bf16[576,576]{1,0:T(8,128)(2,1)}, bf16[576,576]{1,0:T(8,128)(2,1)S(1)}, u32[]{:S(2)}) copy-start(bf16[576,576]{1,0:T(8,128)(2,1)S(1)} %fusion.2) | copy-start | bytes 1990660
  64.5 1.7 %copy-start = (f32[576,1152]{1,0:T(8,128)}, f32[576,1152]{1,0:T(8,128)S(1)}, u32[]{:S(2)}) copy-start(f32[576,1152]{1,0:T(8,128)S(1)} %fusion.37) | copy-start | bytes 7962628
  64.6 0.9 copy-start.2
  66.2 3.0 %copy-start.5 = (bf16[192,1152]{1,0:T(8,128)(2,1)S(1)}, bf16[192,1152]{1,0:T(8,128)(2,1)}, u32[]{:S(2)}) copy-start(bf16[192,1152]{1,0:T(8,128)(2,1)} %copy-done.4) | copy-start | bytes 1327108
  66.9 4.8 %collective-permute-start.10 = (bf16[2,192,1152]{2,1,0:T(8,128)(2,1)S(1)}, bf16[2,192,1152]{2,1,0:T(8,128)(2,1)S(1)}, u32[]{:S(2)}, u32[]{:S(2)}) collective-permute-start(bf16[2,192,1152]{2,1,0:T(8,128)(2,1)S(1)} %pad_maximum_fusion.1), channel_id=1, source_target_pairs={{0,3},{1,4},{2,5},{3,0},{4,1},{5,2},{6,9},{7,10},{8,11},{9,6},{10,... | collective-permute-start | bytes 2654216 | tf_op jit(solution)/shard_map/ppermute | solution.py:21
  71.7 5.3 %copy-start.1 = (f32[576,1152]{1,0:T(8,128)}, f32[576,1152]{1,0:T(8,128)S(1)}, u32[]{:S(2)}) copy-start(f32[576,1152]{1,0:T(8,128)S(1)} %fusion.29) | copy-start | bytes 7962628
  71.9 4.0 %copy-start.3 = (bf16[192,1152]{1,0:T(8,128)(2,1)S(1)}, bf16[192,1152]{1,0:T(8,128)(2,1)}, u32[]{:S(2)}) copy-start(bf16[192,1152]{1,0:T(8,128)(2,1)} %copy-done.2) | copy-start | bytes 1327108
  71.9 4.0 %copy-start.7 = (bf16[192,192]{1,0:T(8,128)(2,1)S(1)}, bf16[192,192]{1,0:T(8,128)(2,1)}, u32[]{:S(2)}) copy-start(bf16[192,192]{1,0:T(8,128)(2,1)} %copy-done.6) | copy-start | bytes 221188
  73.9 13.6 %collective-permute-start.11 = (bf16[192,1152]{1,0:T(8,128)(2,1)S(1)}, bf16[192,1152]{1,0:T(8,128)(2,1)S(1)}, u32[]{:S(2)}, u32[]{:S(2)}) collective-permute-start(bf16[192,1152]{1,0:T(8,128)(2,1)S(1)} %fusion.25), channel_id=1, source_target_pairs={{0,42},{1,43},{2,44},{3,45},{4,46},{5,47},{6,0},{7,1},{8,2},{9,3},... | collective-permute-start | bytes 1327112 | tf_op jit(solution)/shard_map/ppermute | solution.py:21
  77.8 15.9 %collective-permute-start.9 = (bf16[192,1152]{1,0:T(8,128)(2,1)}, bf16[192,1152]{1,0:T(8,128)(2,1)}, u32[]{:S(2)}, u32[]{:S(2)}) collective-permute-start(bf16[192,1152]{1,0:T(8,128)(2,1)} %fusion.28), channel_id=1, source_target_pairs={{0,1},{1,2},{2,0},{3,4},{4,5},{5,3},{6,7},{7,8},{8,6},{9,10},{10,1... | collective-permute-start | bytes 1327112 | tf_op jit(solution)/shard_map/ppermute | solution.py:21
  79.7 27.6 %collective-permute-start.7 = (bf16[192,1152]{1,0:T(8,128)(2,1)}, bf16[192,1152]{1,0:T(8,128)(2,1)}, u32[]{:S(2)}, u32[]{:S(2)}) collective-permute-start(bf16[192,1152]{1,0:T(8,128)(2,1)} %slice.87), channel_id=1, source_target_pairs={{0,2},{1,0},{2,1},{3,5},{4,3},{5,4},{6,8},{7,6},{8,7},{9,11},{10,9... | collective-permute-start | bytes 1327112 | tf_op jit(solution)/shard_map/ppermute | solution.py:21
  84.9 24.8 %collective-permute-start.14 = (bf16[192,1152]{1,0:T(8,128)(2,1)S(1)}, bf16[192,1152]{1,0:T(8,128)(2,1)S(1)}, u32[]{:S(2)}, u32[]{:S(2)}) collective-permute-start(bf16[192,1152]{1,0:T(8,128)(2,1)S(1)} %convolution_convert_fusion), channel_id=1, source_target_pairs={{2,761},{8,767},{14,5},{20,11},{26,17},{32,23},{38,29},{44,35},{50... | collective-permute-start | bytes 1327112 | tf_op jit(solution)/shard_map/ppermute | solution.py:21
  85.6 37.0 %collective-permute-start.13 = (bf16[96,1152]{1,0:T(8,128)(2,1)S(1)}, bf16[96,1152]{1,0:T(8,128)(2,1)S(1)}, u32[]{:S(2)}, u32[]{:S(2)}) collective-permute-start(bf16[96,1152]{1,0:T(8,128)(2,1)S(1)} %slice.61), channel_id=1, source_target_pairs={{0,762},{1,763},{2,764},{3,765},{4,766},{5,767},{48,42},{49,43},{5... | collective-permute-start | bytes 663560 | tf_op jit(solution)/shard_map/ppermute | solution.py:21
  87.6 35.1 %collective-permute-start.12 = (bf16[96,1152]{1,0:T(8,128)(2,1)S(1)}, bf16[96,1152]{1,0:T(8,128)(2,1)S(1)}, u32[]{:S(2)}, u32[]{:S(2)}) collective-permute-start(bf16[96,1152]{1,0:T(8,128)(2,1)S(1)} %slice.60), channel_id=1, source_target_pairs={{42,762},{43,763},{44,764},{45,765},{46,766},{47,767},{90,42},{91,... | collective-permute-start | bytes 663560 | tf_op jit(solution)/shard_map/ppermute | solution.py:21
  (1 other events, 0.6 us)

commit v2 on v1

v2 whole, which is shorter than its diff:
```python
import jax
import jax.numpy as jnp
from jax import lax
from jax.experimental import pallas as pl
from jax.experimental.pallas import tpu as pltpu
from jax.sharding import PartitionSpec as P

AXES = ("dp", "mp")
ROWS = 192
D = 1152
LINE = 3
GROUP = 6
LAP = 8
NB = 768
LOW = jnp.bfloat16
F32 = jnp.float32


def lap_of(b):
    return (b // GROUP) % LAP


def core_of(b):
    return b // LINE % 2


def sent(value, target):
    pairs = [(b, target(b) % NB) for b in range(NB) if target(b) is not None]
    return lax.ppermute(value, AXES, pairs)


def line_turned(value, by):
    return sent(value, lambda b: b // LINE * LINE + (b + by) % LINE)


def cores_swapped(value):
    return sent(value, lambda b: b + LINE if core_of(b) == 0 else b - LINE)


def plane(b, by):
    step = b % LINE if core_of(b) == 0 else GROUP - 1 - b % LINE
    return step if by > 0 else LAP - 1 - step


def detour(value, by):
    start = LAP - 1 if by > 0 else 0
    return sent(value, lambda b: b + GROUP * (plane(b, by) - start) if lap_of(b) == start else None)


def after_detour(value, by):
    end = 0 if by > 0 else LAP - 1
    return sent(value, lambda b: b + GROUP * (by * LAP + end - lap_of(b)) if lap_of(b) == plane(b, by) else None)


def straight(value, by):
    start = LAP - 1 if by > 0 else 0
    return sent(value, lambda b: None if lap_of(b) == start else b + by * GROUP)


def scores(texts, pictures):
    return lax.dot_general(texts, pictures, (((1,), (1,)), ((), ())), preferred_element_type=F32)


def matmul(a, b):
    return jnp.dot(a, b, preferred_element_type=F32)


def own_texts(k_ref, scale_ref, shift_ref, wanted, i0, i1, i2, t0, pictures, coef, gt0):
    scale, shift, k = scale_ref[0], shift_ref[0], k_ref[0]
    pictures[0:ROWS] = i0[...]
    pictures[ROWS : 2 * ROWS] = i1[...]
    pictures[2 * ROWS :] = i2[...]
    logits = scores(t0[...], pictures[...])
    row = lax.broadcasted_iota(jnp.int32, logits.shape, 0)
    column = lax.broadcasted_iota(jnp.int32, logits.shape, 1)
    sign = jnp.where(wanted[...] == row, -1.0, 1.0).astype(F32)
    value = scale * sign * jax.nn.sigmoid(sign * (scale * logits + shift))
    one = (column >= ROWS) & (column < 2 * ROWS)
    unused = (one & (k != 0)) | ((column >= 2 * ROWS) & (k == 2))
    coef[...] = jnp.where(unused, 0.0, value).astype(LOW)
    gt0[...] = matmul(coef[...], pictures[...])


def over_texts(coef, texts):
    return lax.dot_general(coef, texts, (((0,), (0,)), ((), ())), preferred_element_type=F32)


def other_texts(
    k_ref, core_ref, scale_ref, shift_ref, near, crossed, t2, t0, i2, pictures, coef0,
    pair, gt2, gi0, gi1, gi2, texts, coef,
):
    scale, shift, k, core = scale_ref[0], shift_ref[0], k_ref[0], core_ref[0]
    texts[ROWS : 2 * ROWS] = t2[...]
    texts[2 * ROWS :] = t0[...]
    coef[2 * ROWS :] = coef0[...]

    @pl.when(core == 0)
    def _():
        texts[0:ROWS] = crossed[...]

    @pl.when(core != 0)
    def _():
        texts[0:ROWS] = near[...]

    two = slice(0, 2 * ROWS)
    logits = scores(texts[two], pictures[...])
    row = lax.broadcasted_iota(jnp.int32, logits.shape, 0)
    column = lax.broadcasted_iota(jnp.int32, logits.shape, 1)
    value = scale * jax.nn.sigmoid(scale * logits + shift)
    unused = (row >= ROWS) & (column >= ROWS) & (column < 2 * ROWS) & (k == 0)
    coef[two] = jnp.where(unused, 0.0, value).astype(LOW)
    by_text = matmul(coef[two], pictures[...])
    pair[0] = by_text[0:ROWS].astype(LOW)
    gt2[...] = by_text[ROWS:]
    by_image = over_texts(coef[...], texts[...])
    gi0[...] = by_image[0:ROWS]
    gi1[...] = by_image[ROWS : 2 * ROWS].astype(LOW)

    @pl.when(k != 2)
    def _():
        gi2[...] = by_image[2 * ROWS :].astype(LOW)
        pair[1] = jnp.zeros((ROWS, D), LOW)

    def with_far(t3):
        far = (scale * jax.nn.sigmoid(scale * scores(t3[...], i2[...]) + shift)).astype(LOW)
        pair[1] = matmul(far, i2[...]).astype(LOW)
        gi2[...] = (by_image[2 * ROWS :] + over_texts(far, t3[...])).astype(LOW)

    @pl.when((k == 2) & (core == 0))
    def _():
        with_far(near)

    @pl.when((k == 2) & (core != 0))
    def _():
        with_far(crossed)


def kernel_call(body, n_small, args, outs, scratch=()):
    return pl.pallas_call(
        body,
        out_shape=[jax.ShapeDtypeStruct(shape, kind) for shape, kind in outs],
        in_specs=[pl.BlockSpec(memory_space=pltpu.SMEM)] * n_small
        + [pl.BlockSpec(memory_space=pltpu.VMEM)] * (len(args) - n_small),
        out_specs=[pl.BlockSpec(memory_space=pltpu.VMEM)] * len(outs),
        scratch_shapes=[pltpu.VMEM(shape, LOW) for shape in scratch],
        compiler_params=pltpu.CompilerParams(vmem_limit_bytes=12 * 1024 * 1024),
    )(*args)


def on_device(
    picture_embedding_matrix,
    caption_embedding_matrix,
    positive_caption_indices,
    sharpness_multiplier,
    additive_shift_term,
):
    here = lax.axis_index(AXES)
    k = here % LINE
    core = core_of(here)
    y = lap_of(here)
    image0, text0 = picture_embedding_matrix, caption_embedding_matrix
    small = [k.astype(jnp.int32).reshape(1), sharpness_multiplier, additive_shift_term]
    wanted = jnp.concatenate([positive_caption_indices - here * ROWS, jnp.full((2 * ROWS,), -1, jnp.int32)])[None]
    block, three = (ROWS, D), LINE * ROWS

    corner = detour(text0, 1)
    main = straight(text0, 1)
    image1 = line_turned(image0, 1)
    image2 = line_turned(image0, 2)
    near = sent(text0, lambda b: b + LINE if core_of(b) == 0 else (b + 3 * LINE if b % GROUP == 5 else None))
    relayed = after_detour(corner, 1)
    image1, image2, near, main, relayed = lax.optimization_barrier((image1, image2, near, main, relayed))
    pictures, coef0, gt0 = kernel_call(
        own_texts,
        3,
        small + [wanted, image0, image1, image2, text0],
        [((three, D), LOW), ((ROWS, three), LOW), (block, F32)],
    )
    text2 = jnp.where(y == 0, relayed, main)
    crossed = cores_swapped(text2)
    pair, gt2, gi0, gi1, gi2 = kernel_call(
        other_texts,
        4,
        [small[0], core.astype(jnp.int32).reshape(1), *small[1:], near, crossed, text2, text0, image2, pictures, coef0],
        [((2, ROWS, D), LOW), (block, F32), (block, F32), (block, LOW), (block, LOW)],
        [(three, D), (three, three)],
    )
    other = cores_swapped(pair)
    earlier = (gt2 + jnp.where(core == 0, other[1], other[0]).astype(F32)).astype(LOW)
    back_corner = detour(earlier, -1)
    back_main = straight(earlier, -1)
    far = sent(pair[1], lambda b: b - 3 * LINE if b % GROUP == 2 else None)
    back1 = line_turned(gi1, -1)
    back2 = line_turned(gi2, -2)
    back_relayed = after_detour(back_corner, -1)
    back_text = jnp.where(y == LAP - 1, back_relayed, back_main)
    rest = jnp.where(core == 0, other[0].astype(F32), jnp.where(k == 2, far.astype(F32), 0.0))
    grad_text = gt0 + rest + back_text.astype(F32)
    grad_image = gi0 + (back1.astype(F32) + back2.astype(F32))
    return grad_image, grad_text


def solution(mesh):
    in_specs = (P(AXES, None), P(AXES, None), P(AXES), P(), P())
    out_specs = (P(AXES, None), P(AXES, None))
    return jax.shard_map(
        on_device, mesh=mesh, in_specs=in_specs, out_specs=out_specs, check_vma=False
    )
```

time: 126 us -> 94.9 us (0.75)
  the two profiles are of different devices: /device:TPU:65 before, /device:TPU:1 now
where the time goes in v2:
time: 94.9 us; the launch traced here: 94.4 us
  waiting for transfers between devices  50.8 us (54%)
  starting transfers between devices  28.9 us (30%)
  Pallas kernels  6.42 us (7%)
  local copies, waits for them, and re-layouts  3.51 us (4%)
  other arithmetic  2.46 us (3%)
  between operations  2.31 us (2%)
    ppermute x14, waiting for transfers between devices, sent(): return lax.ppermute(value, AXES, pairs)  50.8 us
    ppermute x14, starting transfers between devices, sent(): return lax.ppermute(value, AXES, pairs)  28.9 us
    pallas_call x2, Pallas kernels, kernel_call(): pl.pallas_call(body, out_shape=[jax.ShapeDtypeStruct(shape, kind) for sha...  6.42 us
    unnamed x14, local copies, waits for them, and re-layouts  2.46 us
  transfers between devices with their start and end apart: 14, of which 5 were waited for; matrix products, arithmetic and copies ran while one was open for 2% of the time, Pallas kernels for 1%

profile of v2, /device:TPU:1, one launch (start us, length us, event | category | flops | bytes accessed | tf_op | source)
XLA Modules:
  0.0 94.4 jit_solution(10760376336530562418)
XLA Ops:
  0.7 0.8 collective-permute-start.4
  1.5 4.8 %collective-permute-start = (bf16[192,1152]{1,0:T(8,128)(2,1)}, bf16[192,1152]{1,0:T(8,128)(2,1)S(1)}, u32[]{:S(2)}, u32[]{:S(2)}) collective-permute-start(bf16[192,1152]{1,0:T(8,128)(2,1)} %i0.1), channel_id=1, source_target_pairs={{0,1},{1,2},{2,0},{3,4},{4,5},{5,3},{6,7},{7,8},{8,6},{9,10},{10,1... | collective-permute-start | bytes 1327112 | tf_op jit(solution)/shard_map/ppermute | solution.py:29
  6.3 3.7 %collective-permute-start.1 = (bf16[192,1152]{1,0:T(8,128)(2,1)}, bf16[192,1152]{1,0:T(8,128)(2,1)S(1)}, u32[]{:S(2)}, u32[]{:S(2)}) collective-permute-start(bf16[192,1152]{1,0:T(8,128)(2,1)} %i0.1), channel_id=1, source_target_pairs={{0,2},{1,0},{2,1},{3,5},{4,3},{5,4},{6,8},{7,6},{8,7},{9,11},{10,9... | collective-permute-start | bytes 1327112 | tf_op jit(solution)/shard_map/ppermute | solution.py:29
  10.1 1.3 %collective-permute-start.2 = (bf16[192,1152]{1,0:T(8,128)(2,1)}, bf16[192,1152]{1,0:T(8,128)(2,1)S(1)}, u32[]{:S(2)}, u32[]{:S(2)}) collective-permute-start(bf16[192,1152]{1,0:T(8,128)(2,1)} %t0.3), channel_id=1, source_target_pairs={{0,3},{1,4},{2,5},{5,14},{6,9},{7,10},{8,11},{11,20},{12,15},{13,1... | collective-permute-start | bytes 1327112 | tf_op jit(solution)/shard_map/ppermute | solution.py:29
  11.4 3.2 %collective-permute-start.3 = (bf16[192,1152]{1,0:T(8,128)(2,1)}, bf16[192,1152]{1,0:T(8,128)(2,1)S(1)}, u32[]{:S(2)}, u32[]{:S(2)}) collective-permute-start(bf16[192,1152]{1,0:T(8,128)(2,1)} %t0.3), channel_id=1, source_target_pairs={{0,6},{1,7},{2,8},{3,9},{4,10},{5,11},{6,12},{7,13},{8,14},{9,15},... | collective-permute-start | bytes 1327112 | tf_op jit(solution)/shard_map/ppermute | solution.py:29
  14.6 1.3 %collective-permute-start.5 = (bf16[192,1152]{1,0:T(8,128)(2,1)S(1)}, bf16[192,1152]{1,0:T(8,128)(2,1)S(1)}, u32[]{:S(2)}, u32[]{:S(2)}) collective-permute-start(bf16[192,1152]{1,0:T(8,128)(2,1)S(1)} %collective-permute-done.4), channel_id=1, source_target_pairs={{0,48},{7,49},{14,50},{23,53},{28,52},{33,51},{48,96},{55,97},{62,... | collective-permute-start | bytes 1327112 | tf_op jit(solution)/shard_map/ppermute | solution.py:29
  16.0 3.3 %collective-permute-done.1.i2 = bf16[192,1152]{1,0:T(8,128)(2,1)S(1)} collective-permute-done((bf16[192,1152]{1,0:T(8,128)(2,1)}, bf16[192,1152]{1,0:T(8,128)(2,1)S(1)}, u32[]{:S(2)}, u32[]{:S(2)}) %collective-permute-start.1) | collective-permute-done | bytes 442400 | tf_op jit(solution)/shard_map/ppermute | solution.py:29
  19.3 2.9 %collective-permute-done.2.near = bf16[192,1152]{1,0:T(8,128)(2,1)S(1)} collective-permute-done((bf16[192,1152]{1,0:T(8,128)(2,1)}, bf16[192,1152]{1,0:T(8,128)(2,1)S(1)}, u32[]{:S(2)}, u32[]{:S(2)}) %collective-permute-start.2) | collective-permute-done | bytes 442400 | tf_op jit(solution)/shard_map/ppermute | solution.py:29
  22.1 27.4 %collective-permute-done.5 = bf16[192,1152]{1,0:T(8,128)(2,1)S(1)} collective-permute-done((bf16[192,1152]{1,0:T(8,128)(2,1)S(1)}, bf16[192,1152]{1,0:T(8,128)(2,1)S(1)}, u32[]{:S(2)}, u32[]{:S(2)}) %collective-permute-start.5) | collective-permute-done | bytes 442400 | tf_op jit(solution)/shard_map/ppermute | solution.py:29
  49.6 1.9 %collective-permute-start.6 = (bf16[192,1152]{1,0:T(8,128)(2,1)S(1)}, bf16[192,1152]{1,0:T(8,128)(2,1)}, u32[]{:S(2)}, u32[]{:S(2)}) collective-permute-start(bf16[192,1152]{1,0:T(8,128)(2,1)S(1)} %broadcast_select_fusion.t2), channel_id=1, source_target_pairs={{0,3},{1,4},{2,5},{3,0},{4,1},{5,2},{6,9},{7,10},{8,11},{9,6},{10,... | collective-permute-start | bytes 1327112 | tf_op jit(solution)/shard_map/ppermute | solution.py:29
  53.0 1.3 %shard_map.68 = (bf16[576,1152]{1,0:T(8,128)(2,1)S(1)}, bf16[192,576]{1,0:T(8,128)(2,1)S(1)}, f32[192,1152]{1,0:T(8,128)S(1)}) custom-call(s32[1]{0:T(128)} %bitcast.k_ref, f32[1]{0:T(128)S(6)} %copy.7.scale_ref, f32[1]{0:T(128)S(6)} %copy.8.shift_ref, s32[1,576]{1,0:T(1,128)S(1)} %broadcast_in_dim.8.wanted, bf16[192,1152]{1,0:T(8,128)(2,1)S(1)} %copy-done.3, ...), custom_call_target="tpu_custom_call" | custom-call | tf_op jit(solution)/shard_map/pallas_call | solution.py:139
  54.3 5.2 %shard_map.69 = (bf16[2,192,1152]{2,1,0:T(8,128)(2,1)}, f32[192,1152]{1,0:T(8,128)S(1)}, f32[192,1152]{1,0:T(8,128)S(1)}, bf16[192,1152]{1,0:T(8,128)(2,1)S(1)}, bf16[192,1152]{1,0:T(8,128)(2,1)S(1)}) custom-call(s32[1]{0:T(128)} %bitcast.k_ref, s32[1]{0:T(128)} %bitcast.1.core_ref, f32[1]{0:T(128)S(6)} %copy.7.scale_ref, f32[1]{0:T(128)S(6)} %copy.8.shift_ref, ...), custom_call_target="tpu_custom_call" | custom-call | tf_op jit(solution)/shard_map/pallas_call | solution.py:139
  59.4 0.9 copy-done.1
  61.1 0.8 copy-done.5
  61.9 2.4 %collective-permute-start.9 = (bf16[2,192,1152]{2,1,0:T(8,128)(2,1)}, bf16[2,192,1152]{2,1,0:T(8,128)(2,1)S(1)}, u32[]{:S(2)}, u32[]{:S(2)}) collective-permute-start(bf16[2,192,1152]{2,1,0:T(8,128)(2,1)} %get-tuple-element.26), channel_id=1, source_target_pairs={{0,3},{1,4},{2,5},{3,0},{4,1},{5,2},{6,9},{7,10},{8,11},{9,6},{10,... | collective-permute-start | bytes 2654216 | tf_op jit(solution)/shard_map/ppermute | solution.py:29
  64.3 1.9 %collective-permute-start.7 = (bf16[192,1152]{1,0:T(8,128)(2,1)}, bf16[192,1152]{1,0:T(8,128)(2,1)S(1)}, u32[]{:S(2)}, u32[]{:S(2)}) collective-permute-start(bf16[192,1152]{1,0:T(8,128)(2,1)} %copy-done.5), channel_id=1, source_target_pairs={{0,2},{1,0},{2,1},{3,5},{4,3},{5,4},{6,8},{7,6},{8,7},{9,11},{10,9... | collective-permute-start | bytes 1327112 | tf_op jit(solution)/shard_map/ppermute | solution.py:29
  66.2 3.4 %collective-permute-start.8 = (bf16[192,1152]{1,0:T(8,128)(2,1)}, bf16[192,1152]{1,0:T(8,128)(2,1)S(1)}, u32[]{:S(2)}, u32[]{:S(2)}) collective-permute-start(bf16[192,1152]{1,0:T(8,128)(2,1)} %copy-done.4), channel_id=1, source_target_pairs={{0,1},{1,2},{2,0},{3,4},{4,5},{5,3},{6,7},{7,8},{8,6},{9,10},{10,1... | collective-permute-start | bytes 1327112 | tf_op jit(solution)/shard_map/ppermute | solution.py:29
  69.7 1.4 %collective-permute-start.11 = (bf16[192,1152]{1,0:T(8,128)(2,1)S(1)}, bf16[192,1152]{1,0:T(8,128)(2,1)S(1)}, u32[]{:S(2)}, u32[]{:S(2)}) collective-permute-start(bf16[192,1152]{1,0:T(8,128)(2,1)S(1)} %fusion), channel_id=1, source_target_pairs={{0,42},{1,37},{2,32},{3,15},{4,22},{5,29},{48,90},{49,85},{50,80},... | collective-permute-start | bytes 1327112 | tf_op jit(solution)/shard_map/ppermute | solution.py:29
  71.2 1.1 %slice_bitcast_fusion = bf16[192,1152]{1,0:T(8,128)(2,1)S(1)} fusion(bf16[2,192,1152]{2,1,0:T(8,128)(2,1)} %get-tuple-element.26), kind=kLoop, calls=%fused_computation.8 | loop fusion | bytes 884736 | tf_op jit(solution)/shard_map/squeeze | solution.py:192
  72.9 1.3 %collective-permute-start.13 = (bf16[192,1152]{1,0:T(8,128)(2,1)S(1)}, bf16[192,1152]{1,0:T(8,128)(2,1)S(1)}, u32[]{:S(2)}, u32[]{:S(2)}) collective-permute-start(bf16[192,1152]{1,0:T(8,128)(2,1)S(1)} %fusion), channel_id=1, source_target_pairs={{6,0},{7,1},{8,2},{9,3},{10,4},{11,5},{12,6},{13,7},{14,8},{15,9},... | collective-permute-start | bytes 1327112 | tf_op jit(solution)/shard_map/ppermute | solution.py:29
  74.2 2.2 %collective-permute-done.11 = bf16[192,1152]{1,0:T(8,128)(2,1)S(1)} collective-permute-done((bf16[192,1152]{1,0:T(8,128)(2,1)S(1)}, bf16[192,1152]{1,0:T(8,128)(2,1)S(1)}, u32[]{:S(2)}, u32[]{:S(2)}) %collective-permute-start.11) | collective-permute-done | bytes 442400 | tf_op jit(solution)/shard_map/ppermute | solution.py:29
  77.1 15.0 %collective-permute-done.7 = bf16[192,1152]{1,0:T(8,128)(2,1)S(1)} collective-permute-done((bf16[192,1152]{1,0:T(8,128)(2,1)}, bf16[192,1152]{1,0:T(8,128)(2,1)S(1)}, u32[]{:S(2)}, u32[]{:S(2)}) %collective-permute-start.7) | collective-permute-done | bytes 442400 | tf_op jit(solution)/shard_map/ppermute | solution.py:29
  92.1 1.1 %add_add_fusion = f32[192,1152]{1,0:T(8,128)} fusion(f32[192,1152]{1,0:T(8,128)S(1)} %copy-done.2, bf16[192,1152]{1,0:T(8,128)(2,1)S(1)} %collective-permute-done.8, bf16[192,1152]{1,0:T(8,128)(2,1)S(1)} %collective-permute-done.7), kind=kLoop, calls=%fused_computation.5 | loop fusion | flops 884736 | bytes 2654208 | tf_op jit(solution)/shard_map/add | solution.py:199
  93.1 1.2 %fusion.2 = f32[192,1152]{1,0:T(8,128)} fusion(f32[192,1152]{1,0:T(8,128)S(1)} %get-tuple-element.25, bf16[192,1152]{1,0:T(8,128)(2,1)S(1)} %collective-permute-done.10, bf16[192,1152]{1,0:T(8,128)(2,1)S(1)} %collective-permute-done.12, bf16[192,1152]{1,0:T(8,128)(2,1)S(1)} %collective-permute-done.13, pred[]{:T(512)S(6)} %eq.20, pred[]{:T(512)S(6)} %eq.19, ...), kind=kLoop, calls=%fused_computation.4 | loop fusion | flops 1769472 | bytes 3538947 | tf_op jit(solution)/shard_map/add | solution.py:198
  (28 shorter events, 2.4 us)
Async XLA Ops:
  0.6 52.3 %copy-start = (bf16[192,1152]{1,0:T(8,128)(2,1)S(1)}, bf16[192,1152]{1,0:T(8,128)(2,1)}, u32[]{:S(2)}) copy-start(bf16[192,1152]{1,0:T(8,128)(2,1)} %t0.3) | copy-start | bytes 1327108
  0.6 52.3 %copy-start.3 = (bf16[192,1152]{1,0:T(8,128)(2,1)S(1)}, bf16[192,1152]{1,0:T(8,128)(2,1)}, u32[]{:S(2)}) copy-start(bf16[192,1152]{1,0:T(8,128)(2,1)} %i0.1) | copy-start | bytes 1327108
  0.6 51.0 %copy-start.6 = (s32[192]{0:T(256)S(1)}, s32[192]{0:T(256)}, u32[]{:S(2)}) copy-start(s32[192]{0:T(256)} %param.7) | copy-start | bytes 2308
  0.7 13.9 %collective-permute-start.4 = (bf16[192,1152]{1,0:T(8,128)(2,1)}, bf16[192,1152]{1,0:T(8,128)(2,1)S(1)}, u32[]{:S(2)}, u32[]{:S(2)}) collective-permute-start(bf16[192,1152]{1,0:T(8,128)(2,1)} %t0.3), channel_id=1, source_target_pairs={{42,0},{43,7},{44,14},{45,33},{46,28},{47,23},{90,48},{91,55},{92,... | collective-permute-start | bytes 1327112 | tf_op jit(solution)/shard_map/ppermute | solution.py:29
  1.5 14.5 %collective-permute-start = (bf16[192,1152]{1,0:T(8,128)(2,1)}, bf16[192,1152]{1,0:T(8,128)(2,1)S(1)}, u32[]{:S(2)}, u32[]{:S(2)}) collective-permute-start(bf16[192,1152]{1,0:T(8,128)(2,1)} %i0.1), channel_id=1, source_target_pairs={{0,1},{1,2},{2,0},{3,4},{4,5},{5,3},{6,7},{7,8},{8,6},{9,10},{10,1... | collective-permute-start | bytes 1327112 | tf_op jit(solution)/shard_map/ppermute | solution.py:29
  6.3 12.9 %collective-permute-start.1 = (bf16[192,1152]{1,0:T(8,128)(2,1)}, bf16[192,1152]{1,0:T(8,128)(2,1)S(1)}, u32[]{:S(2)}, u32[]{:S(2)}) collective-permute-start(bf16[192,1152]{1,0:T(8,128)(2,1)} %i0.1), channel_id=1, source_target_pairs={{0,2},{1,0},{2,1},{3,5},{4,3},{5,4},{6,8},{7,6},{8,7},{9,11},{10,9... | collective-permute-start | bytes 1327112 | tf_op jit(solution)/shard_map/ppermute | solution.py:29
  10.1 12.1 %collective-permute-start.2 = (bf16[192,1152]{1,0:T(8,128)(2,1)}, bf16[192,1152]{1,0:T(8,128)(2,1)S(1)}, u32[]{:S(2)}, u32[]{:S(2)}) collective-permute-start(bf16[192,1152]{1,0:T(8,128)(2,1)} %t0.3), channel_id=1, source_target_pairs={{0,3},{1,4},{2,5},{5,14},{6,9},{7,10},{8,11},{11,20},{12,15},{13,1... | collective-permute-start | bytes 1327112 | tf_op jit(solution)/shard_map/ppermute | solution.py:29
  11.4 10.8 %collective-permute-start.3 = (bf16[192,1152]{1,0:T(8,128)(2,1)}, bf16[192,1152]{1,0:T(8,128)(2,1)S(1)}, u32[]{:S(2)}, u32[]{:S(2)}) collective-permute-start(bf16[192,1152]{1,0:T(8,128)(2,1)} %t0.3), channel_id=1, source_target_pairs={{0,6},{1,7},{2,8},{3,9},{4,10},{5,11},{6,12},{7,13},{8,14},{9,15},... | collective-permute-start | bytes 1327112 | tf_op jit(solution)/shard_map/ppermute | solution.py:29
  14.6 35.0 %collective-permute-start.5 = (bf16[192,1152]{1,0:T(8,128)(2,1)S(1)}, bf16[192,1152]{1,0:T(8,128)(2,1)S(1)}, u32[]{:S(2)}, u32[]{:S(2)}) collective-permute-start(bf16[192,1152]{1,0:T(8,128)(2,1)S(1)} %collective-permute-done.4), channel_id=1, source_target_pairs={{0,48},{7,49},{14,50},{23,53},{28,52},{33,51},{48,96},{55,97},{62,... | collective-permute-start | bytes 1327112 | tf_op jit(solution)/shard_map/ppermute | solution.py:29
  49.6 4.6 %collective-permute-start.6 = (bf16[192,1152]{1,0:T(8,128)(2,1)S(1)}, bf16[192,1152]{1,0:T(8,128)(2,1)}, u32[]{:S(2)}, u32[]{:S(2)}) collective-permute-start(bf16[192,1152]{1,0:T(8,128)(2,1)S(1)} %broadcast_select_fusion.t2), channel_id=1, source_target_pairs={{0,3},{1,4},{2,5},{3,0},{4,1},{5,2},{6,9},{7,10},{8,11},{9,6},{10,... | collective-permute-start | bytes 1327112 | tf_op jit(solution)/shard_map/ppermute | solution.py:29
  59.4 0.9 copy-start.1
  60.3 0.8 copy-start.4
  61.1 0.8 copy-start.5
  61.9 7.7 %collective-permute-start.9 = (bf16[2,192,1152]{2,1,0:T(8,128)(2,1)}, bf16[2,192,1152]{2,1,0:T(8,128)(2,1)S(1)}, u32[]{:S(2)}, u32[]{:S(2)}) collective-permute-start(bf16[2,192,1152]{2,1,0:T(8,128)(2,1)} %get-tuple-element.26), channel_id=1, source_target_pairs={{0,3},{1,4},{2,5},{3,0},{4,1},{5,2},{6,9},{7,10},{8,11},{9,6},{10,... | collective-permute-start | bytes 2654216 | tf_op jit(solution)/shard_map/ppermute | solution.py:29
  64.3 27.8 %collective-permute-start.7 = (bf16[192,1152]{1,0:T(8,128)(2,1)}, bf16[192,1152]{1,0:T(8,128)(2,1)S(1)}, u32[]{:S(2)}, u32[]{:S(2)}) collective-permute-start(bf16[192,1152]{1,0:T(8,128)(2,1)} %copy-done.5), channel_id=1, source_target_pairs={{0,2},{1,0},{2,1},{3,5},{4,3},{5,4},{6,8},{7,6},{8,7},{9,11},{10,9... | collective-permute-start | bytes 1327112 | tf_op jit(solution)/shard_map/ppermute | solution.py:29
  66.2 25.9 %collective-permute-start.8 = (bf16[192,1152]{1,0:T(8,128)(2,1)}, bf16[192,1152]{1,0:T(8,128)(2,1)S(1)}, u32[]{:S(2)}, u32[]{:S(2)}) collective-permute-start(bf16[192,1152]{1,0:T(8,128)(2,1)} %copy-done.4), channel_id=1, source_target_pairs={{0,1},{1,2},{2,0},{3,4},{4,5},{5,3},{6,7},{7,8},{8,6},{9,10},{10,1... | collective-permute-start | bytes 1327112 | tf_op jit(solution)/shard_map/ppermute | solution.py:29
  69.6 22.5 %copy-start.2 = (f32[192,1152]{1,0:T(8,128)S(1)}, f32[192,1152]{1,0:T(8,128)}, u32[]{:S(2)}) copy-start(f32[192,1152]{1,0:T(8,128)} %copy-done.1) | copy-start | bytes 2654212
  69.7 6.7 %collective-permute-start.11 = (bf16[192,1152]{1,0:T(8,128)(2,1)S(1)}, bf16[192,1152]{1,0:T(8,128)(2,1)S(1)}, u32[]{:S(2)}, u32[]{:S(2)}) collective-permute-start(bf16[192,1152]{1,0:T(8,128)(2,1)S(1)} %fusion), channel_id=1, source_target_pairs={{0,42},{1,37},{2,32},{3,15},{4,22},{5,29},{48,90},{49,85},{50,80},... | collective-permute-start | bytes 1327112 | tf_op jit(solution)/shard_map/ppermute | solution.py:29
  72.3 20.9 %collective-permute-start.10 = (bf16[192,1152]{1,0:T(8,128)(2,1)S(1)}, bf16[192,1152]{1,0:T(8,128)(2,1)S(1)}, u32[]{:S(2)}, u32[]{:S(2)}) collective-permute-start(bf16[192,1152]{1,0:T(8,128)(2,1)S(1)} %slice_bitcast_fusion), channel_id=1, source_target_pairs={{2,761},{8,767},{14,5},{20,11},{26,17},{32,23},{38,29},{44,35},{50... | collective-permute-start | bytes 1327112 | tf_op jit(solution)/shard_map/ppermute | solution.py:29
  72.9 20.2 %collective-permute-start.13 = (bf16[192,1152]{1,0:T(8,128)(2,1)S(1)}, bf16[192,1152]{1,0:T(8,128)(2,1)S(1)}, u32[]{:S(2)}, u32[]{:S(2)}) collective-permute-start(bf16[192,1152]{1,0:T(8,128)(2,1)S(1)} %fusion), channel_id=1, source_target_pairs={{6,0},{7,1},{8,2},{9,3},{10,4},{11,5},{12,6},{13,7},{14,8},{15,9},... | collective-permute-start | bytes 1327112 | tf_op jit(solution)/shard_map/ppermute | solution.py:29
  76.4 16.7 %collective-permute-start.12 = (bf16[192,1152]{1,0:T(8,128)(2,1)S(1)}, bf16[192,1152]{1,0:T(8,128)(2,1)S(1)}, u32[]{:S(2)}, u32[]{:S(2)}) collective-permute-start(bf16[192,1152]{1,0:T(8,128)(2,1)S(1)} %collective-permute-done.11), channel_id=1, source_target_pairs={{15,765},{22,766},{29,767},{32,764},{37,763},{42,762},{63,45},{70,... | collective-permute-start | bytes 1327112 | tf_op jit(solution)/shard_map/ppermute | solution.py:29

commit v3 on v2

v3 whole, which is shorter than its diff:
```python
import jax
import jax.numpy as jnp
from jax import lax
from jax.experimental import pallas as pl
from jax.experimental.pallas import tpu as pltpu
from jax.sharding import PartitionSpec as P

AXES = ("dp", "mp")
ROWS = 192
D = 1152
LINE = 3
GROUP = 6
LAP = 8
LAPS = 4
NB = 768
LOW = jnp.bfloat16
F32 = jnp.float32


def lap_of(b):
    return (b // GROUP) % LAP


def core_of(b):
    return b // LINE % 2


def sent(value, target):
    pairs = [(b, target(b) % NB) for b in range(NB) if target(b) is not None]
    return lax.ppermute(value, AXES, pairs)


def line_turned(value, by):
    return sent(value, lambda b: b // LINE * LINE + (b + by) % LINE)


def cores_swapped(value):
    return sent(value, lambda b: b + LINE if core_of(b) == 0 else b - LINE)


def plane(b, by):
    step = b % LINE if core_of(b) == 0 else GROUP - 1 - b % LINE
    return step if by > 0 else LAP - 1 - step


def at(x, lap, y, place):
    return ((x % LAPS * LAPS + lap % LAPS) * LAP + y) * GROUP + place


def detour(value, by):
    start, last = (LAP - 1, LAPS - 1) if by > 0 else (0, 0)

    def target(b):
        x, lap = b // (GROUP * LAP * LAPS), b // (GROUP * LAP) % LAPS
        return at(x + (by if lap == last else 0), lap, plane(b, by), b % GROUP) if lap_of(b) == start else None

    return sent(value, target)


def after_detour(value, by):
    end = 0 if by > 0 else LAP - 1

    def target(b):
        x, lap = b // (GROUP * LAP * LAPS), b // (GROUP * LAP) % LAPS
        return at(x, lap + by, end, b % GROUP) if lap_of(b) == plane(b, by) else None

    return sent(value, target)


def straight(value, by):
    start = LAP - 1 if by > 0 else 0
    return sent(value, lambda b: None if lap_of(b) == start else b + by * GROUP)


def scores(texts, pictures):
    return lax.dot_general(texts, pictures, (((1,), (1,)), ((), ())), preferred_element_type=F32)


def matmul(a, b):
    return jnp.dot(a, b, preferred_element_type=F32)


def own_texts(k_ref, scale_ref, shift_ref, wanted, i0, i1, i2, t0, coef, gt0, pictures):
    scale, shift, k = scale_ref[0], shift_ref[0], k_ref[0]
    pictures[0:ROWS] = i0[...]
    pictures[ROWS : 2 * ROWS] = i1[...]
    pictures[2 * ROWS :] = i2[...]
    logits = scores(t0[...], pictures[...])
    row = lax.broadcasted_iota(jnp.int32, logits.shape, 0)
    column = lax.broadcasted_iota(jnp.int32, logits.shape, 1)
    sign = jnp.where(wanted[...] == row, -1.0, 1.0).astype(F32)
    value = scale * sign * jax.nn.sigmoid(sign * (scale * logits + shift))
    one = (column >= ROWS) & (column < 2 * ROWS)
    unused = (one & (k != 0)) | ((column >= 2 * ROWS) & (k == 2))
    coef[...] = jnp.where(unused, 0.0, value).astype(LOW)
    gt0[...] = matmul(coef[...], pictures[...])


def over_texts(coef, texts):
    return lax.dot_general(coef, texts, (((0,), (0,)), ((), ())), preferred_element_type=F32)


def over_texts(coef, texts):
    return lax.dot_general(coef, texts, (((0,), (0,)), ((), ())), preferred_element_type=F32)


def other_texts(
    k_ref, core_ref, scale_ref, shift_ref, t0, t2, far, i0, i1, i2, o1, o02, coef0, gt0p,
    ours, theirs, share, gt0, far_share, texts, coef, spare, others, pictures,
):
    scale, shift, k, core = scale_ref[0], shift_ref[0], k_ref[0], core_ref[0]

    def negatives(some_texts, some_pictures):
        return scale * jax.nn.sigmoid(scale * scores(some_texts, some_pictures) + shift)

    texts[0:ROWS] = t2[...]
    texts[ROWS:] = t0[...]
    coef[ROWS:] = coef0[...]
    pictures[0:ROWS] = i0[...]
    pictures[ROWS : 2 * ROWS] = i1[...]
    pictures[2 * ROWS :] = i2[...]
    others[0:ROWS] = o02[0]
    others[ROWS : 2 * ROWS] = o1[...]
    others[2 * ROWS :] = o02[1]

    @pl.when(core == 0)
    def _():
        spare[...] = t0[...]

    @pl.when(core != 0)
    def _():
        spare[...] = t2[...]

    value = negatives(t2[...], pictures[...])
    column = lax.broadcasted_iota(jnp.int32, value.shape, 1)
    unused = (column >= ROWS) & (column < 2 * ROWS) & (k == 0)
    coef[0:ROWS] = jnp.where(unused, 0.0, value).astype(LOW)
    full = negatives(spare[...], others[...]).astype(LOW)
    by_far_text = matmul(coef[0:ROWS], pictures[...])
    by_text = matmul(full, others[...])
    ours[...] = over_texts(coef[...], texts[...])
    by_image = over_texts(full, spare[...])
    theirs[0 : 2 * ROWS] = by_image[0 : 2 * ROWS].astype(LOW)

    @pl.when(k != 2)
    def _():
        theirs[2 * ROWS :] = by_image[2 * ROWS :].astype(LOW)

    def with_seventh(text):
        single = negatives(text[...], others[2 * ROWS :]).astype(LOW)
        theirs[2 * ROWS :] = (by_image[2 * ROWS :] + over_texts(single, text[...])).astype(LOW)
        return matmul(single, others[2 * ROWS :])

    @pl.when((core == 0) & (k != 2))
    def _():
        gt0[...] = gt0p[...] + by_text
        share[...] = by_far_text.astype(LOW)

    @pl.when((core == 0) & (k == 2))
    def _():
        gt0[...] = gt0p[...] + by_text
        share[...] = (by_far_text + with_seventh(t2)).astype(LOW)

    @pl.when(core != 0)
    def _():
        gt0[...] = gt0p[...]
        share[...] = (by_far_text + by_text).astype(LOW)

    @pl.when((core != 0) & (k == 2))
    def _():
        far_share[...] = with_seventh(far).astype(LOW)

    @pl.when((core == 0) | (k != 2))
    def _():
        far_share[...] = jnp.zeros((ROWS, D), LOW)


def both_cores(ours, received, gi0, gi1, gi2):
    gi0[...] = ours[0:ROWS] + received[0:ROWS].astype(F32)
    gi1[...] = (ours[ROWS : 2 * ROWS] + received[ROWS : 2 * ROWS].astype(F32)).astype(LOW)
    gi2[...] = (ours[2 * ROWS :] + received[2 * ROWS :].astype(F32)).astype(LOW)


def line_total(gu0, back1, back2, grad_text):
    grad_text[...] = gu0[...] + (back1[...].astype(F32) + back2[...].astype(F32))


def shift_total(late_ref, far_ref, gv0, main, relayed, far, grad_picture):
    returned = jnp.where(late_ref[0] != 0, relayed[...], main[...]).astype(F32)
    grad_picture[...] = gv0[...] + (returned + jnp.where(far_ref[0] != 0, far[...].astype(F32), 0.0))


def kernel_call(body, n_small, args, outs, scratch=(), flops=0):
    return pl.pallas_call(
        body,
        out_shape=[jax.ShapeDtypeStruct(shape, kind) for shape, kind in outs],
        in_specs=[pl.BlockSpec(memory_space=pltpu.SMEM)] * n_small
        + [pl.BlockSpec(memory_space=pltpu.VMEM)] * (len(args) - n_small),
        out_specs=[pl.BlockSpec(memory_space=pltpu.VMEM)] * len(outs),
        cost_estimate=pl.CostEstimate(flops=flops, bytes_accessed=0, transcendentals=0) if flops else None,
        scratch_shapes=[pltpu.VMEM(shape, LOW) for shape in scratch],
        compiler_params=pltpu.CompilerParams(vmem_limit_bytes=12 * 1024 * 1024),
    )(*args)


def on_device(
    picture_embedding_matrix,
    caption_embedding_matrix,
    positive_caption_indices,
    sharpness_multiplier,
    additive_shift_term,
):
    here = lax.axis_index(AXES)
    k = here % LINE
    core = core_of(here)
    y = lap_of(here)
    image0, text0 = picture_embedding_matrix, caption_embedding_matrix
    small = [k.astype(jnp.int32).reshape(1), sharpness_multiplier, additive_shift_term]
    wanted = jnp.concatenate([positive_caption_indices - here * ROWS, jnp.full((2 * ROWS,), -1, jnp.int32)])[None]
    block, three = (ROWS, D), LINE * ROWS

    corner = detour(text0, 1)
    main = straight(text0, 1)
    image1 = line_turned(image0, 1)
    image2 = line_turned(image0, 2)
    far = sent(text0, lambda b: b + 2 * GROUP if b % GROUP == 5 else None)
    relayed = after_detour(corner, 1)
    others = [cores_swapped(image1), cores_swapped(jnp.stack([image0, image2]))]
    raw = image1, image2
    image1, image2, main, far, relayed = lax.optimization_barrier((image1, image2, main, far, relayed))
    coef0, gt0 = kernel_call(
        own_texts,
        3,
        small + [wanted, image0, *raw, text0],
        [((ROWS, three), LOW), (block, F32)],
        [(three, D)],
    )
    text2 = jnp.where(y == 0, relayed, main)
    ours, theirs, share, gt0, far = kernel_call(
        other_texts,
        4,
        [small[0], core.astype(jnp.int32).reshape(1), *small[1:], text0, text2, far, image0, image1, image2, *others, coef0, gt0],
        [((three, D), F32), ((three, D), LOW), (block, LOW), (block, F32), (block, LOW)],
        [(2 * ROWS, D), (2 * ROWS, three), (ROWS, D), (three, D), (three, D)],
    )
    received = cores_swapped(theirs)
    back_corner = detour(share, -1)
    back_main = straight(share, -1)
    gi0, gi1, gi2 = kernel_call(
        both_cores, 0, [ours, received], [(block, F32), (block, LOW), (block, LOW)]
    )
    far_back = sent(far, lambda b: b - 2 * GROUP if b % GROUP == 5 else None)
    back1 = line_turned(gi1, -1)
    back2 = line_turned(gi2, -2)
    back_relayed = after_detour(back_corner, -1)
    [grad_image] = kernel_call(line_total, 0, [gi0, back1, back2], [(block, F32)], flops=20_000_000_000)
    grad_image, gt0 = lax.optimization_barrier((grad_image, gt0))
    flag = lambda value: value.astype(jnp.int32).reshape(1)
    [grad_text] = kernel_call(
        shift_total,
        2,
        [flag(y == LAP - 1), flag(here % GROUP == 5), gt0, back_main, back_relayed, far_back],
        [(block, F32)],
    )
    return grad_image, grad_text


def solution(mesh):
    in_specs = (P(AXES, None), P(AXES, None), P(AXES), P(), P())
    out_specs = (P(AXES, None), P(AXES, None))
    return jax.shard_map(
        on_device, mesh=mesh, in_specs=in_specs, out_specs=out_specs, check_vma=False
    )
```

time: 94.9 us -> 90 us (0.948)
  the two profiles are of different devices: /device:TPU:1 before, /device:TPU:254 now
where the time goes in v3:
time: 90 us; the launch traced here: 89.5 us
  waiting for transfers between devices  39.6 us (44%)
  starting transfers between devices  36.1 us (40%)
  Pallas kernels  8.07 us (9%)
  between operations  2.3 us (3%)
  other arithmetic  2.11 us (2%)
  local copies, waits for them, and re-layouts  1.34 us (1%)
    ppermute x15, waiting for transfers between devices, sent(): return lax.ppermute(value, AXES, pairs)  39.6 us
    ppermute x15, starting transfers between devices, sent(): return lax.ppermute(value, AXES, pairs)  36.1 us
    pallas_call x5, Pallas kernels, kernel_call(): pl.pallas_call(body, out_shape=[jax.ShapeDtypeStruct(shape, kind) for sha...  8.07 us
    another operation x1, other arithmetic, on_device(): others = [cores_swapped(image1), cores_swapped(jnp.stack([image0, image2]))]  2.01 us
  transfers between devices with their start and end apart: 15, of which 6 were waited for; matrix products, arithmetic and copies ran while one was open for 2% of the time, Pallas kernels for 3%

profile of v3, /device:TPU:254, one launch (start us, length us, event | category | flops | bytes accessed | tf_op | source)
XLA Modules:
  0.0 89.5 jit_solution(6198978915302356511)
XLA Ops:
  0.7 2.6 %collective-permute-start.4 = (bf16[192,1152]{1,0:T(8,128)(2,1)}, bf16[192,1152]{1,0:T(8,128)(2,1)}, u32[]{:S(2)}, u32[]{:S(2)}) collective-permute-start(bf16[192,1152]{1,0:T(8,128)(2,1)} %t0.3), channel_id=1, source_target_pairs={{42,0},{43,7},{44,14},{45,33},{46,28},{47,23},{90,48},{91,55},{92,... | collective-permute-start | bytes 1327112 | tf_op jit(solution)/shard_map/ppermute | solution.py:30
  3.2 9.3 %collective-permute-start.1 = (bf16[192,1152]{1,0:T(8,128)(2,1)}, bf16[192,1152]{1,0:T(8,128)(2,1)S(1)}, u32[]{:S(2)}, u32[]{:S(2)}) collective-permute-start(bf16[192,1152]{1,0:T(8,128)(2,1)} %i0.3), channel_id=1, source_target_pairs={{0,2},{1,0},{2,1},{3,5},{4,3},{5,4},{6,8},{7,6},{8,7},{9,11},{10,9... | collective-permute-start | bytes 1327112 | tf_op jit(solution)/shard_map/ppermute | solution.py:30
  12.6 1.9 %collective-permute-start = (bf16[192,1152]{1,0:T(8,128)(2,1)}, bf16[192,1152]{1,0:T(8,128)(2,1)S(1)}, u32[]{:S(2)}, u32[]{:S(2)}) collective-permute-start(bf16[192,1152]{1,0:T(8,128)(2,1)} %i0.3), channel_id=1, source_target_pairs={{0,1},{1,2},{2,0},{3,4},{4,5},{5,3},{6,7},{7,8},{8,6},{9,10},{10,1... | collective-permute-start | bytes 1327112 | tf_op jit(solution)/shard_map/ppermute | solution.py:30
  15.2 1.3 %collective-permute-start.2 = (bf16[192,1152]{1,0:T(8,128)(2,1)}, bf16[192,1152]{1,0:T(8,128)(2,1)S(1)}, u32[]{:S(2)}, u32[]{:S(2)}) collective-permute-start(bf16[192,1152]{1,0:T(8,128)(2,1)} %t0.3), channel_id=1, source_target_pairs={{0,6},{1,7},{2,8},{3,9},{4,10},{5,11},{6,12},{7,13},{8,14},{9,15},... | collective-permute-start | bytes 1327112 | tf_op jit(solution)/shard_map/ppermute | solution.py:30
  16.5 1.4 %collective-permute-start.5 = (bf16[192,1152]{1,0:T(8,128)(2,1)}, bf16[192,1152]{1,0:T(8,128)(2,1)}, u32[]{:S(2)}, u32[]{:S(2)}) collective-permute-start(bf16[192,1152]{1,0:T(8,128)(2,1)} %collective-permute-done.4), channel_id=1, source_target_pairs={{0,48},{7,49},{14,50},{23,53},{28,52},{33,51},{48,96},{55,97},{62,... | collective-permute-start | bytes 1327112 | tf_op jit(solution)/shard_map/ppermute | solution.py:30
  17.9 13.9 %collective-permute-done.1.i2 = bf16[192,1152]{1,0:T(8,128)(2,1)S(1)} collective-permute-done((bf16[192,1152]{1,0:T(8,128)(2,1)}, bf16[192,1152]{1,0:T(8,128)(2,1)S(1)}, u32[]{:S(2)}, u32[]{:S(2)}) %collective-permute-start.1) | collective-permute-done | bytes 442400 | tf_op jit(solution)/shard_map/ppermute | solution.py:30
  31.8 2.0 %pad_maximum_fusion = bf16[2,192,1152]{2,1,0:T(8,128)(2,1)} fusion(bf16[1,192,1152]{2,1,0:T(8,128)(2,1)S(1)} %bitcast.7, bf16[1,192,1152]{2,1,0:T(8,128)(2,1)} %bitcast.6), kind=kLoop, calls=%fused_computation | loop fusion | flops 442368 | bytes 1769472 | tf_op jit(solution)/shard_map/stack | solution.py:228
  33.8 1.9 %collective-permute-start.7 = (bf16[2,192,1152]{2,1,0:T(8,128)(2,1)}, bf16[2,192,1152]{2,1,0:T(8,128)(2,1)S(1)}, u32[]{:S(2)}, u32[]{:S(2)}) collective-permute-start(bf16[2,192,1152]{2,1,0:T(8,128)(2,1)} %pad_maximum_fusion), channel_id=1, source_target_pairs={{0,3},{1,4},{2,5},{3,0},{4,1},{5,2},{6,9},{7,10},{8,11},{9,6},{10,... | collective-permute-start | bytes 2654216 | tf_op jit(solution)/shard_map/ppermute | solution.py:30
  37.2 3.8 %collective-permute-done.i1 = bf16[192,1152]{1,0:T(8,128)(2,1)S(1)} collective-permute-done((bf16[192,1152]{1,0:T(8,128)(2,1)}, bf16[192,1152]{1,0:T(8,128)(2,1)S(1)}, u32[]{:S(2)}, u32[]{:S(2)}) %collective-permute-start) | collective-permute-done | bytes 442400 | tf_op jit(solution)/shard_map/ppermute | solution.py:30
  41.0 1.9 %collective-permute-start.6 = (bf16[192,1152]{1,0:T(8,128)(2,1)S(1)}, bf16[192,1152]{1,0:T(8,128)(2,1)S(1)}, u32[]{:S(2)}, u32[]{:S(2)}) collective-permute-start(bf16[192,1152]{1,0:T(8,128)(2,1)S(1)} %collective-permute-done.i1), channel_id=1, source_target_pairs={{0,3},{1,4},{2,5},{3,0},{4,1},{5,2},{6,9},{7,10},{8,11},{9,6},{10,... | collective-permute-start | bytes 1327112 | tf_op jit(solution)/shard_map/ppermute | solution.py:30
  42.9 1.3 %shard_map.68 = (bf16[192,576]{1,0:T(8,128)(2,1)S(1)}, f32[192,1152]{1,0:T(8,128)S(1)}) custom-call(s32[1]{0:T(128)} %bitcast.k_ref, f32[1]{0:T(128)S(6)} %copy.7.scale_ref, f32[1]{0:T(128)S(6)} %copy.8.shift_ref, s32[1,576]{1,0:T(1,128)S(1)} %broadcast_in_dim.4.wanted, bf16[192,1152]{1,0:T(8,128)(2,1)S(1)} %copy-done, ...), custom_call_target="tpu_custom_call" | custom-call | tf_op jit(solution)/shard_map/pallas_call | solution.py:194
  45.0 1.0 %copy-done.3 = bf16[192,1152]{1,0:T(8,128)(2,1)S(1)} copy-done((bf16[192,1152]{1,0:T(8,128)(2,1)S(1)}, bf16[192,1152]{1,0:T(8,128)(2,1)}, u32[]{:S(2)}) %copy-start.3) | copy-done | bytes 442392
  46.0 4.3 %shard_map.69 = (f32[576,1152]{1,0:T(8,128)S(1)}, bf16[576,1152]{1,0:T(8,128)(2,1)S(1)}, bf16[192,1152]{1,0:T(8,128)(2,1)}, f32[192,1152]{1,0:T(8,128)S(1)}, bf16[192,1152]{1,0:T(8,128)(2,1)S(1)}) custom-call(s32[1]{0:T(128)} %bitcast.k_ref, s32[1]{0:T(128)} %bitcast.1.core_ref, f32[1]{0:T(128)S(6)} %copy.7.scale_ref, f32[1]{0:T(128)S(6)} %copy.8.shift_ref, ...), custom_call_target="tpu_custom_call" | custom-call | tf_op jit(solution)/shard_map/pallas_call | solution.py:194
  50.3 2.4 %collective-permute-start.8 = (bf16[576,1152]{1,0:T(8,128)(2,1)S(1)}, bf16[576,1152]{1,0:T(8,128)(2,1)S(1)}, u32[]{:S(2)}, u32[]{:S(2)}) collective-permute-start(bf16[576,1152]{1,0:T(8,128)(2,1)S(1)} %get-tuple-element.27), channel_id=1, source_target_pairs={{0,3},{1,4},{2,5},{3,0},{4,1},{5,2},{6,9},{7,10},{8,11},{9,6},{10,... | collective-permute-start | bytes 3981320 | tf_op jit(solution)/shard_map/ppermute | solution.py:30
  52.7 1.3 %collective-permute-start.12 = (bf16[192,1152]{1,0:T(8,128)(2,1)}, bf16[192,1152]{1,0:T(8,128)(2,1)}, u32[]{:S(2)}, u32[]{:S(2)}) collective-permute-start(bf16[192,1152]{1,0:T(8,128)(2,1)} %get-tuple-element.34), channel_id=1, source_target_pairs={{0,618},{1,613},{2,608},{3,591},{4,598},{5,605},{48,90},{49,85},{5... | collective-permute-start | bytes 1327112 | tf_op jit(solution)/shard_map/ppermute | solution.py:30
  54.0 1.4 %collective-permute-done.8.received = bf16[576,1152]{1,0:T(8,128)(2,1)S(1)} collective-permute-done((bf16[576,1152]{1,0:T(8,128)(2,1)S(1)}, bf16[576,1152]{1,0:T(8,128)(2,1)S(1)}, u32[]{:S(2)}, u32[]{:S(2)}) %collective-permute-start.8) | collective-permute-done | bytes 1327136 | tf_op jit(solution)/shard_map/ppermute | solution.py:30
  55.7 3.9 %collective-permute-start.9 = (bf16[192,1152]{1,0:T(8,128)(2,1)S(1)}, bf16[192,1152]{1,0:T(8,128)(2,1)S(1)}, u32[]{:S(2)}, u32[]{:S(2)}) collective-permute-start(bf16[192,1152]{1,0:T(8,128)(2,1)S(1)} %get-tuple-element.29), channel_id=1, source_target_pairs={{0,2},{1,0},{2,1},{3,5},{4,3},{5,4},{6,8},{7,6},{8,7},{9,11},{10,9... | collective-permute-start | bytes 1327112 | tf_op jit(solution)/shard_map/ppermute | solution.py:30
  59.6 3.5 %collective-permute-start.10 = (bf16[192,1152]{1,0:T(8,128)(2,1)S(1)}, bf16[192,1152]{1,0:T(8,128)(2,1)S(1)}, u32[]{:S(2)}, u32[]{:S(2)}) collective-permute-start(bf16[192,1152]{1,0:T(8,128)(2,1)S(1)} %get-tuple-element.30), channel_id=1, source_target_pairs={{0,1},{1,2},{2,0},{3,4},{4,5},{5,3},{6,7},{7,8},{8,6},{9,10},{10,1... | collective-permute-start | bytes 1327112 | tf_op jit(solution)/shard_map/ppermute | solution.py:30
  63.2 1.3 %collective-permute-start.11 = (bf16[192,1152]{1,0:T(8,128)(2,1)}, bf16[192,1152]{1,0:T(8,128)(2,1)S(1)}, u32[]{:S(2)}, u32[]{:S(2)}) collective-permute-start(bf16[192,1152]{1,0:T(8,128)(2,1)} %get-tuple-element.34), channel_id=1, source_target_pairs={{6,0},{7,1},{8,2},{9,3},{10,4},{11,5},{12,6},{13,7},{14,8},{15,9},... | collective-permute-start | bytes 1327112 | tf_op jit(solution)/shard_map/ppermute | solution.py:30
  65.2 1.9 %collective-permute-start.13 = (bf16[192,1152]{1,0:T(8,128)(2,1)}, bf16[192,1152]{1,0:T(8,128)(2,1)S(1)}, u32[]{:S(2)}, u32[]{:S(2)}) collective-permute-start(bf16[192,1152]{1,0:T(8,128)(2,1)} %collective-permute-done.12), channel_id=1, source_target_pairs={{15,189},{22,190},{29,191},{32,188},{37,187},{42,186},{63,45},{70,... | collective-permute-start | bytes 1327112 | tf_op jit(solution)/shard_map/ppermute | solution.py:30
  67.1 4.8 %collective-permute-done.9.back1 = bf16[192,1152]{1,0:T(8,128)(2,1)S(1)} collective-permute-done((bf16[192,1152]{1,0:T(8,128)(2,1)S(1)}, bf16[192,1152]{1,0:T(8,128)(2,1)S(1)}, u32[]{:S(2)}, u32[]{:S(2)}) %collective-permute-start.9) | collective-permute-done | bytes 442400 | tf_op jit(solution)/shard_map/ppermute | solution.py:30
  71.9 15.4 %collective-permute-done.10.back2 = bf16[192,1152]{1,0:T(8,128)(2,1)S(1)} collective-permute-done((bf16[192,1152]{1,0:T(8,128)(2,1)S(1)}, bf16[192,1152]{1,0:T(8,128)(2,1)S(1)}, u32[]{:S(2)}, u32[]{:S(2)}) %collective-permute-start.10) | collective-permute-done | bytes 442400 | tf_op jit(solution)/shard_map/ppermute | solution.py:30
  87.3 1.0 %shard_map.71 = f32[192,1152]{1,0:T(8,128)} custom-call(f32[192,1152]{1,0:T(8,128)S(1)} %get-tuple-element.28.gu0, bf16[192,1152]{1,0:T(8,128)(2,1)S(1)} %collective-permute-done.9.back1, bf16[192,1152]{1,0:T(8,128)(2,1)S(1)} %collective-permute-done.10.back2), custom_call_target="tpu_custom_call" | custom-call | flops 20000000000 | tf_op jit(solution)/shard_map/pallas_call | solution.py:194
  88.3 1.1 %shard_map.72 = f32[192,1152]{1,0:T(8,128)} custom-call(s32[1]{0:T(128)} %bitcast.4.late_ref, s32[1]{0:T(128)} %bitcast.5.far_ref, f32[192,1152]{1,0:T(8,128)S(1)} %get-tuple-element.33.gv0, bf16[192,1152]{1,0:T(8,128)(2,1)S(1)} %collective-permute-done.11.main, bf16[192,1152]{1,0:T(8,128)(2,1)S(1)} %collective-permute-done.13.relayed, ...), custom_call_target="tpu_custom_call" | custom-call | tf_op jit(solution)/shard_map/pallas_call | solution.py:194
  (28 shorter events, 2.5 us)
Async XLA Ops:
  0.6 42.3 %copy-start.1 = (bf16[192,1152]{1,0:T(8,128)(2,1)S(1)}, bf16[192,1152]{1,0:T(8,128)(2,1)}, u32[]{:S(2)}) copy-start(bf16[192,1152]{1,0:T(8,128)(2,1)} %t0.3) | copy-start | bytes 1327108
  0.6 42.3 %copy-start = (bf16[192,1152]{1,0:T(8,128)(2,1)S(1)}, bf16[192,1152]{1,0:T(8,128)(2,1)}, u32[]{:S(2)}) copy-start(bf16[192,1152]{1,0:T(8,128)(2,1)} %i0.3) | copy-start | bytes 1327108
  0.6 36.5 %copy-start.5 = (s32[192]{0:T(256)S(1)}, s32[192]{0:T(256)}, u32[]{:S(2)}) copy-start(s32[192]{0:T(256)} %param.7) | copy-start | bytes 2308
  0.7 15.8 %collective-permute-start.4 = (bf16[192,1152]{1,0:T(8,128)(2,1)}, bf16[192,1152]{1,0:T(8,128)(2,1)}, u32[]{:S(2)}, u32[]{:S(2)}) collective-permute-start(bf16[192,1152]{1,0:T(8,128)(2,1)} %t0.3), channel_id=1, source_target_pairs={{42,0},{43,7},{44,14},{45,33},{46,28},{47,23},{90,48},{91,55},{92,... | collective-permute-start | bytes 1327112 | tf_op jit(solution)/shard_map/ppermute | solution.py:30
  3.2 28.6 %collective-permute-start.1 = (bf16[192,1152]{1,0:T(8,128)(2,1)}, bf16[192,1152]{1,0:T(8,128)(2,1)S(1)}, u32[]{:S(2)}, u32[]{:S(2)}) collective-permute-start(bf16[192,1152]{1,0:T(8,128)(2,1)} %i0.3), channel_id=1, source_target_pairs={{0,2},{1,0},{2,1},{3,5},{4,3},{5,4},{6,8},{7,6},{8,7},{9,11},{10,9... | collective-permute-start | bytes 1327112 | tf_op jit(solution)/shard_map/ppermute | solution.py:30
  12.6 28.4 %collective-permute-start = (bf16[192,1152]{1,0:T(8,128)(2,1)}, bf16[192,1152]{1,0:T(8,128)(2,1)S(1)}, u32[]{:S(2)}, u32[]{:S(2)}) collective-permute-start(bf16[192,1152]{1,0:T(8,128)(2,1)} %i0.3), channel_id=1, source_target_pairs={{0,1},{1,2},{2,0},{3,4},{4,5},{5,3},{6,7},{7,8},{8,6},{9,10},{10,1... | collective-permute-start | bytes 1327112 | tf_op jit(solution)/shard_map/ppermute | solution.py:30
  14.5 29.7 %collective-permute-start.3 = (bf16[192,1152]{1,0:T(8,128)(2,1)}, bf16[192,1152]{1,0:T(8,128)(2,1)S(1)}, u32[]{:S(2)}, u32[]{:S(2)}) collective-permute-start(bf16[192,1152]{1,0:T(8,128)(2,1)} %t0.3), channel_id=1, source_target_pairs={{5,17},{11,23},{17,29},{23,35},{29,41},{35,47},{41,53},{47,59},{53... | collective-permute-start | bytes 1327112 | tf_op jit(solution)/shard_map/ppermute | solution.py:30
  15.2 29.0 %collective-permute-start.2 = (bf16[192,1152]{1,0:T(8,128)(2,1)}, bf16[192,1152]{1,0:T(8,128)(2,1)S(1)}, u32[]{:S(2)}, u32[]{:S(2)}) collective-permute-start(bf16[192,1152]{1,0:T(8,128)(2,1)} %t0.3), channel_id=1, source_target_pairs={{0,6},{1,7},{2,8},{3,9},{4,10},{5,11},{6,12},{7,13},{8,14},{9,15},... | collective-permute-start | bytes 1327112 | tf_op jit(solution)/shard_map/ppermute | solution.py:30
  16.5 27.7 %collective-permute-start.5 = (bf16[192,1152]{1,0:T(8,128)(2,1)}, bf16[192,1152]{1,0:T(8,128)(2,1)}, u32[]{:S(2)}, u32[]{:S(2)}) collective-permute-start(bf16[192,1152]{1,0:T(8,128)(2,1)} %collective-permute-done.4), channel_id=1, source_target_pairs={{0,48},{7,49},{14,50},{23,53},{28,52},{33,51},{48,96},{55,97},{62,... | collective-permute-start | bytes 1327112 | tf_op jit(solution)/shard_map/ppermute | solution.py:30
  33.8 10.8 %collective-permute-start.7 = (bf16[2,192,1152]{2,1,0:T(8,128)(2,1)}, bf16[2,192,1152]{2,1,0:T(8,128)(2,1)S(1)}, u32[]{:S(2)}, u32[]{:S(2)}) collective-permute-start(bf16[2,192,1152]{2,1,0:T(8,128)(2,1)} %pad_maximum_fusion), channel_id=1, source_target_pairs={{0,3},{1,4},{2,5},{3,0},{4,1},{5,2},{6,9},{7,10},{8,11},{9,6},{10,... | collective-permute-start | bytes 2654216 | tf_op jit(solution)/shard_map/ppermute | solution.py:30
  41.0 3.7 %collective-permute-start.6 = (bf16[192,1152]{1,0:T(8,128)(2,1)S(1)}, bf16[192,1152]{1,0:T(8,128)(2,1)S(1)}, u32[]{:S(2)}, u32[]{:S(2)}) collective-permute-start(bf16[192,1152]{1,0:T(8,128)(2,1)S(1)} %collective-permute-done.i1), channel_id=1, source_target_pairs={{0,3},{1,4},{2,5},{3,0},{4,1},{5,2},{6,9},{7,10},{8,11},{9,6},{10,... | collective-permute-start | bytes 1327112 | tf_op jit(solution)/shard_map/ppermute | solution.py:30
  44.2 0.8 copy-start.2
  45.0 1.0 %copy-start.3 = (bf16[192,1152]{1,0:T(8,128)(2,1)S(1)}, bf16[192,1152]{1,0:T(8,128)(2,1)}, u32[]{:S(2)}) copy-start(bf16[192,1152]{1,0:T(8,128)(2,1)} %copy-done.2) | copy-start | bytes 1327108
  50.3 5.4 %copy-start.4 = (bf16[192,1152]{1,0:T(8,128)(2,1)}, bf16[192,1152]{1,0:T(8,128)(2,1)S(1)}, u32[]{:S(2)}) copy-start(bf16[192,1152]{1,0:T(8,128)(2,1)S(1)} %get-tuple-element.35) | copy-start | bytes 1327108
  50.3 5.1 %collective-permute-start.8 = (bf16[576,1152]{1,0:T(8,128)(2,1)S(1)}, bf16[576,1152]{1,0:T(8,128)(2,1)S(1)}, u32[]{:S(2)}, u32[]{:S(2)}) collective-permute-start(bf16[576,1152]{1,0:T(8,128)(2,1)S(1)} %get-tuple-element.27), channel_id=1, source_target_pairs={{0,3},{1,4},{2,5},{3,0},{4,1},{5,2},{6,9},{7,10},{8,11},{9,6},{10,... | collective-permute-start | bytes 3981320 | tf_op jit(solution)/shard_map/ppermute | solution.py:30
  52.7 12.5 %collective-permute-start.12 = (bf16[192,1152]{1,0:T(8,128)(2,1)}, bf16[192,1152]{1,0:T(8,128)(2,1)}, u32[]{:S(2)}, u32[]{:S(2)}) collective-permute-start(bf16[192,1152]{1,0:T(8,128)(2,1)} %get-tuple-element.34), channel_id=1, source_target_pairs={{0,618},{1,613},{2,608},{3,591},{4,598},{5,605},{48,90},{49,85},{5... | collective-permute-start | bytes 1327112 | tf_op jit(solution)/shard_map/ppermute | solution.py:30
  55.7 16.2 %collective-permute-start.9 = (bf16[192,1152]{1,0:T(8,128)(2,1)S(1)}, bf16[192,1152]{1,0:T(8,128)(2,1)S(1)}, u32[]{:S(2)}, u32[]{:S(2)}) collective-permute-start(bf16[192,1152]{1,0:T(8,128)(2,1)S(1)} %get-tuple-element.29), channel_id=1, source_target_pairs={{0,2},{1,0},{2,1},{3,5},{4,3},{5,4},{6,8},{7,6},{8,7},{9,11},{10,9... | collective-permute-start | bytes 1327112 | tf_op jit(solution)/shard_map/ppermute | solution.py:30
  59.6 27.7 %collective-permute-start.10 = (bf16[192,1152]{1,0:T(8,128)(2,1)S(1)}, bf16[192,1152]{1,0:T(8,128)(2,1)S(1)}, u32[]{:S(2)}, u32[]{:S(2)}) collective-permute-start(bf16[192,1152]{1,0:T(8,128)(2,1)S(1)} %get-tuple-element.30), channel_id=1, source_target_pairs={{0,1},{1,2},{2,0},{3,4},{4,5},{5,3},{6,7},{7,8},{8,6},{9,10},{10,1... | collective-permute-start | bytes 1327112 | tf_op jit(solution)/shard_map/ppermute | solution.py:30
  63.2 25.2 %collective-permute-start.11 = (bf16[192,1152]{1,0:T(8,128)(2,1)}, bf16[192,1152]{1,0:T(8,128)(2,1)S(1)}, u32[]{:S(2)}, u32[]{:S(2)}) collective-permute-start(bf16[192,1152]{1,0:T(8,128)(2,1)} %get-tuple-element.34), channel_id=1, source_target_pairs={{6,0},{7,1},{8,2},{9,3},{10,4},{11,5},{12,6},{13,7},{14,8},{15,9},... | collective-permute-start | bytes 1327112 | tf_op jit(solution)/shard_map/ppermute | solution.py:30
  64.5 23.8 %collective-permute-start.14 = (bf16[192,1152]{1,0:T(8,128)(2,1)}, bf16[192,1152]{1,0:T(8,128)(2,1)S(1)}, u32[]{:S(2)}, u32[]{:S(2)}) collective-permute-start(bf16[192,1152]{1,0:T(8,128)(2,1)} %copy-done.4), channel_id=1, source_target_pairs={{5,761},{11,767},{17,5},{23,11},{29,17},{35,23},{41,29},{47,35},{5... | collective-permute-start | bytes 1327112 | tf_op jit(solution)/shard_map/ppermute | solution.py:30
  65.2 23.1 %collective-permute-start.13 = (bf16[192,1152]{1,0:T(8,128)(2,1)}, bf16[192,1152]{1,0:T(8,128)(2,1)S(1)}, u32[]{:S(2)}, u32[]{:S(2)}) collective-permute-start(bf16[192,1152]{1,0:T(8,128)(2,1)} %collective-permute-done.12), channel_id=1, source_target_pairs={{15,189},{22,190},{29,191},{32,188},{37,187},{42,186},{63,45},{70,... | collective-permute-start | bytes 1327112 | tf_op jit(solution)/shard_map/ppermute | solution.py:30

commit v4 on v3

--- a/solution.py
+++ b/solution.py
@@ -104,75 +104,86 @@
     return lax.dot_general(coef, texts, (((0,), (0,)), ((), ())), preferred_element_type=F32)
 
 
-def other_texts(
-    k_ref, core_ref, scale_ref, shift_ref, t0, t2, far, i0, i1, i2, o1, o02, coef0, gt0p,
-    ours, theirs, share, gt0, far_share, texts, coef, spare, others, pictures,
+def negatives(texts, pictures, scale_ref, shift_ref):
+    scale, shift = scale_ref[0], shift_ref[0]
+    return scale * jax.nn.sigmoid(scale * scores(texts, pictures) + shift)
+
+
+def other_line(
+    k_ref, core_ref, scale_ref, shift_ref, t0, t2, far, o1, o02,
+    theirs, own_part, share_part, far_share, spare, others,
 ):
-    scale, shift, k, core = scale_ref[0], shift_ref[0], k_ref[0], core_ref[0]
-
-    def negatives(some_texts, some_pictures):
-        return scale * jax.nn.sigmoid(scale * scores(some_texts, some_pictures) + shift)
-
+    k, core = k_ref[0], core_ref[0]
+    others[0:ROWS] = o02[0]
+    others[ROWS : 2 * ROWS] = o1[...]
+    others[2 * ROWS :] = o02[1]
+
+    @pl.when(core == 0)
+    def _():
+        spare[...] = t0[...]
+
+    @pl.when(core != 0)
+    def _():
+        spare[...] = t2[...]
+
+    full = negatives(spare[...], others[...], scale_ref, shift_ref).astype(LOW)
+    by_image = over_texts(full, spare[...])
+    theirs[0 : 2 * ROWS] = by_image[0 : 2 * ROWS].astype(LOW)
+    by_text = matmul(full, others[...])
+
+    @pl.when(k != 2)
+    def _():
+        theirs[2 * ROWS :] = by_image[2 * ROWS :].astype(LOW)
+
+    def with_seventh(text):
+        single = negatives(text[...], others[2 * ROWS :], scale_ref, shift_ref).astype(LOW)
+        theirs[2 * ROWS :] = (by_image[2 * ROWS :] + over_texts(single, text[...])).astype(LOW)
+        return matmul(single, others[2 * ROWS :])
+
+    @pl.when(core == 0)
+    def _():
+        own_part[...] = by_text
+
+    @pl.when(core != 0)
+    def _():
+        own_part[...] = jnp.zeros((ROWS, D), F32)
+        share_part[...] = by_text
+
+    @pl.when((core == 0) & (k != 2))
+    def _():
+        share_part[...] = jnp.zeros((ROWS, D), F32)
+
+    @pl.when((core == 0) & (k == 2))
+    def _():
+        share_part[...] = with_seventh(t2)
+
+    @pl.when((core != 0) & (k == 2))
+    def _():
+        far_share[...] = with_seventh(far).astype(LOW)
+
+    @pl.when((core == 0) | (k != 2))
+    def _():
+        far_share[...] = jnp.zeros((ROWS, D), LOW)
+
+
+def own_line(
+    k_ref, scale_ref, shift_ref, t0, t2, i0, i1, i2, coef0, gt0p, own_part, share_part,
+    ours, share, gt0, texts, coef, pictures,
+):
+    k = k_ref[0]
     texts[0:ROWS] = t2[...]
     texts[ROWS:] = t0[...]
     coef[ROWS:] = coef0[...]
     pictures[0:ROWS] = i0[...]
     pictures[ROWS : 2 * ROWS] = i1[...]
     pictures[2 * ROWS :] = i2[...]
-    others[0:ROWS] = o02[0]
-    others[ROWS : 2 * ROWS] = o1[...]
-    others[2 * ROWS :] = o02[1]
-
-    @pl.when(core == 0)
-    def _():
-        spare[...] = t0[...]
-
-    @pl.when(core != 0)
-    def _():
-        spare[...] = t2[...]
-
-    value = negatives(t2[...], pictures[...])
+    value = negatives(t2[...], pictures[...], scale_ref, shift_ref)
     column = lax.broadcasted_iota(jnp.int32, value.shape, 1)
     unused = (column >= ROWS) & (column < 2 * ROWS) & (k == 0)
     coef[0:ROWS] = jnp.where(unused, 0.0, value).astype(LOW)
-    full = negatives(spare[...], others[...]).astype(LOW)
-    by_far_text = matmul(coef[0:ROWS], pictures[...])
-    by_text = matmul(full, others[...])
+    share[...] = (share_part[...] + matmul(coef[0:ROWS], pictures[...])).astype(LOW)
     ours[...] = over_texts(coef[...], texts[...])
-    by_image = over_texts(full, spare[...])
-    theirs[0 : 2 * ROWS] = by_image[0 : 2 * ROWS].astype(LOW)
-
-    @pl.when(k != 2)
-    def _():
-        theirs[2 * ROWS :] = by_image[2 * ROWS :].astype(LOW)
-
-    def with_seventh(text):
-        single = negatives(text[...], others[2 * ROWS :]).astype(LOW)
-        theirs[2 * ROWS :] = (by_image[2 * ROWS :] + over_texts(single, text[...])).astype(LOW)
-        return matmul(single, others[2 * ROWS :])
-
-    @pl.when((core == 0) & (k != 2))
-    def _():
-        gt0[...] = gt0p[...] + by_text
-        share[...] = by_far_text.astype(LOW)
-
-    @pl.when((core == 0) & (k == 2))
-    def _():
-        gt0[...] = gt0p[...] + by_text
-        share[...] = (by_far_text + with_seventh(t2)).astype(LOW)
-
-    @pl.when(core != 0)
-    def _():
-        gt0[...] = gt0p[...]
-        share[...] = (by_far_text + by_text).astype(LOW)
-
-    @pl.when((core != 0) & (k == 2))
-    def _():
-        far_share[...] = with_seventh(far).astype(LOW)
-
-    @pl.when((core == 0) | (k != 2))
-    def _():
-        far_share[...] = jnp.zeros((ROWS, D), LOW)
+    gt0[...] = gt0p[...] + own_part[...]
 
 
 def both_cores(ours, received, gi0, gi1, gi2):
@@ -236,12 +247,20 @@
         [(three, D)],
     )
     text2 = jnp.where(y == 0, relayed, main)
-    ours, theirs, share, gt0, far = kernel_call(
-        other_texts,
+    coef0, far = lax.optimization_barrier((coef0, far))
+    theirs, own_part, share_part, far = kernel_call(
+        other_line,
         4,
-        [small[0], core.astype(jnp.int32).reshape(1), *small[1:], text0, text2, far, image0, image1, image2, *others, coef0, gt0],
-        [((three, D), F32), ((three, D), LOW), (block, LOW), (block, F32), (block, LOW)],
-        [(2 * ROWS, D), (2 * ROWS, three), (ROWS, D), (three, D), (three, D)],
+        [small[0], core.astype(jnp.int32).reshape(1), *small[1:], text0, text2, far, *others],
+        [((three, D), LOW), (block, F32), (block, F32), (block, LOW)],
+        [(ROWS, D), (three, D)],
+    )
+    ours, share, gt0 = kernel_call(
+        own_line,
+        3,
+        [*small, text0, text2, image0, image1, image2, coef0, gt0, own_part, share_part],
+        [((three, D), F32), (block, LOW), (block, F32)],
+        [(2 * ROWS, D), (2 * ROWS, three), (three, D)],
     )
     received = cores_swapped(theirs)
     back_corner = detour(share, -1)

time: 90 us -> 88.7 us (0.986)
  local copies, waits for them, and re-layouts: 1.34 us -> 0.02 us
  Pallas kernels: 8.07 us -> 9.33 us
  waiting for transfers between devices: 39.6 us -> 38.5 us
    unnamed x12 -> x6, local copies, waits for them, and re-layouts: 1.33 us -> 0.01 us
    pallas_call x5 -> x6, Pallas kernels: 8.07 us -> 9.33 us  [kernel_call(): pl.pallas_call(body, out_shape=[jax.ShapeDtypeStruct(shape, kind) for sha...]
    ppermute x15, waiting for transfers between devices: 39.6 us -> 38.5 us  [sent(): return lax.ppermute(value, AXES, pairs)]
  transfers between devices with their start and end apart: 15 -> 15, of which waited for: 6 -> 5; matrix products, arithmetic and copies ran while one was open for 2% -> 2% of each run, Pallas kernels for 3% -> 7%
where the time goes in v4:
time: 88.7 us; the launch traced here: 88.2 us
  waiting for transfers between devices  38.5 us (43%)
  starting transfers between devices  35.9 us (40%)
  Pallas kernels  9.33 us (11%)
  between operations  2.3 us (3%)
  other arithmetic  2.11 us (2%)
    ppermute x15, waiting for transfers between devices, sent(): return lax.ppermute(value, AXES, pairs)  38.5 us
    ppermute x15, starting transfers between devices, sent(): return lax.ppermute(value, AXES, pairs)  35.9 us
    pallas_call x6, Pallas kernels, kernel_call(): pl.pallas_call(body, out_shape=[jax.ShapeDtypeStruct(shape, kind) for sha...  9.33 us
    another operation x1, other arithmetic, on_device(): others = [cores_swapped(image1), cores_swapped(jnp.stack([image0, image2]))]  2.01 us
  transfers between devices with their start and end apart: 15, of which 5 were waited for; matrix products, arithmetic and copies ran while one was open for 2% of the time, Pallas kernels for 7%

profile of v4, /device:TPU:254, one launch (start us, length us, event | category | flops | bytes accessed | tf_op | source)
XLA Modules:
  0.0 88.2 jit_solution(7608424123637248990)
XLA Ops:
  0.7 2.6 %collective-permute-start.4 = (bf16[192,1152]{1,0:T(8,128)(2,1)}, bf16[192,1152]{1,0:T(8,128)(2,1)}, u32[]{:S(2)}, u32[]{:S(2)}) collective-permute-start(bf16[192,1152]{1,0:T(8,128)(2,1)} %t0.5), channel_id=1, source_target_pairs={{42,0},{43,7},{44,14},{45,33},{46,28},{47,23},{90,48},{91,55},{92,... | collective-permute-start | bytes 1327112 | tf_op jit(solution)/shard_map/ppermute | solution.py:30
  3.2 9.3 %collective-permute-start.1 = (bf16[192,1152]{1,0:T(8,128)(2,1)}, bf16[192,1152]{1,0:T(8,128)(2,1)S(1)}, u32[]{:S(2)}, u32[]{:S(2)}) collective-permute-start(bf16[192,1152]{1,0:T(8,128)(2,1)} %i0.3), channel_id=1, source_target_pairs={{0,2},{1,0},{2,1},{3,5},{4,3},{5,4},{6,8},{7,6},{8,7},{9,11},{10,9... | collective-permute-start | bytes 1327112 | tf_op jit(solution)/shard_map/ppermute | solution.py:30
  12.6 1.9 %collective-permute-start = (bf16[192,1152]{1,0:T(8,128)(2,1)}, bf16[192,1152]{1,0:T(8,128)(2,1)S(1)}, u32[]{:S(2)}, u32[]{:S(2)}) collective-permute-start(bf16[192,1152]{1,0:T(8,128)(2,1)} %i0.3), channel_id=1, source_target_pairs={{0,1},{1,2},{2,0},{3,4},{4,5},{5,3},{6,7},{7,8},{8,6},{9,10},{10,1... | collective-permute-start | bytes 1327112 | tf_op jit(solution)/shard_map/ppermute | solution.py:30
  15.2 1.3 %collective-permute-start.2 = (bf16[192,1152]{1,0:T(8,128)(2,1)}, bf16[192,1152]{1,0:T(8,128)(2,1)S(1)}, u32[]{:S(2)}, u32[]{:S(2)}) collective-permute-start(bf16[192,1152]{1,0:T(8,128)(2,1)} %t0.5), channel_id=1, source_target_pairs={{0,6},{1,7},{2,8},{3,9},{4,10},{5,11},{6,12},{7,13},{8,14},{9,15},... | collective-permute-start | bytes 1327112 | tf_op jit(solution)/shard_map/ppermute | solution.py:30
  16.5 1.4 %collective-permute-start.5 = (bf16[192,1152]{1,0:T(8,128)(2,1)}, bf16[192,1152]{1,0:T(8,128)(2,1)}, u32[]{:S(2)}, u32[]{:S(2)}) collective-permute-start(bf16[192,1152]{1,0:T(8,128)(2,1)} %collective-permute-done.4), channel_id=1, source_target_pairs={{0,48},{7,49},{14,50},{23,53},{28,52},{33,51},{48,96},{55,97},{62,... | collective-permute-start | bytes 1327112 | tf_op jit(solution)/shard_map/ppermute | solution.py:30
  17.9 13.9 %collective-permute-done.1.i2 = bf16[192,1152]{1,0:T(8,128)(2,1)S(1)} collective-permute-done((bf16[192,1152]{1,0:T(8,128)(2,1)}, bf16[192,1152]{1,0:T(8,128)(2,1)S(1)}, u32[]{:S(2)}, u32[]{:S(2)}) %collective-permute-start.1) | collective-permute-done | bytes 442400 | tf_op jit(solution)/shard_map/ppermute | solution.py:30
  31.8 2.0 %pad_maximum_fusion = bf16[2,192,1152]{2,1,0:T(8,128)(2,1)} fusion(bf16[1,192,1152]{2,1,0:T(8,128)(2,1)S(1)} %bitcast.7, bf16[1,192,1152]{2,1,0:T(8,128)(2,1)} %bitcast.6), kind=kLoop, calls=%fused_computation | loop fusion | flops 442368 | bytes 1769472 | tf_op jit(solution)/shard_map/stack | solution.py:239
  33.8 1.9 %collective-permute-start.7 = (bf16[2,192,1152]{2,1,0:T(8,128)(2,1)}, bf16[2,192,1152]{2,1,0:T(8,128)(2,1)S(1)}, u32[]{:S(2)}, u32[]{:S(2)}) collective-permute-start(bf16[2,192,1152]{2,1,0:T(8,128)(2,1)} %pad_maximum_fusion), channel_id=1, source_target_pairs={{0,3},{1,4},{2,5},{3,0},{4,1},{5,2},{6,9},{7,10},{8,11},{9,6},{10,... | collective-permute-start | bytes 2654216 | tf_op jit(solution)/shard_map/ppermute | solution.py:30
  37.2 3.8 %collective-permute-done.i1 = bf16[192,1152]{1,0:T(8,128)(2,1)S(1)} collective-permute-done((bf16[192,1152]{1,0:T(8,128)(2,1)}, bf16[192,1152]{1,0:T(8,128)(2,1)S(1)}, u32[]{:S(2)}, u32[]{:S(2)}) %collective-permute-start) | collective-permute-done | bytes 442400 | tf_op jit(solution)/shard_map/ppermute | solution.py:30
  41.0 1.9 %collective-permute-start.6 = (bf16[192,1152]{1,0:T(8,128)(2,1)S(1)}, bf16[192,1152]{1,0:T(8,128)(2,1)S(1)}, u32[]{:S(2)}, u32[]{:S(2)}) collective-permute-start(bf16[192,1152]{1,0:T(8,128)(2,1)S(1)} %collective-permute-done.i1), channel_id=1, source_target_pairs={{0,3},{1,4},{2,5},{3,0},{4,1},{5,2},{6,9},{7,10},{8,11},{9,6},{10,... | collective-permute-start | bytes 1327112 | tf_op jit(solution)/shard_map/ppermute | solution.py:30
  42.9 1.3 %shard_map.68 = (bf16[192,576]{1,0:T(8,128)(2,1)S(1)}, f32[192,1152]{1,0:T(8,128)S(1)}) custom-call(s32[1]{0:T(128)} %bitcast.k_ref, f32[1]{0:T(128)S(6)} %copy.7.scale_ref, f32[1]{0:T(128)S(6)} %copy.8.shift_ref, s32[1,576]{1,0:T(1,128)S(1)} %broadcast_in_dim.4.wanted, bf16[192,1152]{1,0:T(8,128)(2,1)S(1)} %copy-done, ...), custom_call_target="tpu_custom_call" | custom-call | tf_op jit(solution)/shard_map/pallas_call | solution.py:205
  44.7 2.0 %shard_map.69 = (bf16[576,1152]{1,0:T(8,128)(2,1)S(1)}, f32[192,1152]{1,0:T(8,128)S(1)}, f32[192,1152]{1,0:T(8,128)S(1)}, bf16[192,1152]{1,0:T(8,128)(2,1)S(1)}) custom-call(s32[1]{0:T(128)} %bitcast.k_ref, s32[1]{0:T(128)} %bitcast.1.core_ref, f32[1]{0:T(128)S(6)} %copy.7.scale_ref, f32[1]{0:T(128)S(6)} %copy.8.shift_ref, bf16[192,1152]{1,0:T(8,128)(2,1)S(1)} %copy-done.1, ...), custom_call_target="tpu_custom_call" | custom-call | tf_op jit(solution)/shard_map/pallas_call | solution.py:205
  46.7 2.1 %collective-permute-start.8 = (bf16[576,1152]{1,0:T(8,128)(2,1)S(1)}, bf16[576,1152]{1,0:T(8,128)(2,1)S(1)}, u32[]{:S(2)}, u32[]{:S(2)}) collective-permute-start(bf16[576,1152]{1,0:T(8,128)(2,1)S(1)} %get-tuple-element.35), channel_id=1, source_target_pairs={{0,3},{1,4},{2,5},{3,0},{4,1},{5,2},{6,9},{7,10},{8,11},{9,6},{10,... | collective-permute-start | bytes 3981320 | tf_op jit(solution)/shard_map/ppermute | solution.py:30
  48.8 2.0 %shard_map.70 = (f32[576,1152]{1,0:T(8,128)S(1)}, bf16[192,1152]{1,0:T(8,128)(2,1)S(1)}, f32[192,1152]{1,0:T(8,128)S(1)}) custom-call(s32[1]{0:T(128)} %bitcast.k_ref, f32[1]{0:T(128)S(6)} %copy.7.scale_ref, f32[1]{0:T(128)S(6)} %copy.8.shift_ref, bf16[192,1152]{1,0:T(8,128)(2,1)S(1)} %copy-done.1, bf16[192,1152]{1,0:T(8,128)(2,1)S(1)} %broadcast_select_fusion.t2, ...), custom_call_target="tpu_custom_call" | custom-call | tf_op jit(solution)/shard_map/pallas_call | solution.py:205
  50.7 1.3 %collective-permute-start.12 = (bf16[192,1152]{1,0:T(8,128)(2,1)S(1)}, bf16[192,1152]{1,0:T(8,128)(2,1)}, u32[]{:S(2)}, u32[]{:S(2)}) collective-permute-start(bf16[192,1152]{1,0:T(8,128)(2,1)S(1)} %get-tuple-element.42), channel_id=1, source_target_pairs={{0,618},{1,613},{2,608},{3,591},{4,598},{5,605},{48,90},{49,85},{5... | collective-permute-start | bytes 1327112 | tf_op jit(solution)/shard_map/ppermute | solution.py:30
  52.1 0.9 %shard_map.71 = (f32[192,1152]{1,0:T(8,128)S(1)}, bf16[192,1152]{1,0:T(8,128)(2,1)}, bf16[192,1152]{1,0:T(8,128)(2,1)S(1)}) custom-call(f32[576,1152]{1,0:T(8,128)S(1)} %get-tuple-element.34.ours, bf16[576,1152]{1,0:T(8,128)(2,1)S(1)} %collective-permute-done.8.received), custom_call_target="tpu_custom_call" | custom-call | tf_op jit(solution)/shard_map/pallas_call | solution.py:205
  53.0 4.0 %collective-permute-start.9 = (bf16[192,1152]{1,0:T(8,128)(2,1)}, bf16[192,1152]{1,0:T(8,128)(2,1)S(1)}, u32[]{:S(2)}, u32[]{:S(2)}) collective-permute-start(bf16[192,1152]{1,0:T(8,128)(2,1)} %get-tuple-element.37), channel_id=1, source_target_pairs={{0,2},{1,0},{2,1},{3,5},{4,3},{5,4},{6,8},{7,6},{8,7},{9,11},{10,9... | collective-permute-start | bytes 1327112 | tf_op jit(solution)/shard_map/ppermute | solution.py:30
  57.0 3.6 %collective-permute-start.10 = (bf16[192,1152]{1,0:T(8,128)(2,1)S(1)}, bf16[192,1152]{1,0:T(8,128)(2,1)}, u32[]{:S(2)}, u32[]{:S(2)}) collective-permute-start(bf16[192,1152]{1,0:T(8,128)(2,1)S(1)} %get-tuple-element.38), channel_id=1, source_target_pairs={{0,1},{1,2},{2,0},{3,4},{4,5},{5,3},{6,7},{7,8},{8,6},{9,10},{10,1... | collective-permute-start | bytes 1327112 | tf_op jit(solution)/shard_map/ppermute | solution.py:30
  60.6 1.3 %collective-permute-start.11 = (bf16[192,1152]{1,0:T(8,128)(2,1)S(1)}, bf16[192,1152]{1,0:T(8,128)(2,1)S(1)}, u32[]{:S(2)}, u32[]{:S(2)}) collective-permute-start(bf16[192,1152]{1,0:T(8,128)(2,1)S(1)} %get-tuple-element.42), channel_id=1, source_target_pairs={{6,0},{7,1},{8,2},{9,3},{10,4},{11,5},{12,6},{13,7},{14,8},{15,9},... | collective-permute-start | bytes 1327112 | tf_op jit(solution)/shard_map/ppermute | solution.py:30
  62.6 1.9 %collective-permute-start.13 = (bf16[192,1152]{1,0:T(8,128)(2,1)}, bf16[192,1152]{1,0:T(8,128)(2,1)S(1)}, u32[]{:S(2)}, u32[]{:S(2)}) collective-permute-start(bf16[192,1152]{1,0:T(8,128)(2,1)} %collective-permute-done.12), channel_id=1, source_target_pairs={{15,189},{22,190},{29,191},{32,188},{37,187},{42,186},{63,45},{70,... | collective-permute-start | bytes 1327112 | tf_op jit(solution)/shard_map/ppermute | solution.py:30
  64.5 5.0 %collective-permute-done.9.back1 = bf16[192,1152]{1,0:T(8,128)(2,1)S(1)} collective-permute-done((bf16[192,1152]{1,0:T(8,128)(2,1)}, bf16[192,1152]{1,0:T(8,128)(2,1)S(1)}, u32[]{:S(2)}, u32[]{:S(2)}) %collective-permute-start.9) | collective-permute-done | bytes 442400 | tf_op jit(solution)/shard_map/ppermute | solution.py:30
  69.5 15.5 %collective-permute-done.10.back2 = bf16[192,1152]{1,0:T(8,128)(2,1)} collective-permute-done((bf16[192,1152]{1,0:T(8,128)(2,1)S(1)}, bf16[192,1152]{1,0:T(8,128)(2,1)}, u32[]{:S(2)}, u32[]{:S(2)}) %collective-permute-start.10) | collective-permute-done | bytes 442400 | tf_op jit(solution)/shard_map/ppermute | solution.py:30
  85.0 2.0 %shard_map.72 = f32[192,1152]{1,0:T(8,128)} custom-call(f32[192,1152]{1,0:T(8,128)S(1)} %get-tuple-element.36.gu0, bf16[192,1152]{1,0:T(8,128)(2,1)S(1)} %collective-permute-done.9.back1, bf16[192,1152]{1,0:T(8,128)(2,1)} %collective-permute-done.10.back2), custom_call_target="tpu_custom_call" | custom-call | flops 20000000000 | tf_op jit(solution)/shard_map/pallas_call | solution.py:205
  87.0 1.1 %shard_map.73 = f32[192,1152]{1,0:T(8,128)} custom-call(s32[1]{0:T(128)} %bitcast.4.late_ref, s32[1]{0:T(128)} %bitcast.5.far_ref, f32[192,1152]{1,0:T(8,128)S(1)} %get-tuple-element.41.gv0, bf16[192,1152]{1,0:T(8,128)(2,1)S(1)} %collective-permute-done.11.main, bf16[192,1152]{1,0:T(8,128)(2,1)S(1)} %collective-permute-done.13.relayed, ...), custom_call_target="tpu_custom_call" | custom-call | tf_op jit(solution)/shard_map/pallas_call | solution.py:205
  (23 shorter events, 1.9 us)
Async XLA Ops:
  0.6 42.3 %copy-start.1 = (bf16[192,1152]{1,0:T(8,128)(2,1)S(1)}, bf16[192,1152]{1,0:T(8,128)(2,1)}, u32[]{:S(2)}) copy-start(bf16[192,1152]{1,0:T(8,128)(2,1)} %t0.5) | copy-start | bytes 1327108
  0.6 42.3 %copy-start = (bf16[192,1152]{1,0:T(8,128)(2,1)S(1)}, bf16[192,1152]{1,0:T(8,128)(2,1)}, u32[]{:S(2)}) copy-start(bf16[192,1152]{1,0:T(8,128)(2,1)} %i0.3) | copy-start | bytes 1327108
  0.6 36.5 %copy-start.2 = (s32[192]{0:T(256)S(1)}, s32[192]{0:T(256)}, u32[]{:S(2)}) copy-start(s32[192]{0:T(256)} %param.7) | copy-start | bytes 2308
  0.7 15.8 %collective-permute-start.4 = (bf16[192,1152]{1,0:T(8,128)(2,1)}, bf16[192,1152]{1,0:T(8,128)(2,1)}, u32[]{:S(2)}, u32[]{:S(2)}) collective-permute-start(bf16[192,1152]{1,0:T(8,128)(2,1)} %t0.5), channel_id=1, source_target_pairs={{42,0},{43,7},{44,14},{45,33},{46,28},{47,23},{90,48},{91,55},{92,... | collective-permute-start | bytes 1327112 | tf_op jit(solution)/shard_map/ppermute | solution.py:30
  3.2 28.6 %collective-permute-start.1 = (bf16[192,1152]{1,0:T(8,128)(2,1)}, bf16[192,1152]{1,0:T(8,128)(2,1)S(1)}, u32[]{:S(2)}, u32[]{:S(2)}) collective-permute-start(bf16[192,1152]{1,0:T(8,128)(2,1)} %i0.3), channel_id=1, source_target_pairs={{0,2},{1,0},{2,1},{3,5},{4,3},{5,4},{6,8},{7,6},{8,7},{9,11},{10,9... | collective-permute-start | bytes 1327112 | tf_op jit(solution)/shard_map/ppermute | solution.py:30
  12.6 28.4 %collective-permute-start = (bf16[192,1152]{1,0:T(8,128)(2,1)}, bf16[192,1152]{1,0:T(8,128)(2,1)S(1)}, u32[]{:S(2)}, u32[]{:S(2)}) collective-permute-start(bf16[192,1152]{1,0:T(8,128)(2,1)} %i0.3), channel_id=1, source_target_pairs={{0,1},{1,2},{2,0},{3,4},{4,5},{5,3},{6,7},{7,8},{8,6},{9,10},{10,1... | collective-permute-start | bytes 1327112 | tf_op jit(solution)/shard_map/ppermute | solution.py:30
  14.5 29.7 %collective-permute-start.3 = (bf16[192,1152]{1,0:T(8,128)(2,1)}, bf16[192,1152]{1,0:T(8,128)(2,1)S(1)}, u32[]{:S(2)}, u32[]{:S(2)}) collective-permute-start(bf16[192,1152]{1,0:T(8,128)(2,1)} %t0.5), channel_id=1, source_target_pairs={{5,17},{11,23},{17,29},{23,35},{29,41},{35,47},{41,53},{47,59},{53... | collective-permute-start | bytes 1327112 | tf_op jit(solution)/shard_map/ppermute | solution.py:30
  15.2 29.0 %collective-permute-start.2 = (bf16[192,1152]{1,0:T(8,128)(2,1)}, bf16[192,1152]{1,0:T(8,128)(2,1)S(1)}, u32[]{:S(2)}, u32[]{:S(2)}) collective-permute-start(bf16[192,1152]{1,0:T(8,128)(2,1)} %t0.5), channel_id=1, source_target_pairs={{0,6},{1,7},{2,8},{3,9},{4,10},{5,11},{6,12},{7,13},{8,14},{9,15},... | collective-permute-start | bytes 1327112 | tf_op jit(solution)/shard_map/ppermute | solution.py:30
  16.5 27.7 %collective-permute-start.5 = (bf16[192,1152]{1,0:T(8,128)(2,1)}, bf16[192,1152]{1,0:T(8,128)(2,1)}, u32[]{:S(2)}, u32[]{:S(2)}) collective-permute-start(bf16[192,1152]{1,0:T(8,128)(2,1)} %collective-permute-done.4), channel_id=1, source_target_pairs={{0,48},{7,49},{14,50},{23,53},{28,52},{33,51},{48,96},{55,97},{62,... | collective-permute-start | bytes 1327112 | tf_op jit(solution)/shard_map/ppermute | solution.py:30
  33.8 10.8 %collective-permute-start.7 = (bf16[2,192,1152]{2,1,0:T(8,128)(2,1)}, bf16[2,192,1152]{2,1,0:T(8,128)(2,1)S(1)}, u32[]{:S(2)}, u32[]{:S(2)}) collective-permute-start(bf16[2,192,1152]{2,1,0:T(8,128)(2,1)} %pad_maximum_fusion), channel_id=1, source_target_pairs={{0,3},{1,4},{2,5},{3,0},{4,1},{5,2},{6,9},{7,10},{8,11},{9,6},{10,... | collective-permute-start | bytes 2654216 | tf_op jit(solution)/shard_map/ppermute | solution.py:30
  41.0 3.7 %collective-permute-start.6 = (bf16[192,1152]{1,0:T(8,128)(2,1)S(1)}, bf16[192,1152]{1,0:T(8,128)(2,1)S(1)}, u32[]{:S(2)}, u32[]{:S(2)}) collective-permute-start(bf16[192,1152]{1,0:T(8,128)(2,1)S(1)} %collective-permute-done.i1), channel_id=1, source_target_pairs={{0,3},{1,4},{2,5},{3,0},{4,1},{5,2},{6,9},{7,10},{8,11},{9,6},{10,... | collective-permute-start | bytes 1327112 | tf_op jit(solution)/shard_map/ppermute | solution.py:30
  46.7 5.4 %collective-permute-start.8 = (bf16[576,1152]{1,0:T(8,128)(2,1)S(1)}, bf16[576,1152]{1,0:T(8,128)(2,1)S(1)}, u32[]{:S(2)}, u32[]{:S(2)}) collective-permute-start(bf16[576,1152]{1,0:T(8,128)(2,1)S(1)} %get-tuple-element.35), channel_id=1, source_target_pairs={{0,3},{1,4},{2,5},{3,0},{4,1},{5,2},{6,9},{7,10},{8,11},{9,6},{10,... | collective-permute-start | bytes 3981320 | tf_op jit(solution)/shard_map/ppermute | solution.py:30
  50.7 11.9 %collective-permute-start.12 = (bf16[192,1152]{1,0:T(8,128)(2,1)S(1)}, bf16[192,1152]{1,0:T(8,128)(2,1)}, u32[]{:S(2)}, u32[]{:S(2)}) collective-permute-start(bf16[192,1152]{1,0:T(8,128)(2,1)S(1)} %get-tuple-element.42), channel_id=1, source_target_pairs={{0,618},{1,613},{2,608},{3,591},{4,598},{5,605},{48,90},{49,85},{5... | collective-permute-start | bytes 1327112 | tf_op jit(solution)/shard_map/ppermute | solution.py:30
  53.0 16.5 %collective-permute-start.9 = (bf16[192,1152]{1,0:T(8,128)(2,1)}, bf16[192,1152]{1,0:T(8,128)(2,1)S(1)}, u32[]{:S(2)}, u32[]{:S(2)}) collective-permute-start(bf16[192,1152]{1,0:T(8,128)(2,1)} %get-tuple-element.37), channel_id=1, source_target_pairs={{0,2},{1,0},{2,1},{3,5},{4,3},{5,4},{6,8},{7,6},{8,7},{9,11},{10,9... | collective-permute-start | bytes 1327112 | tf_op jit(solution)/shard_map/ppermute | solution.py:30
  57.0 28.0 %collective-permute-start.10 = (bf16[192,1152]{1,0:T(8,128)(2,1)S(1)}, bf16[192,1152]{1,0:T(8,128)(2,1)}, u32[]{:S(2)}, u32[]{:S(2)}) collective-permute-start(bf16[192,1152]{1,0:T(8,128)(2,1)S(1)} %get-tuple-element.38), channel_id=1, source_target_pairs={{0,1},{1,2},{2,0},{3,4},{4,5},{5,3},{6,7},{7,8},{8,6},{9,10},{10,1... | collective-permute-start | bytes 1327112 | tf_op jit(solution)/shard_map/ppermute | solution.py:30
  60.6 26.5 %collective-permute-start.11 = (bf16[192,1152]{1,0:T(8,128)(2,1)S(1)}, bf16[192,1152]{1,0:T(8,128)(2,1)S(1)}, u32[]{:S(2)}, u32[]{:S(2)}) collective-permute-start(bf16[192,1152]{1,0:T(8,128)(2,1)S(1)} %get-tuple-element.42), channel_id=1, source_target_pairs={{6,0},{7,1},{8,2},{9,3},{10,4},{11,5},{12,6},{13,7},{14,8},{15,9},... | collective-permute-start | bytes 1327112 | tf_op jit(solution)/shard_map/ppermute | solution.py:30
  61.9 25.1 %collective-permute-start.14 = (bf16[192,1152]{1,0:T(8,128)(2,1)S(1)}, bf16[192,1152]{1,0:T(8,128)(2,1)S(1)}, u32[]{:S(2)}, u32[]{:S(2)}) collective-permute-start(bf16[192,1152]{1,0:T(8,128)(2,1)S(1)} %get-tuple-element.43), channel_id=1, source_target_pairs={{5,761},{11,767},{17,5},{23,11},{29,17},{35,23},{41,29},{47,35},{5... | collective-permute-start | bytes 1327112 | tf_op jit(solution)/shard_map/ppermute | solution.py:30
  62.6 24.4 %collective-permute-start.13 = (bf16[192,1152]{1,0:T(8,128)(2,1)}, bf16[192,1152]{1,0:T(8,128)(2,1)S(1)}, u32[]{:S(2)}, u32[]{:S(2)}) collective-permute-start(bf16[192,1152]{1,0:T(8,128)(2,1)} %collective-permute-done.12), channel_id=1, source_target_pairs={{15,189},{22,190},{29,191},{32,188},{37,187},{42,186},{63,45},{70,... | collective-permute-start | bytes 1327112 | tf_op jit(solution)/shard_map/ppermute | solution.py:30

commit v5 on v4

--- a/solution.py
+++ b/solution.py
@@ -192,23 +192,13 @@
     gi2[...] = (ours[2 * ROWS :] + received[2 * ROWS :].astype(F32)).astype(LOW)
 
 
-def line_total(gu0, back1, back2, grad_text):
-    grad_text[...] = gu0[...] + (back1[...].astype(F32) + back2[...].astype(F32))
-
-
-def shift_total(late_ref, far_ref, gv0, main, relayed, far, grad_picture):
-    returned = jnp.where(late_ref[0] != 0, relayed[...], main[...]).astype(F32)
-    grad_picture[...] = gv0[...] + (returned + jnp.where(far_ref[0] != 0, far[...].astype(F32), 0.0))
-
-
-def kernel_call(body, n_small, args, outs, scratch=(), flops=0):
+def kernel_call(body, n_small, args, outs, scratch=()):
     return pl.pallas_call(
         body,
         out_shape=[jax.ShapeDtypeStruct(shape, kind) for shape, kind in outs],
         in_specs=[pl.BlockSpec(memory_space=pltpu.SMEM)] * n_small
         + [pl.BlockSpec(memory_space=pltpu.VMEM)] * (len(args) - n_small),
         out_specs=[pl.BlockSpec(memory_space=pltpu.VMEM)] * len(outs),
-        cost_estimate=pl.CostEstimate(flops=flops, bytes_accessed=0, transcendentals=0) if flops else None,
         scratch_shapes=[pltpu.VMEM(shape, LOW) for shape in scratch],
         compiler_params=pltpu.CompilerParams(vmem_limit_bytes=12 * 1024 * 1024),
     )(*args)
@@ -238,7 +228,7 @@
     relayed = after_detour(corner, 1)
     others = [cores_swapped(image1), cores_swapped(jnp.stack([image0, image2]))]
     raw = image1, image2
-    image1, image2, main, far, relayed = lax.optimization_barrier((image1, image2, main, far, relayed))
+    image1, image2, far, main, relayed = lax.optimization_barrier((image1, image2, far, main, relayed))
     coef0, gt0 = kernel_call(
         own_texts,
         3,
@@ -272,15 +262,10 @@
     back1 = line_turned(gi1, -1)
     back2 = line_turned(gi2, -2)
     back_relayed = after_detour(back_corner, -1)
-    [grad_image] = kernel_call(line_total, 0, [gi0, back1, back2], [(block, F32)], flops=20_000_000_000)
+    grad_image = gi0 + (back1.astype(F32) + back2.astype(F32))
     grad_image, gt0 = lax.optimization_barrier((grad_image, gt0))
-    flag = lambda value: value.astype(jnp.int32).reshape(1)
-    [grad_text] = kernel_call(
-        shift_total,
-        2,
-        [flag(y == LAP - 1), flag(here % GROUP == 5), gt0, back_main, back_relayed, far_back],
-        [(block, F32)],
-    )
+    back_text = jnp.where(y == LAP - 1, back_relayed, back_main)
+    grad_text = gt0 + (back_text.astype(F32) + jnp.where(here % GROUP == 5, far_back.astype(F32), 0.0))
     return grad_image, grad_text
 
 

time: 88.7 us -> 87.2 us (0.983)
  the two profiles are of different devices: /device:TPU:254 before, /device:TPU:1 now
where the time goes in v5:
time: 87.2 us; the launch traced here: 85.9 us
  starting transfers between devices  48 us (55%)
  waiting for transfers between devices  23.7 us (27%)
  other arithmetic  6.41 us (7%)
  Pallas kernels  5.45 us (6%)
  between operations  2.32 us (3%)
    ppermute x15, starting transfers between devices, sent(): return lax.ppermute(value, AXES, pairs)  48 us
    ppermute x15, waiting for transfers between devices, sent(): return lax.ppermute(value, AXES, pairs)  23.7 us
    pallas_call x4, Pallas kernels, kernel_call(): pl.pallas_call(body, out_shape=[jax.ShapeDtypeStruct(shape, kind) for sha...  5.45 us
    add x1, other arithmetic, on_device(): grad_image = gi0 + (back1.astype(F32) + back2.astype(F32))  2.17 us
    another operation x1, other arithmetic, on_device(): others = [cores_swapped(image1), cores_swapped(jnp.stack([image0, image2]))]  2.02 us
  transfers between devices with their start and end apart: 15, of which 3 were waited for; matrix products, arithmetic and copies ran while one was open for 6% of the time, Pallas kernels for 4%

profile of v5, /device:TPU:1, one launch (start us, length us, event | category | flops | bytes accessed | tf_op | source)
XLA Modules:
  0.0 85.9 jit_solution(5749129654338856945)
XLA Ops:
  0.7 1.6 %collective-permute-start.4 = (bf16[192,1152]{1,0:T(8,128)(2,1)}, bf16[192,1152]{1,0:T(8,128)(2,1)}, u32[]{:S(2)}, u32[]{:S(2)}) collective-permute-start(bf16[192,1152]{1,0:T(8,128)(2,1)} %t0.5), channel_id=1, source_target_pairs={{42,0},{43,7},{44,14},{45,33},{46,28},{47,23},{90,48},{91,55},{92,... | collective-permute-start | bytes 1327112 | tf_op jit(solution)/shard_map/ppermute | solution.py:30
  2.2 6.6 %collective-permute-start.1 = (bf16[192,1152]{1,0:T(8,128)(2,1)}, bf16[192,1152]{1,0:T(8,128)(2,1)S(1)}, u32[]{:S(2)}, u32[]{:S(2)}) collective-permute-start(bf16[192,1152]{1,0:T(8,128)(2,1)} %i0.3), channel_id=1, source_target_pairs={{0,2},{1,0},{2,1},{3,5},{4,3},{5,4},{6,8},{7,6},{8,7},{9,11},{10,9... | collective-permute-start | bytes 1327112 | tf_op jit(solution)/shard_map/ppermute | solution.py:30
  8.9 1.9 %collective-permute-start = (bf16[192,1152]{1,0:T(8,128)(2,1)}, bf16[192,1152]{1,0:T(8,128)(2,1)S(1)}, u32[]{:S(2)}, u32[]{:S(2)}) collective-permute-start(bf16[192,1152]{1,0:T(8,128)(2,1)} %i0.3), channel_id=1, source_target_pairs={{0,1},{1,2},{2,0},{3,4},{4,5},{5,3},{6,7},{7,8},{8,6},{9,10},{10,1... | collective-permute-start | bytes 1327112 | tf_op jit(solution)/shard_map/ppermute | solution.py:30
  10.8 3.2 %collective-permute-start.3 = (bf16[192,1152]{1,0:T(8,128)(2,1)}, bf16[192,1152]{1,0:T(8,128)(2,1)S(1)}, u32[]{:S(2)}, u32[]{:S(2)}) collective-permute-start(bf16[192,1152]{1,0:T(8,128)(2,1)} %t0.5), channel_id=1, source_target_pairs={{0,6},{1,7},{2,8},{3,9},{4,10},{5,11},{6,12},{7,13},{8,14},{9,15},... | collective-permute-start | bytes 1327112 | tf_op jit(solution)/shard_map/ppermute | solution.py:30
  14.0 0.7 collective-permute-start.2
  14.7 1.3 %collective-permute-start.5 = (bf16[192,1152]{1,0:T(8,128)(2,1)}, bf16[192,1152]{1,0:T(8,128)(2,1)}, u32[]{:S(2)}, u32[]{:S(2)}) collective-permute-start(bf16[192,1152]{1,0:T(8,128)(2,1)} %collective-permute-done.4), channel_id=1, source_target_pairs={{0,48},{7,49},{14,50},{23,53},{28,52},{33,51},{48,96},{55,97},{62,... | collective-permute-start | bytes 1327112 | tf_op jit(solution)/shard_map/ppermute | solution.py:30
  16.0 2.0 %pad_maximum_fusion = bf16[2,192,1152]{2,1,0:T(8,128)(2,1)} fusion(bf16[1,192,1152]{2,1,0:T(8,128)(2,1)S(1)} %bitcast.5, bf16[1,192,1152]{2,1,0:T(8,128)(2,1)} %bitcast.4), kind=kLoop, calls=%fused_computation | loop fusion | flops 442368 | bytes 1769472 | tf_op jit(solution)/shard_map/stack | solution.py:229
  18.1 18.3 %collective-permute-start.7 = (bf16[2,192,1152]{2,1,0:T(8,128)(2,1)}, bf16[2,192,1152]{2,1,0:T(8,128)(2,1)S(1)}, u32[]{:S(2)}, u32[]{:S(2)}) collective-permute-start(bf16[2,192,1152]{2,1,0:T(8,128)(2,1)} %pad_maximum_fusion), channel_id=1, source_target_pairs={{0,3},{1,4},{2,5},{3,0},{4,1},{5,2},{6,9},{7,10},{8,11},{9,6},{10,... | collective-permute-start | bytes 2654216 | tf_op jit(solution)/shard_map/ppermute | solution.py:30
  37.9 1.9 %collective-permute-start.6 = (bf16[192,1152]{1,0:T(8,128)(2,1)S(1)}, bf16[192,1152]{1,0:T(8,128)(2,1)S(1)}, u32[]{:S(2)}, u32[]{:S(2)}) collective-permute-start(bf16[192,1152]{1,0:T(8,128)(2,1)S(1)} %collective-permute-done.i1), channel_id=1, source_target_pairs={{0,3},{1,4},{2,5},{3,0},{4,1},{5,2},{6,9},{7,10},{8,11},{9,6},{10,... | collective-permute-start | bytes 1327112 | tf_op jit(solution)/shard_map/ppermute | solution.py:30
  39.8 1.3 %shard_map.68 = (bf16[192,576]{1,0:T(8,128)(2,1)S(1)}, f32[192,1152]{1,0:T(8,128)S(1)}) custom-call(s32[1]{0:T(128)} %bitcast.k_ref, f32[1]{0:T(128)S(6)} %copy.7.scale_ref, f32[1]{0:T(128)S(6)} %copy.8.shift_ref, s32[1,576]{1,0:T(1,128)S(1)} %broadcast_in_dim.8.wanted, bf16[192,1152]{1,0:T(8,128)(2,1)S(1)} %copy-done, ...), custom_call_target="tpu_custom_call" | custom-call | tf_op jit(solution)/shard_map/pallas_call | solution.py:196
  41.1 7.8 %collective-permute-done.5 = bf16[192,1152]{1,0:T(8,128)(2,1)} collective-permute-done((bf16[192,1152]{1,0:T(8,128)(2,1)}, bf16[192,1152]{1,0:T(8,128)(2,1)}, u32[]{:S(2)}, u32[]{:S(2)}) %collective-permute-start.5) | collective-permute-done | bytes 442400 | tf_op jit(solution)/shard_map/ppermute | solution.py:30
  48.9 1.1 %broadcast_select_fusion.t2 = bf16[192,1152]{1,0:T(8,128)(2,1)S(1)} fusion(bf16[192,1152]{1,0:T(8,128)(2,1)} %collective-permute-done.5, bf16[192,1152]{1,0:T(8,128)(2,1)S(1)} %collective-permute-done.3, pred[]{:T(512)S(6)} %eq.14), kind=kLoop, calls=%fused_computation.3 | loop fusion | flops 221184 | bytes 1327105 | tf_op jit(solution)/shard_map/jit(_where)/select_n | solution.py:239
  50.0 2.0 %shard_map.69 = (bf16[576,1152]{1,0:T(8,128)(2,1)S(1)}, f32[192,1152]{1,0:T(8,128)S(1)}, f32[192,1152]{1,0:T(8,128)S(1)}, bf16[192,1152]{1,0:T(8,128)(2,1)S(1)}) custom-call(s32[1]{0:T(128)} %bitcast.k_ref, s32[1]{0:T(128)} %bitcast.1.core_ref, f32[1]{0:T(128)S(6)} %copy.7.scale_ref, f32[1]{0:T(128)S(6)} %copy.8.shift_ref, bf16[192,1152]{1,0:T(8,128)(2,1)S(1)} %copy-done.1, ...), custom_call_target="tpu_custom_call" | custom-call | tf_op jit(solution)/shard_map/pallas_call | solution.py:196
  52.0 1.9 %collective-permute-start.8 = (bf16[576,1152]{1,0:T(8,128)(2,1)S(1)}, bf16[576,1152]{1,0:T(8,128)(2,1)S(1)}, u32[]{:S(2)}, u32[]{:S(2)}) collective-permute-start(bf16[576,1152]{1,0:T(8,128)(2,1)S(1)} %get-tuple-element.35), channel_id=1, source_target_pairs={{0,3},{1,4},{2,5},{3,0},{4,1},{5,2},{6,9},{7,10},{8,11},{9,6},{10,... | collective-permute-start | bytes 3981320 | tf_op jit(solution)/shard_map/ppermute | solution.py:30
  54.0 2.0 %shard_map.70 = (f32[576,1152]{1,0:T(8,128)S(1)}, bf16[192,1152]{1,0:T(8,128)(2,1)S(1)}, f32[192,1152]{1,0:T(8,128)S(1)}) custom-call(s32[1]{0:T(128)} %bitcast.k_ref, f32[1]{0:T(128)S(6)} %copy.7.scale_ref, f32[1]{0:T(128)S(6)} %copy.8.shift_ref, bf16[192,1152]{1,0:T(8,128)(2,1)S(1)} %copy-done.1, bf16[192,1152]{1,0:T(8,128)(2,1)S(1)} %broadcast_select_fusion.t2, ...), custom_call_target="tpu_custom_call" | custom-call | tf_op jit(solution)/shard_map/pallas_call | solution.py:196
  55.9 2.1 %collective-permute-start.11 = (bf16[192,1152]{1,0:T(8,128)(2,1)S(1)}, bf16[192,1152]{1,0:T(8,128)(2,1)}, u32[]{:S(2)}, u32[]{:S(2)}) collective-permute-start(bf16[192,1152]{1,0:T(8,128)(2,1)S(1)} %get-tuple-element.42), channel_id=1, source_target_pairs={{0,618},{1,613},{2,608},{3,591},{4,598},{5,605},{48,90},{49,85},{5... | collective-permute-start | bytes 1327112 | tf_op jit(solution)/shard_map/ppermute | solution.py:30
  58.2 1.9 %collective-permute-start.9 = (bf16[192,1152]{1,0:T(8,128)(2,1)S(1)}, bf16[192,1152]{1,0:T(8,128)(2,1)}, u32[]{:S(2)}, u32[]{:S(2)}) collective-permute-start(bf16[192,1152]{1,0:T(8,128)(2,1)S(1)} %get-tuple-element.37), channel_id=1, source_target_pairs={{0,2},{1,0},{2,1},{3,5},{4,3},{5,4},{6,8},{7,6},{8,7},{9,11},{10,9... | collective-permute-start | bytes 1327112 | tf_op jit(solution)/shard_map/ppermute | solution.py:30
  60.2 3.8 %collective-permute-start.10 = (bf16[192,1152]{1,0:T(8,128)(2,1)S(1)}, bf16[192,1152]{1,0:T(8,128)(2,1)}, u32[]{:S(2)}, u32[]{:S(2)}) collective-permute-start(bf16[192,1152]{1,0:T(8,128)(2,1)S(1)} %get-tuple-element.38), channel_id=1, source_target_pairs={{0,1},{1,2},{2,0},{3,4},{4,5},{5,3},{6,7},{7,8},{8,6},{9,10},{10,1... | collective-permute-start | bytes 1327112 | tf_op jit(solution)/shard_map/ppermute | solution.py:30
  64.0 1.3 %collective-permute-start.13 = (bf16[192,1152]{1,0:T(8,128)(2,1)S(1)}, bf16[192,1152]{1,0:T(8,128)(2,1)S(1)}, u32[]{:S(2)}, u32[]{:S(2)}) collective-permute-start(bf16[192,1152]{1,0:T(8,128)(2,1)S(1)} %get-tuple-element.42), channel_id=1, source_target_pairs={{6,0},{7,1},{8,2},{9,3},{10,4},{11,5},{12,6},{13,7},{14,8},{15,9},... | collective-permute-start | bytes 1327112 | tf_op jit(solution)/shard_map/ppermute | solution.py:30
  66.0 0.7 collective-permute-start.12
  66.7 5.5 %collective-permute-done.9 = bf16[192,1152]{1,0:T(8,128)(2,1)} collective-permute-done((bf16[192,1152]{1,0:T(8,128)(2,1)S(1)}, bf16[192,1152]{1,0:T(8,128)(2,1)}, u32[]{:S(2)}, u32[]{:S(2)}) %collective-permute-start.9) | collective-permute-done | bytes 442400 | tf_op jit(solution)/shard_map/ppermute | solution.py:30
  72.3 10.3 %collective-permute-done.10 = bf16[192,1152]{1,0:T(8,128)(2,1)} collective-permute-done((bf16[192,1152]{1,0:T(8,128)(2,1)S(1)}, bf16[192,1152]{1,0:T(8,128)(2,1)}, u32[]{:S(2)}, u32[]{:S(2)}) %collective-permute-start.10) | collective-permute-done | bytes 442400 | tf_op jit(solution)/shard_map/ppermute | solution.py:30
  82.6 2.2 %add_add_fusion.1 = f32[192,1152]{1,0:T(8,128)} fusion(f32[192,1152]{1,0:T(8,128)S(1)} %get-tuple-element.36, bf16[192,1152]{1,0:T(8,128)(2,1)} %collective-permute-done.10, bf16[192,1152]{1,0:T(8,128)(2,1)} %collective-permute-done.9), kind=kLoop, calls=%fused_computation.2 | loop fusion | flops 884736 | bytes 2654208 | tf_op jit(solution)/shard_map/add | solution.py:265
  84.8 1.1 %add_add_fusion = f32[192,1152]{1,0:T(8,128)} fusion(f32[192,1152]{1,0:T(8,128)S(1)} %get-tuple-element.41, bf16[192,1152]{1,0:T(8,128)(2,1)S(1)} %collective-permute-done.14, bf16[192,1152]{1,0:T(8,128)(2,1)S(1)} %collective-permute-done.12, bf16[192,1152]{1,0:T(8,128)(2,1)S(1)} %collective-permute-done.13, pred[]{:T(512)S(6)} %eq.16, pred[]{:T(512)S(6)} %eq.15), kind=kLoop, calls=%fused_computation.1 | loop fusion | flops 1327104 | bytes 3096578 | tf_op jit(solution)/shard_map/add | solution.py:268
  (23 shorter events, 1.0 us)
Async XLA Ops:
  0.6 39.2 %copy-start.1 = (bf16[192,1152]{1,0:T(8,128)(2,1)S(1)}, bf16[192,1152]{1,0:T(8,128)(2,1)}, u32[]{:S(2)}) copy-start(bf16[192,1152]{1,0:T(8,128)(2,1)} %t0.5) | copy-start | bytes 1327108
  0.6 39.2 %copy-start = (bf16[192,1152]{1,0:T(8,128)(2,1)S(1)}, bf16[192,1152]{1,0:T(8,128)(2,1)}, u32[]{:S(2)}) copy-start(bf16[192,1152]{1,0:T(8,128)(2,1)} %i0.3) | copy-start | bytes 1327108
  0.6 37.1 %copy-start.2 = (s32[192]{0:T(256)S(1)}, s32[192]{0:T(256)}, u32[]{:S(2)}) copy-start(s32[192]{0:T(256)} %param.7) | copy-start | bytes 2308
  0.7 14.1 %collective-permute-start.4 = (bf16[192,1152]{1,0:T(8,128)(2,1)}, bf16[192,1152]{1,0:T(8,128)(2,1)}, u32[]{:S(2)}, u32[]{:S(2)}) collective-permute-start(bf16[192,1152]{1,0:T(8,128)(2,1)} %t0.5), channel_id=1, source_target_pairs={{42,0},{43,7},{44,14},{45,33},{46,28},{47,23},{90,48},{91,55},{92,... | collective-permute-start | bytes 1327112 | tf_op jit(solution)/shard_map/ppermute | solution.py:30
  2.2 13.8 %collective-permute-start.1 = (bf16[192,1152]{1,0:T(8,128)(2,1)}, bf16[192,1152]{1,0:T(8,128)(2,1)S(1)}, u32[]{:S(2)}, u32[]{:S(2)}) collective-permute-start(bf16[192,1152]{1,0:T(8,128)(2,1)} %i0.3), channel_id=1, source_target_pairs={{0,2},{1,0},{2,1},{3,5},{4,3},{5,4},{6,8},{7,6},{8,7},{9,11},{10,9... | collective-permute-start | bytes 1327112 | tf_op jit(solution)/shard_map/ppermute | solution.py:30
  8.9 29.0 %collective-permute-start = (bf16[192,1152]{1,0:T(8,128)(2,1)}, bf16[192,1152]{1,0:T(8,128)(2,1)S(1)}, u32[]{:S(2)}, u32[]{:S(2)}) collective-permute-start(bf16[192,1152]{1,0:T(8,128)(2,1)} %i0.3), channel_id=1, source_target_pairs={{0,1},{1,2},{2,0},{3,4},{4,5},{5,3},{6,7},{7,8},{8,6},{9,10},{10,1... | collective-permute-start | bytes 1327112 | tf_op jit(solution)/shard_map/ppermute | solution.py:30
  10.8 30.3 %collective-permute-start.3 = (bf16[192,1152]{1,0:T(8,128)(2,1)}, bf16[192,1152]{1,0:T(8,128)(2,1)S(1)}, u32[]{:S(2)}, u32[]{:S(2)}) collective-permute-start(bf16[192,1152]{1,0:T(8,128)(2,1)} %t0.5), channel_id=1, source_target_pairs={{0,6},{1,7},{2,8},{3,9},{4,10},{5,11},{6,12},{7,13},{8,14},{9,15},... | collective-permute-start | bytes 1327112 | tf_op jit(solution)/shard_map/ppermute | solution.py:30
  14.0 27.1 %collective-permute-start.2 = (bf16[192,1152]{1,0:T(8,128)(2,1)}, bf16[192,1152]{1,0:T(8,128)(2,1)S(1)}, u32[]{:S(2)}, u32[]{:S(2)}) collective-permute-start(bf16[192,1152]{1,0:T(8,128)(2,1)} %t0.5), channel_id=1, source_target_pairs={{5,17},{11,23},{17,29},{23,35},{29,41},{35,47},{41,53},{47,59},{53... | collective-permute-start | bytes 1327112 | tf_op jit(solution)/shard_map/ppermute | solution.py:30
  14.7 34.2 %collective-permute-start.5 = (bf16[192,1152]{1,0:T(8,128)(2,1)}, bf16[192,1152]{1,0:T(8,128)(2,1)}, u32[]{:S(2)}, u32[]{:S(2)}) collective-permute-start(bf16[192,1152]{1,0:T(8,128)(2,1)} %collective-permute-done.4), channel_id=1, source_target_pairs={{0,48},{7,49},{14,50},{23,53},{28,52},{33,51},{48,96},{55,97},{62,... | collective-permute-start | bytes 1327112 | tf_op jit(solution)/shard_map/ppermute | solution.py:30
  18.1 31.9 %collective-permute-start.7 = (bf16[2,192,1152]{2,1,0:T(8,128)(2,1)}, bf16[2,192,1152]{2,1,0:T(8,128)(2,1)S(1)}, u32[]{:S(2)}, u32[]{:S(2)}) collective-permute-start(bf16[2,192,1152]{2,1,0:T(8,128)(2,1)} %pad_maximum_fusion), channel_id=1, source_target_pairs={{0,3},{1,4},{2,5},{3,0},{4,1},{5,2},{6,9},{7,10},{8,11},{9,6},{10,... | collective-permute-start | bytes 2654216 | tf_op jit(solution)/shard_map/ppermute | solution.py:30
  37.9 12.1 %collective-permute-start.6 = (bf16[192,1152]{1,0:T(8,128)(2,1)S(1)}, bf16[192,1152]{1,0:T(8,128)(2,1)S(1)}, u32[]{:S(2)}, u32[]{:S(2)}) collective-permute-start(bf16[192,1152]{1,0:T(8,128)(2,1)S(1)} %collective-permute-done.i1), channel_id=1, source_target_pairs={{0,3},{1,4},{2,5},{3,0},{4,1},{5,2},{6,9},{7,10},{8,11},{9,6},{10,... | collective-permute-start | bytes 1327112 | tf_op jit(solution)/shard_map/ppermute | solution.py:30
  52.0 6.0 %collective-permute-start.8 = (bf16[576,1152]{1,0:T(8,128)(2,1)S(1)}, bf16[576,1152]{1,0:T(8,128)(2,1)S(1)}, u32[]{:S(2)}, u32[]{:S(2)}) collective-permute-start(bf16[576,1152]{1,0:T(8,128)(2,1)S(1)} %get-tuple-element.35), channel_id=1, source_target_pairs={{0,3},{1,4},{2,5},{3,0},{4,1},{5,2},{6,9},{7,10},{8,11},{9,6},{10,... | collective-permute-start | bytes 3981320 | tf_op jit(solution)/shard_map/ppermute | solution.py:30
  55.9 10.1 %collective-permute-start.11 = (bf16[192,1152]{1,0:T(8,128)(2,1)S(1)}, bf16[192,1152]{1,0:T(8,128)(2,1)}, u32[]{:S(2)}, u32[]{:S(2)}) collective-permute-start(bf16[192,1152]{1,0:T(8,128)(2,1)S(1)} %get-tuple-element.42), channel_id=1, source_target_pairs={{0,618},{1,613},{2,608},{3,591},{4,598},{5,605},{48,90},{49,85},{5... | collective-permute-start | bytes 1327112 | tf_op jit(solution)/shard_map/ppermute | solution.py:30
  58.2 14.0 %collective-permute-start.9 = (bf16[192,1152]{1,0:T(8,128)(2,1)S(1)}, bf16[192,1152]{1,0:T(8,128)(2,1)}, u32[]{:S(2)}, u32[]{:S(2)}) collective-permute-start(bf16[192,1152]{1,0:T(8,128)(2,1)S(1)} %get-tuple-element.37), channel_id=1, source_target_pairs={{0,2},{1,0},{2,1},{3,5},{4,3},{5,4},{6,8},{7,6},{8,7},{9,11},{10,9... | collective-permute-start | bytes 1327112 | tf_op jit(solution)/shard_map/ppermute | solution.py:30
  60.2 22.4 %collective-permute-start.10 = (bf16[192,1152]{1,0:T(8,128)(2,1)S(1)}, bf16[192,1152]{1,0:T(8,128)(2,1)}, u32[]{:S(2)}, u32[]{:S(2)}) collective-permute-start(bf16[192,1152]{1,0:T(8,128)(2,1)S(1)} %get-tuple-element.38), channel_id=1, source_target_pairs={{0,1},{1,2},{2,0},{3,4},{4,5},{5,3},{6,7},{7,8},{8,6},{9,10},{10,1... | collective-permute-start | bytes 1327112 | tf_op jit(solution)/shard_map/ppermute | solution.py:30
  64.0 20.7 %collective-permute-start.13 = (bf16[192,1152]{1,0:T(8,128)(2,1)S(1)}, bf16[192,1152]{1,0:T(8,128)(2,1)S(1)}, u32[]{:S(2)}, u32[]{:S(2)}) collective-permute-start(bf16[192,1152]{1,0:T(8,128)(2,1)S(1)} %get-tuple-element.42), channel_id=1, source_target_pairs={{6,0},{7,1},{8,2},{9,3},{10,4},{11,5},{12,6},{13,7},{14,8},{15,9},... | collective-permute-start | bytes 1327112 | tf_op jit(solution)/shard_map/ppermute | solution.py:30
  65.3 19.5 %collective-permute-start.14 = (bf16[192,1152]{1,0:T(8,128)(2,1)S(1)}, bf16[192,1152]{1,0:T(8,128)(2,1)S(1)}, u32[]{:S(2)}, u32[]{:S(2)}) collective-permute-start(bf16[192,1152]{1,0:T(8,128)(2,1)S(1)} %get-tuple-element.43), channel_id=1, source_target_pairs={{5,761},{11,767},{17,5},{23,11},{29,17},{35,23},{41,29},{47,35},{5... | collective-permute-start | bytes 1327112 | tf_op jit(solution)/shard_map/ppermute | solution.py:30
  66.0 18.7 %collective-permute-start.12 = (bf16[192,1152]{1,0:T(8,128)(2,1)}, bf16[192,1152]{1,0:T(8,128)(2,1)S(1)}, u32[]{:S(2)}, u32[]{:S(2)}) collective-permute-start(bf16[192,1152]{1,0:T(8,128)(2,1)} %collective-permute-done.11), channel_id=1, source_target_pairs={{15,189},{22,190},{29,191},{32,188},{37,187},{42,186},{63,45},{70,... | collective-permute-start | bytes 1327112 | tf_op jit(solution)/shard_map/ppermute | solution.py:30

commit v6 on v5

--- a/solution.py
+++ b/solution.py
@@ -186,8 +186,7 @@
     gt0[...] = gt0p[...] + own_part[...]
 
 
-def both_cores(ours, received, gi0, gi1, gi2):
-    gi0[...] = ours[0:ROWS] + received[0:ROWS].astype(F32)
+def both_cores(ours, received, gi1, gi2):
     gi1[...] = (ours[ROWS : 2 * ROWS] + received[ROWS : 2 * ROWS].astype(F32)).astype(LOW)
     gi2[...] = (ours[2 * ROWS :] + received[2 * ROWS :].astype(F32)).astype(LOW)
 
@@ -255,13 +254,12 @@
     received = cores_swapped(theirs)
     back_corner = detour(share, -1)
     back_main = straight(share, -1)
-    gi0, gi1, gi2 = kernel_call(
-        both_cores, 0, [ours, received], [(block, F32), (block, LOW), (block, LOW)]
-    )
+    gi1, gi2 = kernel_call(both_cores, 0, [ours, received], [(block, LOW), (block, LOW)])
     far_back = sent(far, lambda b: b - 2 * GROUP if b % GROUP == 5 else None)
     back1 = line_turned(gi1, -1)
     back2 = line_turned(gi2, -2)
     back_relayed = after_detour(back_corner, -1)
+    gi0 = ours[:ROWS] + received[:ROWS].astype(F32)
     grad_image = gi0 + (back1.astype(F32) + back2.astype(F32))
     grad_image, gt0 = lax.optimization_barrier((grad_image, gt0))
     back_text = jnp.where(y == LAP - 1, back_relayed, back_main)

time: 87.2 us -> 91.4 us (1.048)
  local copies, waits for them, and re-layouts: 0.02 us -> 2.83 us
  Pallas kernels: 5.45 us -> 6.42 us
    unnamed x6 -> x22, local copies, waits for them, and re-layouts: 0.01 us -> 2.82 us
    pallas_call x4, Pallas kernels: 5.45 us -> 6.42 us  [kernel_call(): pl.pallas_call(body, out_shape=[jax.ShapeDtypeStruct(shape, kind) for sha...]
  transfers between devices with their start and end apart: 15 -> 15, of which waited for: 3 -> 3; matrix products, arithmetic and copies ran while one was open for 6% -> 6% of each run, Pallas kernels for 4% -> 5%
where the time goes in v6:
time: 91.4 us; the launch traced here: 90.1 us
  starting transfers between devices  48.1 us (53%)
  waiting for transfers between devices  23.7 us (26%)
  other arithmetic  6.57 us (7%)
  Pallas kernels  6.42 us (7%)
  local copies, waits for them, and re-layouts  2.83 us (3%)
  between operations  2.39 us (3%)
    ppermute x15, starting transfers between devices, sent(): return lax.ppermute(value, AXES, pairs)  48.1 us
    ppermute x15, waiting for transfers between devices, sent(): return lax.ppermute(value, AXES, pairs)  23.7 us
    pallas_call x4, Pallas kernels, kernel_call(): pl.pallas_call(body, out_shape=[jax.ShapeDtypeStruct(shape, kind) for sha...  6.42 us
    unnamed x22, local copies, waits for them, and re-layouts  2.82 us
    add x1, other arithmetic, on_device(): grad_image = gi0 + (back1.astype(F32) + back2.astype(F32))  2.36 us
    another operation x1, other arithmetic, on_device(): others = [cores_swapped(image1), cores_swapped(jnp.stack([image0, image2]))]  2.02 us
  transfers between devices with their start and end apart: 15, of which 3 were waited for; matrix products, arithmetic and copies ran while one was open for 6% of the time, Pallas kernels for 5%

profile of v6, /device:TPU:1, one launch (start us, length us, event | category | flops | bytes accessed | tf_op | source)
XLA Modules:
  0.0 90.1 jit_solution(17079157717061044812)
XLA Ops:
  0.7 1.6 %collective-permute-start.4 = (bf16[192,1152]{1,0:T(8,128)(2,1)}, bf16[192,1152]{1,0:T(8,128)(2,1)}, u32[]{:S(2)}, u32[]{:S(2)}) collective-permute-start(bf16[192,1152]{1,0:T(8,128)(2,1)} %t0.5), channel_id=1, source_target_pairs={{42,0},{43,7},{44,14},{45,33},{46,28},{47,23},{90,48},{91,55},{92,... | collective-permute-start | bytes 1327112 | tf_op jit(solution)/shard_map/ppermute | solution.py:30
  2.2 6.6 %collective-permute-start.1 = (bf16[192,1152]{1,0:T(8,128)(2,1)}, bf16[192,1152]{1,0:T(8,128)(2,1)S(1)}, u32[]{:S(2)}, u32[]{:S(2)}) collective-permute-start(bf16[192,1152]{1,0:T(8,128)(2,1)} %i0.3), channel_id=1, source_target_pairs={{0,2},{1,0},{2,1},{3,5},{4,3},{5,4},{6,8},{7,6},{8,7},{9,11},{10,9... | collective-permute-start | bytes 1327112 | tf_op jit(solution)/shard_map/ppermute | solution.py:30
  8.9 1.9 %collective-permute-start = (bf16[192,1152]{1,0:T(8,128)(2,1)}, bf16[192,1152]{1,0:T(8,128)(2,1)S(1)}, u32[]{:S(2)}, u32[]{:S(2)}) collective-permute-start(bf16[192,1152]{1,0:T(8,128)(2,1)} %i0.3), channel_id=1, source_target_pairs={{0,1},{1,2},{2,0},{3,4},{4,5},{5,3},{6,7},{7,8},{8,6},{9,10},{10,1... | collective-permute-start | bytes 1327112 | tf_op jit(solution)/shard_map/ppermute | solution.py:30
  10.8 4.0 %collective-permute-start.3 = (bf16[192,1152]{1,0:T(8,128)(2,1)}, bf16[192,1152]{1,0:T(8,128)(2,1)}, u32[]{:S(2)}, u32[]{:S(2)}) collective-permute-start(bf16[192,1152]{1,0:T(8,128)(2,1)} %t0.5), channel_id=1, source_target_pairs={{0,6},{1,7},{2,8},{3,9},{4,10},{5,11},{6,12},{7,13},{8,14},{9,15},... | collective-permute-start | bytes 1327112 | tf_op jit(solution)/shard_map/ppermute | solution.py:30
  15.5 1.3 %collective-permute-start.5 = (bf16[192,1152]{1,0:T(8,128)(2,1)}, bf16[192,1152]{1,0:T(8,128)(2,1)}, u32[]{:S(2)}, u32[]{:S(2)}) collective-permute-start(bf16[192,1152]{1,0:T(8,128)(2,1)} %collective-permute-done.4), channel_id=1, source_target_pairs={{0,48},{7,49},{14,50},{23,53},{28,52},{33,51},{48,96},{55,97},{62,... | collective-permute-start | bytes 1327112 | tf_op jit(solution)/shard_map/ppermute | solution.py:30
  16.8 2.0 %pad_maximum_fusion = bf16[2,192,1152]{2,1,0:T(8,128)(2,1)} fusion(bf16[1,192,1152]{2,1,0:T(8,128)(2,1)S(1)} %bitcast.5, bf16[1,192,1152]{2,1,0:T(8,128)(2,1)} %bitcast.4), kind=kLoop, calls=%fused_computation | loop fusion | flops 442368 | bytes 1769472 | tf_op jit(solution)/shard_map/stack | solution.py:228
  18.8 17.6 %collective-permute-start.7 = (bf16[2,192,1152]{2,1,0:T(8,128)(2,1)}, bf16[2,192,1152]{2,1,0:T(8,128)(2,1)S(1)}, u32[]{:S(2)}, u32[]{:S(2)}) collective-permute-start(bf16[2,192,1152]{2,1,0:T(8,128)(2,1)} %pad_maximum_fusion), channel_id=1, source_target_pairs={{0,3},{1,4},{2,5},{3,0},{4,1},{5,2},{6,9},{7,10},{8,11},{9,6},{10,... | collective-permute-start | bytes 2654216 | tf_op jit(solution)/shard_map/ppermute | solution.py:30
  37.9 1.9 %collective-permute-start.6 = (bf16[192,1152]{1,0:T(8,128)(2,1)S(1)}, bf16[192,1152]{1,0:T(8,128)(2,1)S(1)}, u32[]{:S(2)}, u32[]{:S(2)}) collective-permute-start(bf16[192,1152]{1,0:T(8,128)(2,1)S(1)} %collective-permute-done.i1), channel_id=1, source_target_pairs={{0,3},{1,4},{2,5},{3,0},{4,1},{5,2},{6,9},{7,10},{8,11},{9,6},{10,... | collective-permute-start | bytes 1327112 | tf_op jit(solution)/shard_map/ppermute | solution.py:30
  39.8 1.3 %shard_map.68 = (bf16[192,576]{1,0:T(8,128)(2,1)S(1)}, f32[192,1152]{1,0:T(8,128)S(1)}) custom-call(s32[1]{0:T(128)} %bitcast.k_ref, f32[1]{0:T(128)S(6)} %copy.7.scale_ref, f32[1]{0:T(128)S(6)} %copy.8.shift_ref, s32[1,576]{1,0:T(1,128)S(1)} %broadcast_in_dim.8.wanted, bf16[192,1152]{1,0:T(8,128)(2,1)S(1)} %copy-done, ...), custom_call_target="tpu_custom_call" | custom-call | tf_op jit(solution)/shard_map/pallas_call | solution.py:195
  41.1 7.8 %collective-permute-done.5 = bf16[192,1152]{1,0:T(8,128)(2,1)} collective-permute-done((bf16[192,1152]{1,0:T(8,128)(2,1)}, bf16[192,1152]{1,0:T(8,128)(2,1)}, u32[]{:S(2)}, u32[]{:S(2)}) %collective-permute-start.5) | collective-permute-done | bytes 442400 | tf_op jit(solution)/shard_map/ppermute | solution.py:30
  48.9 1.1 %broadcast_select_fusion.t2 = bf16[192,1152]{1,0:T(8,128)(2,1)S(1)} fusion(bf16[192,1152]{1,0:T(8,128)(2,1)} %collective-permute-done.5, bf16[192,1152]{1,0:T(8,128)(2,1)} %collective-permute-done.3, pred[]{:T(512)S(6)} %eq.14), kind=kLoop, calls=%fused_computation.3 | loop fusion | flops 221184 | bytes 1327105 | tf_op jit(solution)/shard_map/jit(_where)/select_n | solution.py:238
  50.0 2.0 %shard_map.69 = (bf16[576,1152]{1,0:T(8,128)(2,1)S(1)}, f32[192,1152]{1,0:T(8,128)S(1)}, f32[192,1152]{1,0:T(8,128)S(1)}, bf16[192,1152]{1,0:T(8,128)(2,1)S(1)}) custom-call(s32[1]{0:T(128)} %bitcast.k_ref, s32[1]{0:T(128)} %bitcast.1.core_ref, f32[1]{0:T(128)S(6)} %copy.7.scale_ref, f32[1]{0:T(128)S(6)} %copy.8.shift_ref, bf16[192,1152]{1,0:T(8,128)(2,1)S(1)} %copy-done.1, ...), custom_call_target="tpu_custom_call" | custom-call | tf_op jit(solution)/shard_map/pallas_call | solution.py:195
  52.8 1.9 %collective-permute-start.8 = (bf16[576,1152]{1,0:T(8,128)(2,1)S(1)}, bf16[576,1152]{1,0:T(8,128)(2,1)S(1)}, u32[]{:S(2)}, u32[]{:S(2)}) collective-permute-start(bf16[576,1152]{1,0:T(8,128)(2,1)S(1)} %get-tuple-element.34), channel_id=1, source_target_pairs={{0,3},{1,4},{2,5},{3,0},{4,1},{5,2},{6,9},{7,10},{8,11},{9,6},{10,... | collective-permute-start | bytes 3981320 | tf_op jit(solution)/shard_map/ppermute | solution.py:30
  54.8 2.2 %shard_map.70 = (f32[576,1152]{1,0:T(8,128)S(1)}, bf16[192,1152]{1,0:T(8,128)(2,1)}, f32[192,1152]{1,0:T(8,128)S(1)}) custom-call(s32[1]{0:T(128)} %bitcast.k_ref, f32[1]{0:T(128)S(6)} %copy.7.scale_ref, f32[1]{0:T(128)S(6)} %copy.8.shift_ref, bf16[192,1152]{1,0:T(8,128)(2,1)S(1)} %copy-done.2, bf16[192,1152]{1,0:T(8,128)(2,1)S(1)} %broadcast_select_fusion.t2, ...), custom_call_target="tpu_custom_call" | custom-call | tf_op jit(solution)/shard_map/pallas_call | solution.py:195
  57.9 2.0 %collective-permute-start.11 = (bf16[192,1152]{1,0:T(8,128)(2,1)}, bf16[192,1152]{1,0:T(8,128)(2,1)}, u32[]{:S(2)}, u32[]{:S(2)}) collective-permute-start(bf16[192,1152]{1,0:T(8,128)(2,1)} %get-tuple-element.40), channel_id=1, source_target_pairs={{0,618},{1,613},{2,608},{3,591},{4,598},{5,605},{48,90},{49,85},{5... | collective-permute-start | bytes 1327112 | tf_op jit(solution)/shard_map/ppermute | solution.py:30
  60.0 1.1 %copy-done.3 = bf16[576,1152]{1,0:T(8,128)(2,1)} copy-done((bf16[576,1152]{1,0:T(8,128)(2,1)}, bf16[576,1152]{1,0:T(8,128)(2,1)S(1)}, u32[]{:S(2)}) %copy-start.3) | copy-done | bytes 1327128
  61.1 0.9 %shard_map.71 = (bf16[192,1152]{1,0:T(8,128)(2,1)}, bf16[192,1152]{1,0:T(8,128)(2,1)S(1)}) custom-call(f32[576,1152]{1,0:T(8,128)S(1)} %get-tuple-element.33.ours, bf16[576,1152]{1,0:T(8,128)(2,1)S(1)} %collective-permute-done.8.received), custom_call_target="tpu_custom_call" | custom-call | tf_op jit(solution)/shard_map/pallas_call | solution.py:195
  62.0 1.9 %collective-permute-start.9 = (bf16[192,1152]{1,0:T(8,128)(2,1)}, bf16[192,1152]{1,0:T(8,128)(2,1)}, u32[]{:S(2)}, u32[]{:S(2)}) collective-permute-start(bf16[192,1152]{1,0:T(8,128)(2,1)} %get-tuple-element.35), channel_id=1, source_target_pairs={{0,2},{1,0},{2,1},{3,5},{4,3},{5,4},{6,8},{7,6},{8,7},{9,11},{10,9... | collective-permute-start | bytes 1327112 | tf_op jit(solution)/shard_map/ppermute | solution.py:30
  63.9 3.8 %collective-permute-start.10 = (bf16[192,1152]{1,0:T(8,128)(2,1)S(1)}, bf16[192,1152]{1,0:T(8,128)(2,1)}, u32[]{:S(2)}, u32[]{:S(2)}) collective-permute-start(bf16[192,1152]{1,0:T(8,128)(2,1)S(1)} %get-tuple-element.36), channel_id=1, source_target_pairs={{0,1},{1,2},{2,0},{3,4},{4,5},{5,3},{6,7},{7,8},{8,6},{9,10},{10,1... | collective-permute-start | bytes 1327112 | tf_op jit(solution)/shard_map/ppermute | solution.py:30
  67.8 1.3 %collective-permute-start.13 = (bf16[192,1152]{1,0:T(8,128)(2,1)}, bf16[192,1152]{1,0:T(8,128)(2,1)S(1)}, u32[]{:S(2)}, u32[]{:S(2)}) collective-permute-start(bf16[192,1152]{1,0:T(8,128)(2,1)} %get-tuple-element.40), channel_id=1, source_target_pairs={{6,0},{7,1},{8,2},{9,3},{10,4},{11,5},{12,6},{13,7},{14,8},{15,9},... | collective-permute-start | bytes 1327112 | tf_op jit(solution)/shard_map/ppermute | solution.py:30
  70.6 5.6 %collective-permute-done.9 = bf16[192,1152]{1,0:T(8,128)(2,1)} collective-permute-done((bf16[192,1152]{1,0:T(8,128)(2,1)}, bf16[192,1152]{1,0:T(8,128)(2,1)}, u32[]{:S(2)}, u32[]{:S(2)}) %collective-permute-start.9) | collective-permute-done | bytes 442400 | tf_op jit(solution)/shard_map/ppermute | solution.py:30
  76.2 10.3 %collective-permute-done.10 = bf16[192,1152]{1,0:T(8,128)(2,1)} collective-permute-done((bf16[192,1152]{1,0:T(8,128)(2,1)S(1)}, bf16[192,1152]{1,0:T(8,128)(2,1)}, u32[]{:S(2)}, u32[]{:S(2)}) %collective-permute-start.10) | collective-permute-done | bytes 442400 | tf_op jit(solution)/shard_map/ppermute | solution.py:30
  86.5 2.4 %add_add_fusion.1 = f32[192,1152]{1,0:T(8,128)} fusion(bf16[192,1152]{1,0:T(8,128)(2,1)} %collective-permute-done.10, bf16[192,1152]{1,0:T(8,128)(2,1)} %collective-permute-done.9, f32[576,1152]{1,0:T(8,128)S(1)} %get-tuple-element.33.ours, bf16[576,1152]{1,0:T(8,128)(2,1)} %copy-done.3), kind=kLoop, calls=%fused_computation.2 | loop fusion | flops 1327104 | bytes 3096576 | tf_op jit(solution)/shard_map/add | solution.py:263
  88.9 1.1 %add_add_fusion = f32[192,1152]{1,0:T(8,128)} fusion(f32[192,1152]{1,0:T(8,128)S(1)} %copy-done.7, bf16[192,1152]{1,0:T(8,128)(2,1)S(1)} %collective-permute-done.14, bf16[192,1152]{1,0:T(8,128)(2,1)S(1)} %collective-permute-done.12, bf16[192,1152]{1,0:T(8,128)(2,1)S(1)} %collective-permute-done.13, pred[]{:T(512)S(6)} %eq.16, pred[]{:T(512)S(6)} %eq.15), kind=kLoop, calls=%fused_computation.1 | loop fusion | flops 1327104 | bytes 3096578 | tf_op jit(solution)/shard_map/add | solution.py:266
  (39 shorter events, 4.0 us)
Async XLA Ops:
  0.6 39.2 %copy-start.1 = (bf16[192,1152]{1,0:T(8,128)(2,1)S(1)}, bf16[192,1152]{1,0:T(8,128)(2,1)}, u32[]{:S(2)}) copy-start(bf16[192,1152]{1,0:T(8,128)(2,1)} %t0.5) | copy-start | bytes 1327108
  0.6 39.2 %copy-start = (bf16[192,1152]{1,0:T(8,128)(2,1)S(1)}, bf16[192,1152]{1,0:T(8,128)(2,1)}, u32[]{:S(2)}) copy-start(bf16[192,1152]{1,0:T(8,128)(2,1)} %i0.3) | copy-start | bytes 1327108
  0.7 37.1 %copy-start.10 = (s32[192]{0:T(256)S(1)}, s32[192]{0:T(256)}, u32[]{:S(2)}) copy-start(s32[192]{0:T(256)} %param.7) | copy-start | bytes 2308
  0.7 14.8 %collective-permute-start.4 = (bf16[192,1152]{1,0:T(8,128)(2,1)}, bf16[192,1152]{1,0:T(8,128)(2,1)}, u32[]{:S(2)}, u32[]{:S(2)}) collective-permute-start(bf16[192,1152]{1,0:T(8,128)(2,1)} %t0.5), channel_id=1, source_target_pairs={{42,0},{43,7},{44,14},{45,33},{46,28},{47,23},{90,48},{91,55},{92,... | collective-permute-start | bytes 1327112 | tf_op jit(solution)/shard_map/ppermute | solution.py:30
  2.2 14.6 %collective-permute-start.1 = (bf16[192,1152]{1,0:T(8,128)(2,1)}, bf16[192,1152]{1,0:T(8,128)(2,1)S(1)}, u32[]{:S(2)}, u32[]{:S(2)}) collective-permute-start(bf16[192,1152]{1,0:T(8,128)(2,1)} %i0.3), channel_id=1, source_target_pairs={{0,2},{1,0},{2,1},{3,5},{4,3},{5,4},{6,8},{7,6},{8,7},{9,11},{10,9... | collective-permute-start | bytes 1327112 | tf_op jit(solution)/shard_map/ppermute | solution.py:30
  8.9 29.0 %collective-permute-start = (bf16[192,1152]{1,0:T(8,128)(2,1)}, bf16[192,1152]{1,0:T(8,128)(2,1)S(1)}, u32[]{:S(2)}, u32[]{:S(2)}) collective-permute-start(bf16[192,1152]{1,0:T(8,128)(2,1)} %i0.3), channel_id=1, source_target_pairs={{0,1},{1,2},{2,0},{3,4},{4,5},{5,3},{6,7},{7,8},{8,6},{9,10},{10,1... | collective-permute-start | bytes 1327112 | tf_op jit(solution)/shard_map/ppermute | solution.py:30
  10.8 30.3 %collective-permute-start.3 = (bf16[192,1152]{1,0:T(8,128)(2,1)}, bf16[192,1152]{1,0:T(8,128)(2,1)}, u32[]{:S(2)}, u32[]{:S(2)}) collective-permute-start(bf16[192,1152]{1,0:T(8,128)(2,1)} %t0.5), channel_id=1, source_target_pairs={{0,6},{1,7},{2,8},{3,9},{4,10},{5,11},{6,12},{7,13},{8,14},{9,15},... | collective-permute-start | bytes 1327112 | tf_op jit(solution)/shard_map/ppermute | solution.py:30
  14.8 26.3 %collective-permute-start.2 = (bf16[192,1152]{1,0:T(8,128)(2,1)}, bf16[192,1152]{1,0:T(8,128)(2,1)S(1)}, u32[]{:S(2)}, u32[]{:S(2)}) collective-permute-start(bf16[192,1152]{1,0:T(8,128)(2,1)} %t0.5), channel_id=1, source_target_pairs={{5,17},{11,23},{17,29},{23,35},{29,41},{35,47},{41,53},{47,59},{53... | collective-permute-start | bytes 1327112 | tf_op jit(solution)/shard_map/ppermute | solution.py:30
  15.5 33.4 %collective-permute-start.5 = (bf16[192,1152]{1,0:T(8,128)(2,1)}, bf16[192,1152]{1,0:T(8,128)(2,1)}, u32[]{:S(2)}, u32[]{:S(2)}) collective-permute-start(bf16[192,1152]{1,0:T(8,128)(2,1)} %collective-permute-done.4), channel_id=1, source_target_pairs={{0,48},{7,49},{14,50},{23,53},{28,52},{33,51},{48,96},{55,97},{62,... | collective-permute-start | bytes 1327112 | tf_op jit(solution)/shard_map/ppermute | solution.py:30
  18.8 31.2 %collective-permute-start.7 = (bf16[2,192,1152]{2,1,0:T(8,128)(2,1)}, bf16[2,192,1152]{2,1,0:T(8,128)(2,1)S(1)}, u32[]{:S(2)}, u32[]{:S(2)}) collective-permute-start(bf16[2,192,1152]{2,1,0:T(8,128)(2,1)} %pad_maximum_fusion), channel_id=1, source_target_pairs={{0,3},{1,4},{2,5},{3,0},{4,1},{5,2},{6,9},{7,10},{8,11},{9,6},{10,... | collective-permute-start | bytes 2654216 | tf_op jit(solution)/shard_map/ppermute | solution.py:30
  37.9 12.1 %copy-start.4 = (bf16[192,1152]{1,0:T(8,128)(2,1)}, bf16[192,1152]{1,0:T(8,128)(2,1)S(1)}, u32[]{:S(2)}) copy-start(bf16[192,1152]{1,0:T(8,128)(2,1)S(1)} %collective-permute-done.i1) | copy-start | bytes 1327108
  37.9 12.1 %collective-permute-start.6 = (bf16[192,1152]{1,0:T(8,128)(2,1)S(1)}, bf16[192,1152]{1,0:T(8,128)(2,1)S(1)}, u32[]{:S(2)}, u32[]{:S(2)}) collective-permute-start(bf16[192,1152]{1,0:T(8,128)(2,1)S(1)} %collective-permute-done.i1), channel_id=1, source_target_pairs={{0,3},{1,4},{2,5},{3,0},{4,1},{5,2},{6,9},{7,10},{8,11},{9,6},{10,... | collective-permute-start | bytes 1327112 | tf_op jit(solution)/shard_map/ppermute | solution.py:30
  50.0 4.7 %copy-start.2 = (bf16[192,1152]{1,0:T(8,128)(2,1)S(1)}, bf16[192,1152]{1,0:T(8,128)(2,1)}, u32[]{:S(2)}) copy-start(bf16[192,1152]{1,0:T(8,128)(2,1)} %t0.5) | copy-start | bytes 1327108
  50.0 4.7 %copy-start.5 = (bf16[192,1152]{1,0:T(8,128)(2,1)S(1)}, bf16[192,1152]{1,0:T(8,128)(2,1)}, u32[]{:S(2)}) copy-start(bf16[192,1152]{1,0:T(8,128)(2,1)} %copy-done.4) | copy-start | bytes 1327108
  52.8 7.1 %collective-permute-start.8 = (bf16[576,1152]{1,0:T(8,128)(2,1)S(1)}, bf16[576,1152]{1,0:T(8,128)(2,1)S(1)}, u32[]{:S(2)}, u32[]{:S(2)}) collective-permute-start(bf16[576,1152]{1,0:T(8,128)(2,1)S(1)} %get-tuple-element.34), channel_id=1, source_target_pairs={{0,3},{1,4},{2,5},{3,0},{4,1},{5,2},{6,9},{7,10},{8,11},{9,6},{10,... | collective-permute-start | bytes 3981320 | tf_op jit(solution)/shard_map/ppermute | solution.py:30
  57.9 12.0 %collective-permute-start.11 = (bf16[192,1152]{1,0:T(8,128)(2,1)}, bf16[192,1152]{1,0:T(8,128)(2,1)}, u32[]{:S(2)}, u32[]{:S(2)}) collective-permute-start(bf16[192,1152]{1,0:T(8,128)(2,1)} %get-tuple-element.40), channel_id=1, source_target_pairs={{0,618},{1,613},{2,608},{3,591},{4,598},{5,605},{48,90},{49,85},{5... | collective-permute-start | bytes 1327112 | tf_op jit(solution)/shard_map/ppermute | solution.py:30
  60.0 1.1 %copy-start.3 = (bf16[576,1152]{1,0:T(8,128)(2,1)}, bf16[576,1152]{1,0:T(8,128)(2,1)S(1)}, u32[]{:S(2)}) copy-start(bf16[576,1152]{1,0:T(8,128)(2,1)S(1)} %collective-permute-done.8.received) | copy-start | bytes 3981316
  61.1 8.0 %copy-start.9 = (bf16[192,1152]{1,0:T(8,128)(2,1)S(1)}, bf16[192,1152]{1,0:T(8,128)(2,1)}, u32[]{:S(2)}) copy-start(bf16[192,1152]{1,0:T(8,128)(2,1)} %copy-done.8) | copy-start | bytes 1327108
  62.0 14.2 %collective-permute-start.9 = (bf16[192,1152]{1,0:T(8,128)(2,1)}, bf16[192,1152]{1,0:T(8,128)(2,1)}, u32[]{:S(2)}, u32[]{:S(2)}) collective-permute-start(bf16[192,1152]{1,0:T(8,128)(2,1)} %get-tuple-element.35), channel_id=1, source_target_pairs={{0,2},{1,0},{2,1},{3,5},{4,3},{5,4},{6,8},{7,6},{8,7},{9,11},{10,9... | collective-permute-start | bytes 1327112 | tf_op jit(solution)/shard_map/ppermute | solution.py:30
  63.9 22.6 %collective-permute-start.10 = (bf16[192,1152]{1,0:T(8,128)(2,1)S(1)}, bf16[192,1152]{1,0:T(8,128)(2,1)}, u32[]{:S(2)}, u32[]{:S(2)}) collective-permute-start(bf16[192,1152]{1,0:T(8,128)(2,1)S(1)} %get-tuple-element.36), channel_id=1, source_target_pairs={{0,1},{1,2},{2,0},{3,4},{4,5},{5,3},{6,7},{7,8},{8,6},{9,10},{10,1... | collective-permute-start | bytes 1327112 | tf_op jit(solution)/shard_map/ppermute | solution.py:30
  67.8 21.1 %collective-permute-start.13 = (bf16[192,1152]{1,0:T(8,128)(2,1)}, bf16[192,1152]{1,0:T(8,128)(2,1)S(1)}, u32[]{:S(2)}, u32[]{:S(2)}) collective-permute-start(bf16[192,1152]{1,0:T(8,128)(2,1)} %get-tuple-element.40), channel_id=1, source_target_pairs={{6,0},{7,1},{8,2},{9,3},{10,4},{11,5},{12,6},{13,7},{14,8},{15,9},... | collective-permute-start | bytes 1327112 | tf_op jit(solution)/shard_map/ppermute | solution.py:30
  69.1 19.8 %copy-start.7 = (f32[192,1152]{1,0:T(8,128)S(1)}, f32[192,1152]{1,0:T(8,128)}, u32[]{:S(2)}) copy-start(f32[192,1152]{1,0:T(8,128)} %copy-done.6) | copy-start | bytes 2654212
  69.1 19.8 %collective-permute-start.14 = (bf16[192,1152]{1,0:T(8,128)(2,1)S(1)}, bf16[192,1152]{1,0:T(8,128)(2,1)S(1)}, u32[]{:S(2)}, u32[]{:S(2)}) collective-permute-start(bf16[192,1152]{1,0:T(8,128)(2,1)S(1)} %copy-done.9), channel_id=1, source_target_pairs={{5,761},{11,767},{17,5},{23,11},{29,17},{35,23},{41,29},{47,35},{5... | collective-permute-start | bytes 1327112 | tf_op jit(solution)/shard_map/ppermute | solution.py:30
  69.9 19.0 %collective-permute-start.12 = (bf16[192,1152]{1,0:T(8,128)(2,1)}, bf16[192,1152]{1,0:T(8,128)(2,1)S(1)}, u32[]{:S(2)}, u32[]{:S(2)}) collective-permute-start(bf16[192,1152]{1,0:T(8,128)(2,1)} %collective-permute-done.11), channel_id=1, source_target_pairs={{15,189},{22,190},{29,191},{32,188},{37,187},{42,186},{63,45},{70,... | collective-permute-start | bytes 1327112 | tf_op jit(solution)/shard_map/ppermute | solution.py:30
  (2 other events, 1.7 us)
